TPU v7x, 32 devices: a whole 2x2x4 slice. The times are simulated.
32 devices in a mesh: dp: 2 (over x), blk: 16 (over z, y, core).
Axes of the slice: x: 2, y: 2, z: 4, core: 2. Of those that a mesh axis runs over, the one named last changes fastest.
Arguments:
- tokens: bfloat16 [24576, 16384], P('dp', 'blk'), may hold values from -6 to 6
- left: bfloat16 [128, 128, 128], P('blk'), may hold values from -0.5 to 0.5
- right: bfloat16 [128, 128, 128], P('blk'), may hold values from -0.5 to 0.5
- cotangent: bfloat16 [24576, 16384], P('dp', 'blk'), may hold values from -6 to 6
- keep_mask: int32 [128, 24576], P('blk', 'dp'), may hold values 0 or 1
- channel_order: int32 [128], replicated, may hold values from 0 to 127, each once
Outputs:
- mixed: bfloat16 [24576, 16384], P('dp', 'blk')
- grad_tokens: bfloat16 [24576, 16384], P('dp', 'blk')
- grad_left: float32 [128, 128, 128], P('blk')
- grad_right: float32 [128, 128, 128], P('blk')
Inputs may be any that keep to these rules, and one draw needn't show every extreme that they name: `channel_order`: each of 0 to 127 appears once.
All inputs are finite; a program needn't handle non-finite values. No bound on the sum of `keep_mask` on one device may be relied on, other than what follows from the above.
Results may differ from a plain program's by a relative error of at most 0.0075.
Values may be sent and summed in bfloat16 or wider, within the bound.
No kernel may reach another device: no remote copies, remote signals or barrier semaphores. Data moves between devices by JAX's collectives and lax.ppermute only.
A program may use at most 384 MiB of HBM per device.

v0:
```python
import math

import jax
import jax.numpy as jnp
from jax import lax
from jax.sharding import PartitionSpec as P

keep_rate = 0.9


def normal_parts(value):
    normal_cdf = 0.5 * (1.0 + jax.scipy.special.erf(value / math.sqrt(2.0)))
    normal_pdf = jnp.exp(-0.5 * value * value) / math.sqrt(2.0 * math.pi)
    return (normal_cdf, normal_pdf)


def local(tokens, left, right, cotangent, keep_mask, channel_order):
    row_count = tokens.shape[0]
    own_blocks = left.shape[0]
    block_size = left.shape[1]
    own_outputs = right.shape[0]
    block_order = right.shape[1]
    token_total = row_count * lax.axis_size("dp")
    columns_iota = lax.broadcasted_iota(jnp.int32, (block_size, block_size), 1)
    selector = (channel_order[:, None] == columns_iota).astype(jnp.bfloat16)
    left_permutation = jnp.einsum(
        "qm,bqo->bmo", selector, left, preferred_element_type=jnp.float32
    ).astype(jnp.bfloat16)
    block_shaped = tokens.reshape(row_count, own_blocks, block_size)
    exchanged = lax.all_to_all(
        jnp.einsum(
            "uaf,afh->uha", block_shaped, left_permutation, preferred_element_type=jnp.float32
        ).astype(jnp.bfloat16),
        "blk",
        split_axis=1,
        concat_axis=2,
        tiled=True,
    )
    mixing = jnp.einsum("tjb,jbi->tji", exchanged, right, preferred_element_type=jnp.float32)
    kept = keep_mask.T.astype(jnp.float32) / keep_rate
    normal_cdf, normal_pdf = normal_parts(mixing)
    branch = (kept[:, :, None] * mixing * normal_cdf).reshape(row_count, own_outputs * block_order)
    mixed = (tokens.astype(jnp.float32) + branch).astype(jnp.bfloat16)
    up_projection_gradient = cotangent.reshape(row_count, own_outputs, block_order).astype(
        jnp.float32
    )
    grad_mix = (
        up_projection_gradient * kept[:, :, None] * (normal_cdf + mixing * normal_pdf)
    ).astype(jnp.bfloat16)
    part_right = jnp.einsum("tjb,tji->jbi", exchanged, grad_mix, preferred_element_type=jnp.float32)
    summed_right = lax.psum(part_right.astype(jnp.bfloat16), "dp").astype(jnp.float32)
    first_factor_gradient = lax.all_to_all(
        jnp.einsum("tji,jbi->tjb", grad_mix, right, preferred_element_type=jnp.float32).astype(
            jnp.bfloat16
        ),
        "blk",
        split_axis=2,
        concat_axis=1,
        tiled=True,
    )
    unpermuted_left = jnp.einsum(
        "lgc,lag->gca", block_shaped, first_factor_gradient, preferred_element_type=jnp.float32
    )
    part_left = jnp.einsum(
        "km,bmo->bko",
        selector.astype(jnp.float32),
        unpermuted_left,
        precision=lax.Precision.HIGHEST,
    )
    summed_left = lax.psum(part_left.astype(jnp.bfloat16), "dp").astype(jnp.float32)
    grad_input = jnp.einsum(
        "jri,ipr->jip", first_factor_gradient, left_permutation, preferred_element_type=jnp.float32
    )
    grad_tokens = (
        cotangent.astype(jnp.float32) + grad_input.reshape(row_count, own_blocks * block_size)
    ).astype(jnp.bfloat16)
    factor = 1.0 / math.sqrt(token_total)
    return (mixed, grad_tokens, summed_left * factor, summed_right * factor)


def solution(mesh):
    in_specs = (
        P("dp", "blk"),
        P("blk", None, None),
        P("blk", None, None),
        P("dp", "blk"),
        P("blk", "dp"),
        P(),
    )
    out_specs = (P("dp", "blk"), P("dp", "blk"), P("blk", None, None), P("blk", None, None))
    return jax.shard_map(local, mesh=mesh, in_specs=in_specs, out_specs=out_specs, check_vma=False)
```

profile of v0, /device:TPU:16, one launch (start us, length us, event | category | flops | bytes accessed | tf_op | source)
XLA Modules:
  0.0 1513.5 jit_solution(13663268493769970100)
XLA Ops:
  7.2 0.0 copy-start
  7.2 1.3 fusion.36
  8.5 0.0 copy-start.2
  8.5 18.6 %convert_bitcast_fusion.1 = bf16[12288,128,8]{0,1,2:T(8,128)(2,1)} fusion(bf16[8,128,128]{2,1,0:T(8,128)(2,1)S(1)} %fusion.36, bf16[12288,1024]{1,0:T(8,128)(2,1)} %param.6), kind=kOutput, calls=%fused_computation.24 | convolution fusion | flops 3233808384 | bytes 50593792 | tf_op jit(solution)/shard_map/uaf,afh->uha/dot_general | solution.py:31
  27.1 0.0 copy-done.2
  27.1 26.7 %copy.65 = bf16[12288,128,8]{0,2,1:T(8,128)(2,1)} copy(bf16[12288,128,8]{0,1,2:T(8,128)(2,1)} %convert_bitcast_fusion.1) | data formatting | bytes 50331648 | tf_op jit(solution)/shard_map/convert_element_type | solution.py:33
  53.8 6.2 all-to-all-start
  60.0 34.6 %copy.70 = f32[12288,1024]{0,1:T(8,128)} copy(bf16[12288,1024]{1,0:T(8,128)(2,1)} %param.9) | data formatting | bytes 75497472 | tf_op jit(solution)/shard_map/convert_element_type | solution.py:75
  94.7 0.0 copy-done.4
  94.7 507.4 %all-to-all-done = bf16[12288,128,8]{0,2,1:T(8,128)(2,1)} async-done(((bf16[12288,128,8]{0,2,1:T(8,128)(2,1)}), bf16[12288,128,8]{0,2,1:T(8,128)(2,1)}, u32[]{:S(2)}, u32[]{:S(2)}) %all-to-all-start) | async-done | bytes 25165856 | tf_op jit(solution)/shard_map/all_to_all | solution.py:30
  602.1 0.0 copy-done
  602.1 59.2 %fusion.5 = (bf16[12288,8,128]{0,2,1:T(8,128)(2,1)}, f32[12288,8,128]{0,2,1:T(8,128)}) fusion(f32[12288,8,128]{0,2,1:T(8,128)} %bitcast.82, f32[12288,8]{0,1:T(8,128)S(1)} %multiply_bitcast_fusion, bf16[8,128,128]{2,1,0:T(8,128)(2,1)S(1)} %copy-done, bf16[12288,8,16,8]{0,3,1,2:T(8,128)(2,1)} %bitcast.5), kind=kOutput, calls=%fused_computation.6 | convolution fusion | flops 3384803328 | bytes 151650304 | tf_op jit(solution)/shard_map/tjb,jbi->tji/dot_general | solution.py:39
  661.3 20.4 %convert_bitcast_fusion = bf16[12288,8,128]{2,0,1:T(8,128)(2,1)} fusion(bf16[12288,8,128]{0,2,1:T(8,128)(2,1)} %get-tuple-element.22, bf16[8,128,128]{2,1,0:T(8,128)(2,1)S(1)} %copy-done), kind=kOutput, calls=%fused_computation.23 | convolution fusion | flops 3233808384 | bytes 50593792 | tf_op jit(solution)/shard_map/tji,jbi->tjb/dot_general | solution.py:53
  681.7 32.1 %copy.72 = bf16[12288,8,128]{0,1,2:T(8,128)(2,1)} copy(bf16[12288,8,128]{2,0,1:T(8,128)(2,1)} %convert_bitcast_fusion) | data formatting | bytes 50331648 | tf_op jit(solution)/shard_map/convert_element_type | solution.py:53
  713.8 5.5 all-to-all-start.1
  719.3 0.3 all-reduce.3.cloned.1.call-start
  719.6 48.8 %copy.69 = f32[12288,1024]{1,0:T(8,128)} copy(f32[12288,1024]{0,1:T(8,128)} %bitcast.81) | data formatting | bytes 100663296 | tf_op jit(solution)/shard_map/reshape | solution.py:42
  768.4 18.6 %fusion.32 = bf16[8,128,128]{1,2,0:T(8,128)(2,1)} fusion(bf16[12288,8,128]{0,2,1:T(8,128)(2,1)} %get-tuple-element.22, bf16[12288,8,16,8]{0,3,1,2:T(8,128)(2,1)} %bitcast.5), kind=kOutput, calls=%fused_computation.35 | convolution fusion | flops 3221356544 | bytes 50593792 | tf_op jit(solution)/shard_map/tjb,tji->jbi/dot_general | solution.py:50
  787.0 474.0 %all-to-all-done.1 = bf16[12288,8,128]{0,1,2:T(8,128)(2,1)} async-done(((bf16[12288,8,128]{0,1,2:T(8,128)(2,1)}), bf16[12288,8,128]{0,1,2:T(8,128)(2,1)}, u32[]{:S(2)}, u32[]{:S(2)}) %all-to-all-start.1) | async-done | bytes 25165856 | tf_op jit(solution)/shard_map/all_to_all | solution.py:52
  1261.0 26.7 %copy.74 = bf16[12288,16,8,8]{0,3,2,1:T(8,128)(2,1)} copy(bf16[12288,16,8,8]{0,2,3,1:T(8,128)(2,1)} %bitcast.13) | data formatting | bytes 50331648 | tf_op jit(solution)/shard_map/all_to_all | solution.py:52
  1287.7 41.7 %fusion.27 = f32[8,128,128]{1,2,0:T(8,128)S(1)} fusion(bf16[12288,128,8]{0,2,1:T(8,128)(2,1)} %bitcast.79, bf16[12288,1024]{1,0:T(8,128)(2,1)} %param.6), kind=kOutput, calls=%fused_computation.32 | convolution fusion | flops 3221225472 | bytes 50855936 | tf_op jit(solution)/shard_map/lgc,lag->gca/dot_general | solution.py:61
  1329.4 0.0 copy-done.3
  1329.4 0.0 copy-start.5
  1329.4 59.0 %fusion.22 = f32[8,128,12288]{2,1,0:T(8,128)} fusion(bf16[8,128,128]{2,1,0:T(8,128)(2,1)S(1)} %copy-done.3, bf16[12288,128,8]{0,2,1:T(8,128)(2,1)} %bitcast.80), kind=kOutput, calls=%fused_computation.27 | convolution fusion | flops 3221225472 | bytes 75759616 | tf_op jit(solution)/shard_map/jri,ipr->jip/dot_general | solution.py:71
  1388.4 1.2 fusion.35
  1389.5 48.8 %copy.76 = f32[12288,1024]{1,0:T(8,128)} copy(f32[12288,1024]{0,1:T(8,128)} %bitcast.78) | data formatting | bytes 100663296 | tf_op jit(solution)/shard_map/reshape | solution.py:75
  1438.4 0.0 all-reduce.3.cloned.1.call-update
  1438.4 0.0 copy-start.1
  1438.4 64.9 %add_convert_fusion = (bf16[12288,1024]{1,0:T(8,128)(2,1)}, bf16[12288,1024]{1,0:T(8,128)(2,1)}) fusion(f32[12288,1024]{1,0:T(8,128)} %copy.76, bf16[12288,1024]{1,0:T(8,128)(2,1)} %param.9, f32[12288,1024]{1,0:T(8,128)} %copy.69, bf16[12288,1024]{1,0:T(8,128)(2,1)} %param.6), kind=kLoop, calls=%fused_computation.13 | loop fusion | flops 75497472 | bytes 201326592 | tf_op jit(solution)/shard_map/convert_element_type | solution.py:76
  1503.3 1.1 convert_multiply_fusion
  1504.4 1.0 copy.82
  1505.4 1.0 copy.81
  (6 shorter events, 0.0 us)
Async XLA Ops:
  7.2 595.0 %copy-start = (bf16[8,128,128]{2,1,0:T(8,128)(2,1)S(1)}, bf16[8,128,128]{2,1,0:T(8,128)(2,1)}, u32[]{:S(2)}) copy-start(bf16[8,128,128]{2,1,0:T(8,128)(2,1)} %param.8) | copy-start | bytes 786436
  8.5 18.6 %copy-start.2 = (bf16[8,128,128]{2,1,0:T(8,128)(2,1)}, bf16[8,128,128]{2,1,0:T(8,128)(2,1)S(1)}, u32[]{:S(2)}) copy-start(bf16[8,128,128]{2,1,0:T(8,128)(2,1)S(1)} %fusion.36) | copy-start | bytes 786436
  53.8 548.3 %all-to-all-start = ((bf16[12288,128,8]{0,2,1:T(8,128)(2,1)}), bf16[12288,128,8]{0,2,1:T(8,128)(2,1)}, u32[]{:S(2)}, u32[]{:S(2)}) async-start(bf16[12288,128,8]{0,2,1:T(8,128)(2,1)} %copy.65), calls=%async_computation | async-start | bytes 50331648 | tf_op jit(solution)/shard_map/all_to_all | solution.py:30
  60.0 34.7 %copy-start.4 = (s32[8,12288]{1,0:T(8,128)S(1)}, s32[8,12288]{1,0:T(8,128)}, u32[]{:S(2)}) copy-start(s32[8,12288]{1,0:T(8,128)} %param.10) | copy-start | bytes 1179652
  713.8 547.2 %all-to-all-start.1 = ((bf16[12288,8,128]{0,1,2:T(8,128)(2,1)}), bf16[12288,8,128]{0,1,2:T(8,128)(2,1)}, u32[]{:S(2)}, u32[]{:S(2)}) async-start(bf16[12288,8,128]{0,1,2:T(8,128)(2,1)} %copy.72), calls=%async_computation.1 | async-start | bytes 50331648 | tf_op jit(solution)/shard_map/all_to_all | solution.py:52
  719.3 784.0 %all-reduce.3.cloned.1.call-start = ((), (), s32[]{:S(2)}) async-start(), calls=%async_computation.2 | async-start | bytes 1048576 | tf_op jit(solution)/shard_map/psum | solution.py:70
  1287.7 41.7 %copy-start.3 = (bf16[8,128,128]{2,1,0:T(8,128)(2,1)S(1)}, bf16[8,128,128]{2,1,0:T(8,128)(2,1)}, u32[]{:S(2)}) copy-start(bf16[8,128,128]{2,1,0:T(8,128)(2,1)} %copy-done.2) | copy-start | bytes 786436
  1329.4 59.0 %copy-start.5 = (s32[128]{0:T(128)S(1)}, s32[128]{0:T(128)}, u32[]{:S(2)}) copy-start(s32[128]{0:T(128)} %param.11) | copy-start | bytes 1540
  1438.4 68.0 %copy-start.1 = (bf16[8,128,128]{2,1,0:T(8,128)(2,1)S(1)}, bf16[8,128,128]{2,1,0:T(8,128)(2,1)}, u32[]{:S(2)}) copy-start(bf16[8,128,128]{2,1,0:T(8,128)(2,1)} %param.8) | copy-start | bytes 786436
Sparse Core Ops, SparseCore 0:
  1438.5 27.9 all-reduce.2
where the time goes:
time: 1520 us; the launch traced here: 1510 us
  waiting for transfers between devices  981 us (65%)
  local copies, waits for them, and re-layouts  220 us (14%)
  matrix products  220 us (14%)
  other arithmetic  66.1 us (4%)
    all_to_all x1, waiting for transfers between devices, local(): lax.all_to_all(jnp.einsum('uaf,afh->uha', block_shaped, left_permutation,...  507 us
    all_to_all x1, waiting for transfers between devices, local(): lax.all_to_all(jnp.einsum('tji,jbi->tjb', grad_mix, right, preferred_elem...  474 us
    convert_element_type x1, other arithmetic, local(): grad_tokens = (cotangent.astype(jnp.float32) + grad_input.reshape(row_cou...  64.9 us
    dot_general x1, matrix products, local(): jnp.einsum('tjb,jbi->tji', exchanged, right, preferred_element_type=jnp.f...  59.2 us
    dot_general x1, matrix products, local(): jnp.einsum('jri,ipr->jip', first_factor_gradient, left_permutation, prefe...  59 us
    reshape x1, local copies, waits for them, and re-layouts, local(): grad_input.reshape(row_count, own_blocks * block_size)  48.8 us
    reshape x1, local copies, waits for them, and re-layouts, local(): (kept[:, :, None] * mixing * normal_cdf).reshape(row_count, own_outputs *...  48.8 us
    dot_general x1, matrix products, local(): jnp.einsum('lgc,lag->gca', block_shaped, first_factor_gradient, preferred...  41.7 us
  transfers between devices with their start and end apart: 3, of which 2 were waited for; matrix products, arithmetic and copies ran while one was open for 11% of the time, Pallas kernels for 0%

commit v1 on v0

v1 whole, which is shorter than its diff:
```python
import functools
import math

import jax
import jax.numpy as jnp
from jax import lax
from jax.experimental import pallas as pl
from jax.experimental.pallas import tpu as pltpu
from jax.sharding import PartitionSpec as P

keep_rate = 0.9
CHUNKS = 8
TILE = 512
VMEM_LIMIT = 44 * 1024 * 1024
NT = (((1,), (1,)), ((), ()))
TN = (((0,), (0,)), ((), ()))
NN = (((1,), (0,)), ((), ()))


def dot(lhs, rhs, dims):
    return lax.dot_general(lhs, rhs, dims, preferred_element_type=jnp.float32)


class Plan:
    def __init__(self, rows, own, order, devices):
        self.rows, self.own, self.order, self.devices = rows, own, order, devices
        self.direct = (2 * own) % 16 == 0 and own >= 2
        self.pair = 2 if self.direct else own
        self.pairs = own // self.pair
        self.slots = devices if self.direct else 1
        self.height = devices * own * own
        self.slot_height = self.height // self.slots
        self.width = own * order
        self.chunks = CHUNKS
        self.chunk = rows // self.chunks
        self.tile = math.gcd(self.chunk, TILE)
        self.steps = self.chunk // self.tile

    def token_spec(self, chunk):
        return pl.BlockSpec((self.tile, self.width), lambda i: (chunk * self.steps + i, 0))

    def slot_specs(self):
        return [pl.BlockSpec((self.slot_height, self.tile), lambda i: (0, i))] * self.slots

    def slot_shapes(self):
        return [jax.ShapeDtypeStruct((self.slot_height, self.chunk), jnp.bfloat16)] * self.slots

    def pair_rows(self, refs, pair):
        if self.pairs == 1 and self.slots == 1:
            return refs[0][...]
        size = self.pair * self.own
        return jnp.concatenate([ref[pair * size : (pair + 1) * size, :] for ref in refs], axis=0)


def whole(array):
    zeros = (0,) * array.ndim
    return pl.BlockSpec(array.shape, lambda i: zeros)


def call(body, plan, ins, in_specs, outs, out_specs, aliases, flops, scratch=()):
    size = sum(math.prod(o.shape) * o.dtype.itemsize for o in outs[: plan.slots]) * 4
    return pl.pallas_call(
        body,
        out_shape=outs,
        grid=(plan.steps,),
        in_specs=in_specs,
        out_specs=out_specs,
        scratch_shapes=scratch,
        input_output_aliases=aliases,
        compiler_params=pltpu.CompilerParams(vmem_limit_bytes=VMEM_LIMIT),
        cost_estimate=pl.CostEstimate(flops=flops, bytes_accessed=size, transcendentals=0),
    )(*ins)


def first_factor(plan, chunk, tokens, wide_left):
    def body(tokens_ref, left_ref, *out_refs):
        product = dot(left_ref[...], tokens_ref[...], NT).astype(jnp.bfloat16)
        for slot, ref in enumerate(out_refs):
            ref[...] = product[slot * plan.slot_height : (slot + 1) * plan.slot_height, :]

    return call(
        body,
        plan,
        (tokens, wide_left),
        [plan.token_spec(chunk), whole(wide_left)],
        plan.slot_shapes(),
        plan.slot_specs(),
        {},
        2 * plan.height * plan.width * plan.chunk,
    )


def second_factor(plan, chunk, received, tokens, cotangent, keep_mask, spread, wide_right, state):
    slots, span = plan.slots, plan.pair * plan.order

    def body(*refs):
        got = refs[:slots]
        tokens_ref, cotangent_ref, mask_ref, spread_ref, right_ref = refs[slots : slots + 5]
        outs = refs[len(refs) - slots - 2 :]
        sent, mixed_ref, total_ref = outs[:slots], outs[slots], outs[slots + 1]

        @pl.when(pl.program_id(0) == 0)
        def _():
            if chunk == 0:
                total_ref[...] = jnp.zeros_like(total_ref)
            else:
                total_ref[...] = refs[slots + 6][...]

        mask = mask_ref[...].astype(jnp.float32).astype(jnp.bfloat16)
        for pair in range(plan.pairs):
            columns = slice(pair * span, (pair + 1) * span)
            kept = dot(mask, spread_ref[:, columns], TN) * jnp.float32(1.0 / keep_rate)
            rows = plan.pair_rows(got, pair)
            mixing = dot(rows, right_ref[pair], TN)
            cdf = 0.5 * (1.0 + lax.erf(mixing * jnp.float32(1.0 / math.sqrt(2.0))))
            pdf = jnp.exp(-0.5 * mixing * mixing) * jnp.float32(1.0 / math.sqrt(2.0 * math.pi))
            branch = kept * mixing * cdf
            mixed_ref[:, columns] = (tokens_ref[:, columns].astype(jnp.float32) + branch).astype(jnp.bfloat16)
            grad_mix = (cotangent_ref[:, columns].astype(jnp.float32) * kept * (cdf + mixing * pdf)).astype(
                jnp.bfloat16
            )
            total_ref[pair] += dot(rows, grad_mix, NN)
            back = dot(right_ref[pair], grad_mix, NT).astype(jnp.bfloat16)
            if plan.pairs == 1 and slots == 1:
                sent[0][...] = back
            else:
                size = plan.pair * plan.own
                for slot, ref in enumerate(sent):
                    ref[pair * size : (pair + 1) * size, :] = back[slot * size : (slot + 1) * size, :]

    ins = (*received, tokens, cotangent, keep_mask, spread, wide_right)
    in_specs = [
        *plan.slot_specs(),
        plan.token_spec(chunk),
        plan.token_spec(chunk),
        pl.BlockSpec((plan.own, plan.tile), lambda i: (0, chunk * plan.steps + i)),
        whole(spread),
        whole(wide_right),
    ]
    aliases = {}
    if state is not None:
        aliases = {len(ins): slots, len(ins) + 1: slots + 1}
        ins = (*ins, *state)
        in_specs += [pl.BlockSpec(memory_space=pl.ANY), whole(state[1])]
    outs = [
        *plan.slot_shapes(),
        jax.ShapeDtypeStruct(tokens.shape, jnp.bfloat16),
        jax.ShapeDtypeStruct((plan.pairs, plan.pair * plan.order, span), jnp.float32),
    ]
    out_specs = [*plan.slot_specs(), plan.token_spec(chunk), whole(outs[-1])]
    flops = 6 * plan.height * span * plan.chunk * 4
    result = call(body, plan, ins, in_specs, outs, out_specs, aliases, flops)
    return result[:slots], (result[slots], result[slots + 1])


def first_factor_back(plan, chunk, received, tokens, cotangent, wide_left, state):
    slots, own, order = plan.slots, plan.own, plan.order

    def body(*refs):
        got = refs[:slots]
        tokens_ref, cotangent_ref, left_ref = refs[slots : slots + 3]
        grad_ref, total_ref, scratch_ref = refs[-3:]
        step = pl.program_id(0)

        rows = got[0][...] if slots == 1 else jnp.concatenate([ref[...] for ref in got], axis=0)
        grad = dot(rows, left_ref[...], TN)
        grad_ref[...] = (cotangent_ref[...].astype(jnp.float32) + grad).astype(jnp.bfloat16)
        product = dot(rows, tokens_ref[...], NN)

        for block in range(own):
            part = product[:, block * order : (block + 1) * order]

            @pl.when(step == 0)
            def _():
                scratch_ref[block] = part

            @pl.when(step > 0)
            def _():
                scratch_ref[block] += part

        @pl.when(step == plan.steps - 1)
        def _():
            for block in range(own):
                part = scratch_ref[block, pl.ds(block, order, stride=own), :]
                total_ref[block] = part if chunk == 0 else part + refs[slots + 4][block]

    ins = (*received, tokens, cotangent, wide_left)
    in_specs = [*plan.slot_specs(), plan.token_spec(chunk), plan.token_spec(chunk), whole(wide_left)]
    aliases = {}
    if state is not None:
        aliases = {len(ins): 0, len(ins) + 1: 1}
        ins = (*ins, *state)
        in_specs += [pl.BlockSpec(memory_space=pl.ANY), whole(state[1])]
    outs = [
        jax.ShapeDtypeStruct(tokens.shape, jnp.bfloat16),
        jax.ShapeDtypeStruct((own, order, order), jnp.float32),
    ]
    out_specs = [plan.token_spec(chunk), whole(outs[1])]
    return call(
        body,
        plan,
        ins,
        in_specs,
        outs,
        out_specs,
        aliases,
        4 * plan.height * plan.width * plan.chunk,
        [pltpu.VMEM((own, plan.height, order), jnp.float32)],
    )


def exchange(plan, parts):
    if plan.direct:
        return [
            part if slot == 0 else lax.ppermute(part, "blk", [(i, i ^ slot) for i in range(plan.devices)])
            for slot, part in enumerate(parts)
        ]
    split = parts[0].reshape(plan.devices, plan.own * plan.own, plan.chunk)
    return [lax.all_to_all(split, "blk", 0, 0, tiled=True).reshape(plan.height, plan.chunk)]


def sum_over_dp(value):
    size = lax.axis_size("dp")
    if size == 2:
        return value.astype(jnp.float32) + lax.ppermute(value, "dp", [(0, 1), (1, 0)]).astype(jnp.float32)
    return lax.psum(value, "dp").astype(jnp.float32)


def local(tokens, left, right, cotangent, keep_mask, channel_order):
    rows, (own, order, _) = tokens.shape[0], left.shape
    devices = lax.axis_size("blk")
    plan = Plan(rows, own, order, devices)
    pair, pairs, span = plan.pair, plan.pairs, plan.pair * order
    partner = lax.iota(jnp.int32, devices)
    if plan.direct:
        partner = partner ^ lax.axis_index("blk")
    factor = 1.0 / math.sqrt(rows * lax.axis_size("dp"))

    selector = (channel_order[:, None] == lax.broadcasted_iota(jnp.int32, (order, order), 1)).astype(jnp.bfloat16)
    unpermuted_left = jnp.einsum("km,bko->obm", selector, left, preferred_element_type=jnp.float32).astype(jnp.bfloat16)
    slotted_left = jnp.take(unpermuted_left.reshape(devices, own, own, order), partner, axis=0)
    eye = jnp.eye(own, dtype=jnp.bfloat16)
    wide_left = (slotted_left.reshape(order, 1, own, order) * eye[None, :, :, None]).reshape(plan.height, plan.width)

    slotted_right = jnp.take(right.reshape(own, devices, own, order), partner, axis=1)
    slotted_right = slotted_right.reshape(pairs, pair, devices, own, order).transpose(0, 2, 1, 3, 4)
    eye_pair = jnp.eye(pair, dtype=jnp.bfloat16)
    wide_right = (slotted_right[:, :, :, :, None, :] * eye_pair[None, None, :, None, :, None]).reshape(
        pairs, pair * order, span
    )
    spread = jnp.repeat(eye, order, axis=1)

    forward = [
        exchange(plan, first_factor(plan, chunk, tokens, wide_left)) for chunk in range(plan.chunks)
    ]
    state, backward = None, []
    for chunk in range(plan.chunks):
        sent, state = second_factor(
            plan, chunk, forward[chunk], tokens, cotangent, keep_mask, spread, wide_right, state
        )
        backward.append(exchange(plan, sent))
    mixed, wide_total = state

    split_total = wide_total.reshape(pairs, devices, pair, own, pair, order)
    part_right = jnp.stack([split_total[:, :, jj, :, jj, :] for jj in range(pair)], axis=1)
    part_right = jnp.take(part_right.reshape(own, devices, own, order), partner, axis=1).reshape(own, order, order)
    grad_right = sum_over_dp(part_right.astype(jnp.bfloat16)) * factor

    state = None
    for chunk in range(plan.chunks):
        state = first_factor_back(plan, chunk, backward[chunk], tokens, cotangent, wide_left, state)
    grad_tokens, part_left = state
    part_left = jnp.take(part_left.astype(jnp.bfloat16).reshape(own, devices, own, order), partner, axis=1)
    part_left = jnp.einsum(
        "km,bom->bko", selector, part_left.reshape(own, order, order), preferred_element_type=jnp.float32
    ).astype(jnp.bfloat16)
    grad_left = sum_over_dp(part_left) * factor
    return (mixed, grad_tokens, grad_left, grad_right)


def solution(mesh):
    in_specs = (
        P("dp", "blk"),
        P("blk", None, None),
        P("blk", None, None),
        P("dp", "blk"),
        P("blk", "dp"),
        P(),
    )
    out_specs = (P("dp", "blk"), P("dp", "blk"), P("blk", None, None), P("blk", None, None))
    return jax.shard_map(local, mesh=mesh, in_specs=in_specs, out_specs=out_specs, check_vma=False)
```

time: 1520 us -> 1350 us (0.89)
  waiting for transfers between devices: 981 us -> 639 us
  starting transfers between devices: 11.9 us -> 312 us
  Pallas kernels: 0 us -> 237 us
  matrix products: 220 us -> 1.85 us
  local copies, waits for them, and re-layouts: 220 us -> 146 us
  other arithmetic: 66.1 us -> 4.5 us
    all_to_all x2 -> x0, waiting for transfers between devices: 981 us -> none  [the longest x1 507 us: local(): lax.all_to_all(jnp.einsum('uaf,afh->uha', block_shaped, left_permutation,...]
    ppermute x0 -> x242, waiting for transfers between devices: none -> 639 us  [the longest x240 633 us: exchange(): lax.ppermute(part, 'blk', [(i, i ^ slot) for i in range(plan.devices)])]
    ppermute x0 -> x242, starting transfers between devices: none -> 312 us  [the longest x240 309 us: exchange(): lax.ppermute(part, 'blk', [(i, i ^ slot) for i in range(plan.devices)])]
    pallas_call x0 -> x24, Pallas kernels: none -> 237 us  [call(): pl.pallas_call(body, out_shape=outs, grid=(plan.steps,), in_specs=in_spec...]
    dot_general x8 -> x1, matrix products: 220 us -> 0.91 us  [local(): jnp.einsum('km,bom->bko', selector, part_left.reshape(own, order, order),...]
    unnamed x14 -> x927, local copies, waits for them, and re-layouts: 2.03 us -> 136 us
    reshape x2 -> x3, local copies, waits for them, and re-layouts: 97.6 us -> 0.26 us  [the longest x1 0.17 us: local(): unpermuted_left.reshape(devices, own, own, order)]
    convert_element_type x3 -> x0, local copies, waits for them, and re-layouts: 93.5 us -> none  [the longest x1 34.6 us: local(): cotangent.astype(jnp.float32)]
  transfers between devices with their start and end apart: 3 -> 242, of which waited for: 2 -> 113; matrix products, arithmetic and copies ran while one was open for 11% -> 1% of each run, Pallas kernels for 0% -> 16%
where the time goes in v1:
time: 1350 us
  waiting for transfers between devices  639 us (47%)
  starting transfers between devices  312 us (23%)
  Pallas kernels  237 us (18%)
  local copies, waits for them, and re-layouts  146 us (11%)
    ppermute x240, waiting for transfers between devices, exchange(): lax.ppermute(part, 'blk', [(i, i ^ slot) for i in range(plan.devices)])  633 us
    ppermute x240, starting transfers between devices, exchange(): lax.ppermute(part, 'blk', [(i, i ^ slot) for i in range(plan.devices)])  309 us
    pallas_call x24, Pallas kernels, call(): pl.pallas_call(body, out_shape=outs, grid=(plan.steps,), in_specs=in_spec...  237 us
    unnamed x927, local copies, waits for them, and re-layouts  136 us
  transfers between devices with their start and end apart: 242, of which 113 were waited for; matrix products, arithmetic and copies ran while one was open for 1% of the time, Pallas kernels for 16%

profile of v1, /device:TPU:16, one launch (start us, length us, event | category | flops | bytes accessed | tf_op | source)
XLA Modules:
  0.0 1345.5 jit_solution(9095524144588580292)
XLA Ops:
  42.9 18.6 %collective-permute-start.118 = (bf16[64,1536]{1,0:T(8,128)(2,1)S(1)}, bf16[64,1536]{1,0:T(8,128)(2,1)S(1)}, u32[]{:S(2)}, u32[]{:S(2)}) collective-permute-start(bf16[64,1536]{1,0:T(8,128)(2,1)S(1)} %get-tuple-element.419), channel_id=1, source_target_pairs={{0,14},{1,15},{2,12},{3,13},{4,10},{5,11},{6,8},{7,9},{8,6},{9,7},... | collective-permute-start | bytes 589832 | tf_op jit(solution)/shard_map/ppermute | solution.py:215
  120.4 19.8 %collective-permute-done.99.refs_10_ = bf16[64,1536]{1,0:T(8,128)(2,1)S(1)} collective-permute-done((bf16[64,1536]{1,0:T(8,128)(2,1)S(1)}, bf16[64,1536]{1,0:T(8,128)(2,1)S(1)}, u32[]{:S(2)}, u32[]{:S(2)}) %collective-permute-start.99) | collective-permute-done | bytes 196640 | tf_op jit(solution)/shard_map/ppermute | solution.py:215
  194.4 17.3 %collective-permute-done.83.refs_9_ = bf16[64,1536]{1,0:T(8,128)(2,1)S(1)} collective-permute-done((bf16[64,1536]{1,0:T(8,128)(2,1)S(1)}, bf16[64,1536]{1,0:T(8,128)(2,1)S(1)}, u32[]{:S(2)}, u32[]{:S(2)}) %collective-permute-start.83) | collective-permute-done | bytes 196640 | tf_op jit(solution)/shard_map/ppermute | solution.py:215
  269.9 18.8 %collective-permute-done.68.refs_9_ = bf16[64,1536]{1,0:T(8,128)(2,1)S(1)} collective-permute-done((bf16[64,1536]{1,0:T(8,128)(2,1)}, bf16[64,1536]{1,0:T(8,128)(2,1)S(1)}, u32[]{:S(2)}, u32[]{:S(2)}) %collective-permute-start.68) | collective-permute-done | bytes 196640 | tf_op jit(solution)/shard_map/ppermute | solution.py:215
  355.7 21.9 %collective-permute-done.53.refs_9_ = bf16[64,1536]{1,0:T(8,128)(2,1)S(1)} collective-permute-done((bf16[64,1536]{1,0:T(8,128)(2,1)S(1)}, bf16[64,1536]{1,0:T(8,128)(2,1)S(1)}, u32[]{:S(2)}, u32[]{:S(2)}) %collective-permute-start.53) | collective-permute-done | bytes 196640 | tf_op jit(solution)/shard_map/ppermute | solution.py:215
  382.6 11.7 collective-permute-done.55.refs_11_
  438.5 19.4 %collective-permute-done.39.refs_10_ = bf16[64,1536]{1,0:T(8,128)(2,1)S(1)} collective-permute-done((bf16[64,1536]{1,0:T(8,128)(2,1)S(1)}, bf16[64,1536]{1,0:T(8,128)(2,1)S(1)}, u32[]{:S(2)}, u32[]{:S(2)}) %collective-permute-start.39) | collective-permute-done | bytes 196640 | tf_op jit(solution)/shard_map/ppermute | solution.py:215
  460.3 11.3 shard_map.101
  488.3 11.7 shard_map.102
  518.3 11.3 shard_map.103
  540.3 18.7 %collective-permute-done.24.refs_10_ = bf16[64,1536]{1,0:T(8,128)(2,1)S(1)} collective-permute-done((bf16[64,1536]{1,0:T(8,128)(2,1)}, bf16[64,1536]{1,0:T(8,128)(2,1)S(1)}, u32[]{:S(2)}, u32[]{:S(2)}) %collective-permute-start.24) | collective-permute-done | bytes 196640 | tf_op jit(solution)/shard_map/ppermute | solution.py:215
  559.0 11.3 shard_map.104
  583.7 11.4 shard_map.105
  613.2 11.5 shard_map.106
  629.9 14.4 %collective-permute-done.8.refs_9_ = bf16[64,1536]{1,0:T(8,128)(2,1)S(1)} collective-permute-done((bf16[64,1536]{1,0:T(8,128)(2,1)}, bf16[64,1536]{1,0:T(8,128)(2,1)S(1)}, u32[]{:S(2)}, u32[]{:S(2)}) %collective-permute-start.8) | collective-permute-done | bytes 196640 | tf_op jit(solution)/shard_map/ppermute | solution.py:215
  680.5 12.0 shard_map.108
  971.9 19.1 %collective-permute-done.233.refs_9_ = bf16[64,1536]{1,0:T(8,128)(2,1)} collective-permute-done((bf16[64,1536]{1,0:T(8,128)(2,1)}, bf16[64,1536]{1,0:T(8,128)(2,1)}, u32[]{:S(2)}, u32[]{:S(2)}) %collective-permute-start.233) | collective-permute-done | bytes 196640 | tf_op jit(solution)/shard_map/ppermute | solution.py:215
  1011.7 23.2 %collective-permute-done.236.refs_12_ = bf16[64,1536]{1,0:T(8,128)(2,1)S(1)} collective-permute-done((bf16[64,1536]{1,0:T(8,128)(2,1)}, bf16[64,1536]{1,0:T(8,128)(2,1)S(1)}, u32[]{:S(2)}, u32[]{:S(2)}) %collective-permute-start.236) | collective-permute-done | bytes 196640 | tf_op jit(solution)/shard_map/ppermute | solution.py:215
  1048.8 12.5 shard_map.109
  1065.9 24.1 %collective-permute-done.224.refs_15_ = bf16[64,1536]{1,0:T(8,128)(2,1)S(1)} collective-permute-done((bf16[64,1536]{1,0:T(8,128)(2,1)}, bf16[64,1536]{1,0:T(8,128)(2,1)S(1)}, u32[]{:S(2)}, u32[]{:S(2)}) %collective-permute-start.224) | collective-permute-done | bytes 196640 | tf_op jit(solution)/shard_map/ppermute | solution.py:215
  1091.1 12.3 shard_map.110
  1108.0 24.1 %collective-permute-done.209.refs_15_ = bf16[64,1536]{1,0:T(8,128)(2,1)S(1)} collective-permute-done((bf16[64,1536]{1,0:T(8,128)(2,1)S(1)}, bf16[64,1536]{1,0:T(8,128)(2,1)S(1)}, u32[]{:S(2)}, u32[]{:S(2)}) %collective-permute-start.209) | collective-permute-done | bytes 196640 | tf_op jit(solution)/shard_map/ppermute | solution.py:215
  1133.2 12.3 shard_map.111
  1150.2 24.1 %collective-permute-done.194.refs_15_ = bf16[64,1536]{1,0:T(8,128)(2,1)S(1)} collective-permute-done((bf16[64,1536]{1,0:T(8,128)(2,1)S(1)}, bf16[64,1536]{1,0:T(8,128)(2,1)S(1)}, u32[]{:S(2)}, u32[]{:S(2)}) %collective-permute-start.194) | collective-permute-done | bytes 196640 | tf_op jit(solution)/shard_map/ppermute | solution.py:215
  1175.3 12.6 shard_map.112
  1192.3 24.1 %collective-permute-done.179.refs_15_ = bf16[64,1536]{1,0:T(8,128)(2,1)S(1)} collective-permute-done((bf16[64,1536]{1,0:T(8,128)(2,1)S(1)}, bf16[64,1536]{1,0:T(8,128)(2,1)S(1)}, u32[]{:S(2)}, u32[]{:S(2)}) %collective-permute-start.179) | collective-permute-done | bytes 196640 | tf_op jit(solution)/shard_map/ppermute | solution.py:215
  1217.4 12.3 shard_map.113
  1234.4 24.1 %collective-permute-done.164.refs_15_ = bf16[64,1536]{1,0:T(8,128)(2,1)S(1)} collective-permute-done((bf16[64,1536]{1,0:T(8,128)(2,1)S(1)}, bf16[64,1536]{1,0:T(8,128)(2,1)S(1)}, u32[]{:S(2)}, u32[]{:S(2)}) %collective-permute-start.164) | collective-permute-done | bytes 196640 | tf_op jit(solution)/shard_map/ppermute | solution.py:215
  1259.6 12.3 shard_map.114
  1276.6 24.1 %collective-permute-done.149.refs_15_ = bf16[64,1536]{1,0:T(8,128)(2,1)S(1)} collective-permute-done((bf16[64,1536]{1,0:T(8,128)(2,1)S(1)}, bf16[64,1536]{1,0:T(8,128)(2,1)S(1)}, u32[]{:S(2)}, u32[]{:S(2)}) %collective-permute-start.149) | collective-permute-done | bytes 196640 | tf_op jit(solution)/shard_map/ppermute | solution.py:215
  1301.7 12.5 shard_map.115
  1321.8 12.0 shard_map.116
  (1436 shorter events, 814.6 us)
Async XLA Ops:
  38.8 42.6 %collective-permute-start.116 = (bf16[64,1536]{1,0:T(8,128)(2,1)S(1)}, bf16[64,1536]{1,0:T(8,128)(2,1)S(1)}, u32[]{:S(2)}, u32[]{:S(2)}) collective-permute-start(bf16[64,1536]{1,0:T(8,128)(2,1)S(1)} %get-tuple-element.417), channel_id=1, source_target_pairs={{0,12},{1,13},{2,14},{3,15},{4,8},{5,9},{6,10},{7,11},{8,4},{9,5},... | collective-permute-start | bytes 589832 | tf_op jit(solution)/shard_map/ppermute | solution.py:215
  40.9 44.1 %collective-permute-start.117 = (bf16[64,1536]{1,0:T(8,128)(2,1)S(1)}, bf16[64,1536]{1,0:T(8,128)(2,1)S(1)}, u32[]{:S(2)}, u32[]{:S(2)}) collective-permute-start(bf16[64,1536]{1,0:T(8,128)(2,1)S(1)} %get-tuple-element.418), channel_id=1, source_target_pairs={{0,13},{1,12},{2,15},{3,14},{4,9},{5,8},{6,11},{7,10},{8,5},{9,4},... | collective-permute-start | bytes 589832 | tf_op jit(solution)/shard_map/ppermute | solution.py:215
  42.9 48.0 %collective-permute-start.118 = (bf16[64,1536]{1,0:T(8,128)(2,1)S(1)}, bf16[64,1536]{1,0:T(8,128)(2,1)S(1)}, u32[]{:S(2)}, u32[]{:S(2)}) collective-permute-start(bf16[64,1536]{1,0:T(8,128)(2,1)S(1)} %get-tuple-element.419), channel_id=1, source_target_pairs={{0,14},{1,15},{2,12},{3,13},{4,10},{5,11},{6,8},{7,9},{8,6},{9,7},... | collective-permute-start | bytes 589832 | tf_op jit(solution)/shard_map/ppermute | solution.py:215
  117.0 44.8 %collective-permute-start.102 = (bf16[64,1536]{1,0:T(8,128)(2,1)S(1)}, bf16[64,1536]{1,0:T(8,128)(2,1)S(1)}, u32[]{:S(2)}, u32[]{:S(2)}) collective-permute-start(bf16[64,1536]{1,0:T(8,128)(2,1)S(1)} %get-tuple-element.402), channel_id=1, source_target_pairs={{0,13},{1,12},{2,15},{3,14},{4,9},{5,8},{6,11},{7,10},{8,5},{9,4},... | collective-permute-start | bytes 589832 | tf_op jit(solution)/shard_map/ppermute | solution.py:215
  118.9 45.6 %collective-permute-start.103 = (bf16[64,1536]{1,0:T(8,128)(2,1)S(1)}, bf16[64,1536]{1,0:T(8,128)(2,1)S(1)}, u32[]{:S(2)}, u32[]{:S(2)}) collective-permute-start(bf16[64,1536]{1,0:T(8,128)(2,1)S(1)} %get-tuple-element.403), channel_id=1, source_target_pairs={{0,14},{1,15},{2,12},{3,13},{4,10},{5,11},{6,8},{7,9},{8,6},{9,7},... | collective-permute-start | bytes 589832 | tf_op jit(solution)/shard_map/ppermute | solution.py:215
  187.2 44.0 %collective-permute-start.85 = (bf16[64,1536]{1,0:T(8,128)(2,1)S(1)}, bf16[64,1536]{1,0:T(8,128)(2,1)S(1)}, u32[]{:S(2)}, u32[]{:S(2)}) collective-permute-start(bf16[64,1536]{1,0:T(8,128)(2,1)S(1)} %get-tuple-element.384), channel_id=1, source_target_pairs={{0,11},{1,10},{2,9},{3,8},{4,15},{5,14},{6,13},{7,12},{8,3},{9,2},... | collective-permute-start | bytes 589832 | tf_op jit(solution)/shard_map/ppermute | solution.py:215
  190.8 43.7 %collective-permute-start.86 = (bf16[64,1536]{1,0:T(8,128)(2,1)S(1)}, bf16[64,1536]{1,0:T(8,128)(2,1)S(1)}, u32[]{:S(2)}, u32[]{:S(2)}) collective-permute-start(bf16[64,1536]{1,0:T(8,128)(2,1)S(1)} %get-tuple-element.385), channel_id=1, source_target_pairs={{0,12},{1,13},{2,14},{3,15},{4,8},{5,9},{6,10},{7,11},{8,4},{9,5},... | collective-permute-start | bytes 589832 | tf_op jit(solution)/shard_map/ppermute | solution.py:215
  193.1 45.5 %collective-permute-start.87 = (bf16[64,1536]{1,0:T(8,128)(2,1)S(1)}, bf16[64,1536]{1,0:T(8,128)(2,1)S(1)}, u32[]{:S(2)}, u32[]{:S(2)}) collective-permute-start(bf16[64,1536]{1,0:T(8,128)(2,1)S(1)} %get-tuple-element.386), channel_id=1, source_target_pairs={{0,13},{1,12},{2,15},{3,14},{4,9},{5,8},{6,11},{7,10},{8,5},{9,4},... | collective-permute-start | bytes 589832 | tf_op jit(solution)/shard_map/ppermute | solution.py:215
  268.5 43.4 %collective-permute-start.71 = (bf16[64,1536]{1,0:T(8,128)(2,1)S(1)}, bf16[64,1536]{1,0:T(8,128)(2,1)S(1)}, u32[]{:S(2)}, u32[]{:S(2)}) collective-permute-start(bf16[64,1536]{1,0:T(8,128)(2,1)S(1)} %copy-done.445), channel_id=1, source_target_pairs={{0,12},{1,13},{2,14},{3,15},{4,8},{5,9},{6,10},{7,11},{8,4},{9,5},... | collective-permute-start | bytes 589832 | tf_op jit(solution)/shard_map/ppermute | solution.py:215
  269.7 45.8 %collective-permute-start.72 = (bf16[64,1536]{1,0:T(8,128)(2,1)S(1)}, bf16[64,1536]{1,0:T(8,128)(2,1)S(1)}, u32[]{:S(2)}, u32[]{:S(2)}) collective-permute-start(bf16[64,1536]{1,0:T(8,128)(2,1)S(1)} %copy-done.443), channel_id=1, source_target_pairs={{0,13},{1,12},{2,15},{3,14},{4,9},{5,8},{6,11},{7,10},{8,5},{9,4},... | collective-permute-start | bytes 589832 | tf_op jit(solution)/shard_map/ppermute | solution.py:215
  354.2 45.3 %collective-permute-start.56 = (bf16[64,1536]{1,0:T(8,128)(2,1)S(1)}, bf16[64,1536]{1,0:T(8,128)(2,1)S(1)}, u32[]{:S(2)}, u32[]{:S(2)}) collective-permute-start(bf16[64,1536]{1,0:T(8,128)(2,1)S(1)} %get-tuple-element.353), channel_id=1, source_target_pairs={{0,12},{1,13},{2,14},{3,15},{4,8},{5,9},{6,10},{7,11},{8,4},{9,5},... | collective-permute-start | bytes 589832 | tf_op jit(solution)/shard_map/ppermute | solution.py:215
  355.3 47.8 %collective-permute-start.57 = (bf16[64,1536]{1,0:T(8,128)(2,1)S(1)}, bf16[64,1536]{1,0:T(8,128)(2,1)S(1)}, u32[]{:S(2)}, u32[]{:S(2)}) collective-permute-start(bf16[64,1536]{1,0:T(8,128)(2,1)S(1)} %get-tuple-element.354), channel_id=1, source_target_pairs={{0,13},{1,12},{2,15},{3,14},{4,9},{5,8},{6,11},{7,10},{8,5},{9,4},... | collective-permute-start | bytes 589832 | tf_op jit(solution)/shard_map/ppermute | solution.py:215
  431.6 46.8 %collective-permute-start.40 = (bf16[64,1536]{1,0:T(8,128)(2,1)}, bf16[64,1536]{1,0:T(8,128)(2,1)S(1)}, u32[]{:S(2)}, u32[]{:S(2)}) collective-permute-start(bf16[64,1536]{1,0:T(8,128)(2,1)} %get-tuple-element.336), channel_id=1, source_target_pairs={{0,11},{1,10},{2,9},{3,8},{4,15},{5,14},{6,13},{7,12},{8,3},{9,2},... | collective-permute-start | bytes 589832 | tf_op jit(solution)/shard_map/ppermute | solution.py:215
  434.7 44.4 %collective-permute-start.41 = (bf16[64,1536]{1,0:T(8,128)(2,1)}, bf16[64,1536]{1,0:T(8,128)(2,1)}, u32[]{:S(2)}, u32[]{:S(2)}) collective-permute-start(bf16[64,1536]{1,0:T(8,128)(2,1)} %get-tuple-element.337), channel_id=1, source_target_pairs={{0,12},{1,13},{2,14},{3,15},{4,8},{5,9},{6,10},{7,11},{8,4},{9,5},... | collective-permute-start | bytes 589832 | tf_op jit(solution)/shard_map/ppermute | solution.py:215
  435.5 44.8 %collective-permute-start.42 = (bf16[64,1536]{1,0:T(8,128)(2,1)}, bf16[64,1536]{1,0:T(8,128)(2,1)}, u32[]{:S(2)}, u32[]{:S(2)}) collective-permute-start(bf16[64,1536]{1,0:T(8,128)(2,1)} %get-tuple-element.338), channel_id=1, source_target_pairs={{0,13},{1,12},{2,15},{3,14},{4,9},{5,8},{6,11},{7,10},{8,5},{9,4},... | collective-permute-start | bytes 589832 | tf_op jit(solution)/shard_map/ppermute | solution.py:215
  436.5 46.8 %collective-permute-start.43 = (bf16[64,1536]{1,0:T(8,128)(2,1)}, bf16[64,1536]{1,0:T(8,128)(2,1)}, u32[]{:S(2)}, u32[]{:S(2)}) collective-permute-start(bf16[64,1536]{1,0:T(8,128)(2,1)} %get-tuple-element.339), channel_id=1, source_target_pairs={{0,14},{1,15},{2,12},{3,13},{4,10},{5,11},{6,8},{7,9},{8,6},{9,7},... | collective-permute-start | bytes 589832 | tf_op jit(solution)/shard_map/ppermute | solution.py:215
  516.2 42.8 %collective-permute-start.24 = (bf16[64,1536]{1,0:T(8,128)(2,1)}, bf16[64,1536]{1,0:T(8,128)(2,1)S(1)}, u32[]{:S(2)}, u32[]{:S(2)}) collective-permute-start(bf16[64,1536]{1,0:T(8,128)(2,1)} %copy-done.414), channel_id=1, source_target_pairs={{0,10},{1,11},{2,8},{3,9},{4,14},{5,15},{6,12},{7,13},{8,2},{9,3},... | collective-permute-start | bytes 589832 | tf_op jit(solution)/shard_map/ppermute | solution.py:215
  539.1 43.0 %collective-permute-start.28 = (bf16[64,1536]{1,0:T(8,128)(2,1)S(1)}, bf16[64,1536]{1,0:T(8,128)(2,1)S(1)}, u32[]{:S(2)}, u32[]{:S(2)}) collective-permute-start(bf16[64,1536]{1,0:T(8,128)(2,1)S(1)} %copy-done.401), channel_id=1, source_target_pairs={{0,14},{1,15},{2,12},{3,13},{4,10},{5,11},{6,8},{7,9},{8,6},{9,7},... | collective-permute-start | bytes 589832 | tf_op jit(solution)/shard_map/ppermute | solution.py:215
  627.4 44.9 %collective-permute-start.10 = (bf16[64,1536]{1,0:T(8,128)(2,1)S(1)}, bf16[64,1536]{1,0:T(8,128)(2,1)S(1)}, u32[]{:S(2)}, u32[]{:S(2)}) collective-permute-start(bf16[64,1536]{1,0:T(8,128)(2,1)S(1)} %copy-done.373), channel_id=1, source_target_pairs={{0,11},{1,10},{2,9},{3,8},{4,15},{5,14},{6,13},{7,12},{8,3},{9,2},... | collective-permute-start | bytes 589832 | tf_op jit(solution)/shard_map/ppermute | solution.py:215
  628.4 43.9 %collective-permute-start.11 = (bf16[64,1536]{1,0:T(8,128)(2,1)S(1)}, bf16[64,1536]{1,0:T(8,128)(2,1)S(1)}, u32[]{:S(2)}, u32[]{:S(2)}) collective-permute-start(bf16[64,1536]{1,0:T(8,128)(2,1)S(1)} %copy-done.371), channel_id=1, source_target_pairs={{0,12},{1,13},{2,14},{3,15},{4,8},{5,9},{6,10},{7,11},{8,4},{9,5},... | collective-permute-start | bytes 589832 | tf_op jit(solution)/shard_map/ppermute | solution.py:215
  629.3 43.0 %collective-permute-start.12 = (bf16[64,1536]{1,0:T(8,128)(2,1)S(1)}, bf16[64,1536]{1,0:T(8,128)(2,1)S(1)}, u32[]{:S(2)}, u32[]{:S(2)}) collective-permute-start(bf16[64,1536]{1,0:T(8,128)(2,1)S(1)} %copy-done.367), channel_id=1, source_target_pairs={{0,13},{1,12},{2,15},{3,14},{4,9},{5,8},{6,11},{7,10},{8,5},{9,4},... | collective-permute-start | bytes 589832 | tf_op jit(solution)/shard_map/ppermute | solution.py:215
  970.6 64.3 %collective-permute-start.236 = (bf16[64,1536]{1,0:T(8,128)(2,1)}, bf16[64,1536]{1,0:T(8,128)(2,1)S(1)}, u32[]{:S(2)}, u32[]{:S(2)}) collective-permute-start(bf16[64,1536]{1,0:T(8,128)(2,1)} %copy-done.263), channel_id=1, source_target_pairs={{0,12},{1,13},{2,14},{3,15},{4,8},{5,9},{6,10},{7,11},{8,4},{9,5},... | collective-permute-start | bytes 589832 | tf_op jit(solution)/shard_map/ppermute | solution.py:215
  971.8 65.9 %collective-permute-start.237 = (bf16[64,1536]{1,0:T(8,128)(2,1)}, bf16[64,1536]{1,0:T(8,128)(2,1)S(1)}, u32[]{:S(2)}, u32[]{:S(2)}) collective-permute-start(bf16[64,1536]{1,0:T(8,128)(2,1)} %copy-done.261), channel_id=1, source_target_pairs={{0,13},{1,12},{2,15},{3,14},{4,9},{5,8},{6,11},{7,10},{8,5},{9,4},... | collective-permute-start | bytes 589832 | tf_op jit(solution)/shard_map/ppermute | solution.py:215
  991.0 52.6 %collective-permute-start.238 = (bf16[64,1536]{1,0:T(8,128)(2,1)}, bf16[64,1536]{1,0:T(8,128)(2,1)S(1)}, u32[]{:S(2)}, u32[]{:S(2)}) collective-permute-start(bf16[64,1536]{1,0:T(8,128)(2,1)} %copy-done.260), channel_id=1, source_target_pairs={{0,14},{1,15},{2,12},{3,13},{4,10},{5,11},{6,8},{7,9},{8,6},{9,7},... | collective-permute-start | bytes 589832 | tf_op jit(solution)/shard_map/ppermute | solution.py:215
  995.2 52.6 %collective-permute-start.239 = (bf16[64,1536]{1,0:T(8,128)(2,1)}, bf16[64,1536]{1,0:T(8,128)(2,1)S(1)}, u32[]{:S(2)}, u32[]{:S(2)}) collective-permute-start(bf16[64,1536]{1,0:T(8,128)(2,1)} %copy-done.259), channel_id=1, source_target_pairs={{0,15},{1,14},{2,13},{3,12},{4,11},{5,10},{6,9},{7,8},{8,7},{9,6},... | collective-permute-start | bytes 589832 | tf_op jit(solution)/shard_map/ppermute | solution.py:215
  1007.9 53.4 %collective-permute-start.220 = (bf16[64,1536]{1,0:T(8,128)(2,1)}, bf16[64,1536]{1,0:T(8,128)(2,1)S(1)}, u32[]{:S(2)}, u32[]{:S(2)}) collective-permute-start(bf16[64,1536]{1,0:T(8,128)(2,1)} %copy-done.274), channel_id=1, source_target_pairs={{0,11},{1,10},{2,9},{3,8},{4,15},{5,14},{6,13},{7,12},{8,3},{9,2},... | collective-permute-start | bytes 589832 | tf_op jit(solution)/shard_map/ppermute | solution.py:215
  1145.5 42.4 %collective-permute-start.175 = (bf16[64,1536]{1,0:T(8,128)(2,1)S(1)}, bf16[64,1536]{1,0:T(8,128)(2,1)S(1)}, u32[]{:S(2)}, u32[]{:S(2)}) collective-permute-start(bf16[64,1536]{1,0:T(8,128)(2,1)S(1)} %copy-done.307), channel_id=1, source_target_pairs={{0,11},{1,10},{2,9},{3,8},{4,15},{5,14},{6,13},{7,12},{8,3},{9,2},... | collective-permute-start | bytes 589832 | tf_op jit(solution)/shard_map/ppermute | solution.py:215
  1145.6 42.4 %collective-permute-start.176 = (bf16[64,1536]{1,0:T(8,128)(2,1)S(1)}, bf16[64,1536]{1,0:T(8,128)(2,1)S(1)}, u32[]{:S(2)}, u32[]{:S(2)}) collective-permute-start(bf16[64,1536]{1,0:T(8,128)(2,1)S(1)} %copy-done.303), channel_id=1, source_target_pairs={{0,12},{1,13},{2,14},{3,15},{4,8},{5,9},{6,10},{7,11},{8,4},{9,5},... | collective-permute-start | bytes 589832 | tf_op jit(solution)/shard_map/ppermute | solution.py:215
  1146.8 42.4 %collective-permute-start.177 = (bf16[64,1536]{1,0:T(8,128)(2,1)S(1)}, bf16[64,1536]{1,0:T(8,128)(2,1)S(1)}, u32[]{:S(2)}, u32[]{:S(2)}) collective-permute-start(bf16[64,1536]{1,0:T(8,128)(2,1)S(1)} %copy-done.299), channel_id=1, source_target_pairs={{0,13},{1,12},{2,15},{3,14},{4,9},{5,8},{6,11},{7,10},{8,5},{9,4},... | collective-permute-start | bytes 589832 | tf_op jit(solution)/shard_map/ppermute | solution.py:215
  1271.9 42.3 %collective-permute-start.130 = (bf16[64,1536]{1,0:T(8,128)(2,1)S(1)}, bf16[64,1536]{1,0:T(8,128)(2,1)S(1)}, u32[]{:S(2)}, u32[]{:S(2)}) collective-permute-start(bf16[64,1536]{1,0:T(8,128)(2,1)S(1)} %copy-done.331), channel_id=1, source_target_pairs={{0,11},{1,10},{2,9},{3,8},{4,15},{5,14},{6,13},{7,12},{8,3},{9,2},... | collective-permute-start | bytes 589832 | tf_op jit(solution)/shard_map/ppermute | solution.py:215
  1272.0 43.8 %collective-permute-start.131 = (bf16[64,1536]{1,0:T(8,128)(2,1)S(1)}, bf16[64,1536]{1,0:T(8,128)(2,1)S(1)}, u32[]{:S(2)}, u32[]{:S(2)}) collective-permute-start(bf16[64,1536]{1,0:T(8,128)(2,1)S(1)} %copy-done.327), channel_id=1, source_target_pairs={{0,12},{1,13},{2,14},{3,15},{4,8},{5,9},{6,10},{7,11},{8,4},{9,5},... | collective-permute-start | bytes 589832 | tf_op jit(solution)/shard_map/ppermute | solution.py:215
  1273.2 42.6 %collective-permute-start.132 = (bf16[64,1536]{1,0:T(8,128)(2,1)S(1)}, bf16[64,1536]{1,0:T(8,128)(2,1)S(1)}, u32[]{:S(2)}, u32[]{:S(2)}) collective-permute-start(bf16[64,1536]{1,0:T(8,128)(2,1)S(1)} %copy-done.321), channel_id=1, source_target_pairs={{0,13},{1,12},{2,15},{3,14},{4,9},{5,8},{6,11},{7,10},{8,5},{9,4},... | collective-permute-start | bytes 589832 | tf_op jit(solution)/shard_map/ppermute | solution.py:215
  (672 other events, 21349.8 us)

commit v2 on v1

--- a/solution.py
+++ b/solution.py
@@ -1,8 +1,8 @@
-import functools
 import math
 
 import jax
 import jax.numpy as jnp
+import numpy as np
 from jax import lax
 from jax.experimental import pallas as pl
 from jax.experimental.pallas import tpu as pltpu
@@ -11,7 +11,10 @@
 keep_rate = 0.9
 CHUNKS = 8
 TILE = 512
-VMEM_LIMIT = 44 * 1024 * 1024
+VMEM_LIMIT = 60 * 1024 * 1024
+FIRST_LAG = 4
+SECOND_LAG = 2
+ANY = pl.BlockSpec(memory_space=pl.ANY)
 NT = (((1,), (1,)), ((), ()))
 TN = (((0,), (0,)), ((), ()))
 NN = (((1,), (0,)), ((), ()))
@@ -28,6 +31,11 @@
         self.pair = 2 if self.direct else own
         self.pairs = own // self.pair
         self.slots = devices if self.direct else 1
+        quarter = max(devices // 4, 1)
+        near, far = list(range(devices // 2)), list(range(devices // 2, devices))
+        near = [hop for both in zip(near[:quarter], near[quarter:]) for hop in both]
+        far = [hop for both in zip(far[:quarter], far[quarter:]) for hop in both]
+        self.hops = [hop for both in zip(near, far) for hop in both]
         self.height = devices * own * own
         self.slot_height = self.height // self.slots
         self.width = own * order
@@ -72,17 +80,17 @@
     )(*ins)
 
 
-def first_factor(plan, chunk, tokens, wide_left):
-    def body(tokens_ref, left_ref, *out_refs):
+def first_factor(plan, chunk, tokens, wide_left, after):
+    def body(tokens_ref, left_ref, *refs):
         product = dot(left_ref[...], tokens_ref[...], NT).astype(jnp.bfloat16)
-        for slot, ref in enumerate(out_refs):
+        for slot, ref in enumerate(refs[len(after) :]):
             ref[...] = product[slot * plan.slot_height : (slot + 1) * plan.slot_height, :]
 
     return call(
         body,
         plan,
-        (tokens, wide_left),
-        [plan.token_spec(chunk), whole(wide_left)],
+        (tokens, wide_left, *after),
+        [plan.token_spec(chunk), whole(wide_left), *[ANY] * len(after)],
         plan.slot_shapes(),
         plan.slot_specs(),
         {},
@@ -90,7 +98,7 @@
     )
 
 
-def second_factor(plan, chunk, received, tokens, cotangent, keep_mask, spread, wide_right, state):
+def second_factor(plan, chunk, received, tokens, cotangent, keep_mask, spread, wide_right, state, after):
     slots, span = plan.slots, plan.pair * plan.order
 
     def body(*refs):
@@ -141,7 +149,9 @@
     if state is not None:
         aliases = {len(ins): slots, len(ins) + 1: slots + 1}
         ins = (*ins, *state)
-        in_specs += [pl.BlockSpec(memory_space=pl.ANY), whole(state[1])]
+        in_specs += [ANY, whole(state[1])]
+    ins = (*ins, *after)
+    in_specs += [ANY] * len(after)
     outs = [
         *plan.slot_shapes(),
         jax.ShapeDtypeStruct(tokens.shape, jnp.bfloat16),
@@ -190,7 +200,7 @@
     if state is not None:
         aliases = {len(ins): 0, len(ins) + 1: 1}
         ins = (*ins, *state)
-        in_specs += [pl.BlockSpec(memory_space=pl.ANY), whole(state[1])]
+        in_specs += [ANY, whole(state[1])]
     outs = [
         jax.ShapeDtypeStruct(tokens.shape, jnp.bfloat16),
         jax.ShapeDtypeStruct((own, order, order), jnp.float32),
@@ -212,8 +222,8 @@
 def exchange(plan, parts):
     if plan.direct:
         return [
-            part if slot == 0 else lax.ppermute(part, "blk", [(i, i ^ slot) for i in range(plan.devices)])
-            for slot, part in enumerate(parts)
+            part if hop == 0 else lax.ppermute(part, "blk", [(i, i ^ hop) for i in range(plan.devices)])
+            for hop, part in zip(plan.hops, parts)
         ]
     split = parts[0].reshape(plan.devices, plan.own * plan.own, plan.chunk)
     return [lax.all_to_all(split, "blk", 0, 0, tiled=True).reshape(plan.height, plan.chunk)]
@@ -231,9 +241,10 @@
     devices = lax.axis_size("blk")
     plan = Plan(rows, own, order, devices)
     pair, pairs, span = plan.pair, plan.pairs, plan.pair * order
-    partner = lax.iota(jnp.int32, devices)
+    partner = place = lax.iota(jnp.int32, devices)
     if plan.direct:
-        partner = partner ^ lax.axis_index("blk")
+        place = jnp.take(jnp.array(np.argsort(plan.hops), jnp.int32), place ^ lax.axis_index("blk"))
+        partner = jnp.array(plan.hops, jnp.int32) ^ lax.axis_index("blk")
     factor = 1.0 / math.sqrt(rows * lax.axis_size("dp"))
 
     selector = (channel_order[:, None] == lax.broadcasted_iota(jnp.int32, (order, order), 1)).astype(jnp.bfloat16)
@@ -250,27 +261,30 @@
     )
     spread = jnp.repeat(eye, order, axis=1)
 
-    forward = [
-        exchange(plan, first_factor(plan, chunk, tokens, wide_left)) for chunk in range(plan.chunks)
-    ]
-    state, backward = None, []
-    for chunk in range(plan.chunks):
-        sent, state = second_factor(
-            plan, chunk, forward[chunk], tokens, cotangent, keep_mask, spread, wide_right, state
-        )
-        backward.append(exchange(plan, sent))
+    forward, backward, state = [], [], None
+    for step in range(plan.chunks + SECOND_LAG):
+        if step < plan.chunks:
+            after = backward[step - FIRST_LAG][1:] if step >= FIRST_LAG else []
+            forward.append(exchange(plan, first_factor(plan, step, tokens, wide_left, after)))
+        chunk = step - SECOND_LAG
+        if chunk >= 0:
+            after = backward[chunk - SECOND_LAG][1:] if chunk >= SECOND_LAG else []
+            sent, state = second_factor(
+                plan, chunk, forward[chunk], tokens, cotangent, keep_mask, spread, wide_right, state, after
+            )
+            backward.append(exchange(plan, sent))
     mixed, wide_total = state
 
     split_total = wide_total.reshape(pairs, devices, pair, own, pair, order)
     part_right = jnp.stack([split_total[:, :, jj, :, jj, :] for jj in range(pair)], axis=1)
-    part_right = jnp.take(part_right.reshape(own, devices, own, order), partner, axis=1).reshape(own, order, order)
+    part_right = jnp.take(part_right.reshape(own, devices, own, order), place, axis=1).reshape(own, order, order)
     grad_right = sum_over_dp(part_right.astype(jnp.bfloat16)) * factor
 
     state = None
     for chunk in range(plan.chunks):
         state = first_factor_back(plan, chunk, backward[chunk], tokens, cotangent, wide_left, state)
     grad_tokens, part_left = state
-    part_left = jnp.take(part_left.astype(jnp.bfloat16).reshape(own, devices, own, order), partner, axis=1)
+    part_left = jnp.take(part_left.astype(jnp.bfloat16).reshape(own, devices, own, order), place, axis=1)
     part_left = jnp.einsum(
         "km,bom->bko", selector, part_left.reshape(own, order, order), preferred_element_type=jnp.float32
     ).astype(jnp.bfloat16)

time: 1350 us -> 1210 us (0.90)
  local copies, waits for them, and re-layouts: 146 us -> 14.4 us
  waiting for transfers between devices: 639 us -> 534 us
  starting transfers between devices: 312 us -> 378 us
  Pallas kernels: 237 us -> 257 us
    unnamed x927 -> x433, local copies, waits for them, and re-layouts: 136 us -> 7.08 us
    ppermute x240, waiting for transfers between devices: 633 us -> 528 us  [exchange(): lax.ppermute(part, 'blk', [(i, i ^ hop) for i in range(plan.devices)])]
    ppermute x240, starting transfers between devices: 309 us -> 375 us  [exchange(): lax.ppermute(part, 'blk', [(i, i ^ hop) for i in range(plan.devices)])]
    pallas_call x24, Pallas kernels: 237 us -> 257 us  [call(): pl.pallas_call(body, out_shape=outs, grid=(plan.steps,), in_specs=in_spec...]
  transfers between devices with their start and end apart: 242 -> 242, of which waited for: 113 -> 81; matrix products, arithmetic and copies ran while one was open for 1% -> 1% of each run, Pallas kernels for 16% -> 21%
where the time goes in v2:
time: 1210 us; the launch traced here: 1190 us
  waiting for transfers between devices  534 us (44%)
  starting transfers between devices  378 us (31%)
  Pallas kernels  257 us (21%)
  local copies, waits for them, and re-layouts  14.4 us (1%)
    ppermute x240, waiting for transfers between devices, exchange(): lax.ppermute(part, 'blk', [(i, i ^ hop) for i in range(plan.devices)])  528 us
    ppermute x240, starting transfers between devices, exchange(): lax.ppermute(part, 'blk', [(i, i ^ hop) for i in range(plan.devices)])  375 us
    pallas_call x24, Pallas kernels, call(): pl.pallas_call(body, out_shape=outs, grid=(plan.steps,), in_specs=in_spec...  257 us
  transfers between devices with their start and end apart: 242, of which 81 were waited for; matrix products, arithmetic and copies ran while one was open for 1% of the time, Pallas kernels for 21%

profile of v2, /device:TPU:16, one launch (start us, length us, event | category | flops | bytes accessed | tf_op | source)
XLA Modules:
  0.0 1194.5 jit_solution(7848630413961092435)
XLA Ops:
  29.6 11.6 collective-permute-done.47.refs_3_
  126.8 12.3 %collective-permute-start.43 = (bf16[64,1536]{1,0:T(8,128)(2,1)}, bf16[64,1536]{1,0:T(8,128)(2,1)}, u32[]{:S(2)}, u32[]{:S(2)}) collective-permute-start(bf16[64,1536]{1,0:T(8,128)(2,1)} %get-tuple-element.339), channel_id=1, source_target_pairs={{0,7},{1,6},{2,5},{3,4},{4,3},{5,2},{6,1},{7,0},{8,15},{9,14},{10,... | collective-permute-start | bytes 589832 | tf_op jit(solution)/shard_map/ppermute | solution.py:225
  154.7 14.6 %collective-permute-done.44.refs_15_ = bf16[64,1536]{1,0:T(8,128)(2,1)} collective-permute-done((bf16[64,1536]{1,0:T(8,128)(2,1)}, bf16[64,1536]{1,0:T(8,128)(2,1)}, u32[]{:S(2)}, u32[]{:S(2)}) %collective-permute-start.44) | collective-permute-done | bytes 196640 | tf_op jit(solution)/shard_map/ppermute | solution.py:225
  282.4 11.8 shard_map.115
  332.9 12.0 %collective-permute-done.68.refs_31_.refs_8_.refs_9_ = bf16[64,1536]{1,0:T(8,128)(2,1)S(1)} collective-permute-done((bf16[64,1536]{1,0:T(8,128)(2,1)}, bf16[64,1536]{1,0:T(8,128)(2,1)S(1)}, u32[]{:S(2)}, u32[]{:S(2)}) %collective-permute-start.68) | collective-permute-done | bytes 196640 | tf_op jit(solution)/shard_map/ppermute | solution.py:225
  350.0 12.0 %shard_map.116 = (bf16[64,1536]{1,0:T(8,128)(2,1)}, bf16[64,1536]{1,0:T(8,128)(2,1)}, bf16[64,1536]{1,0:T(8,128)(2,1)}, bf16[64,1536]{1,0:T(8,128)(2,1)}, bf16[6...) custom-call(bf16[64,1536]{1,0:T(8,128)(2,1)} %get-tuple-element.325., ...), custom_call_target="tpu_custom_call", output_to_operand_aliasing={{16}: (21, {}), {17}: (22, {})} | custom-call | flops 9663676416 | bytes 12582912 | tf_op jit(solution)/shard_map/pallas_call | solution.py:70
  368.6 12.7 %collective-permute-done.75.refs_23_.refs_0_.refs_1_ = bf16[64,1536]{1,0:T(8,128)(2,1)S(1)} collective-permute-done((bf16[64,1536]{1,0:T(8,128)(2,1)}, bf16[64,1536]{1,0:T(8,128)(2,1)S(1)}, u32[]{:S(2)}, u32[]{:S(2)}) %collective-permute-start.75) | collective-permute-done | bytes 196640 | tf_op jit(solution)/shard_map/ppermute | solution.py:225
  386.8 11.3 collective-permute-done.79.refs_27_.refs_4_.refs_5_
  434.2 11.3 collective-permute-done.89.refs_37_.refs_14_.refs_15_
  455.3 11.3 collective-permute-done.169.refs_5_
  487.0 12.2 %shard_map.117 = (bf16[64,1536]{1,0:T(8,128)(2,1)}, bf16[64,1536]{1,0:T(8,128)(2,1)}, bf16[64,1536]{1,0:T(8,128)(2,1)}, bf16[64,1536]{1,0:T(8,128)(2,1)}, bf16[6...) custom-call(bf16[64,1536]{1,0:T(8,128)(2,1)} %get-tuple-element.309., ...), custom_call_target="tpu_custom_call", output_to_operand_aliasing={{16}: (21, {}), {17}: (22, {})} | custom-call | flops 9663676416 | bytes 12582912 | tf_op jit(solution)/shard_map/pallas_call | solution.py:70
  511.0 10.9 collective-permute-start.125
  575.1 12.7 %collective-permute-done.150.refs_1_ = bf16[64,1536]{1,0:T(8,128)(2,1)} collective-permute-done((bf16[64,1536]{1,0:T(8,128)(2,1)}, bf16[64,1536]{1,0:T(8,128)(2,1)}, u32[]{:S(2)}, u32[]{:S(2)}) %collective-permute-start.150) | collective-permute-done | bytes 196640 | tf_op jit(solution)/shard_map/ppermute | solution.py:225
  611.0 10.6 collective-permute-done.158.refs_9_
  625.7 12.0 %shard_map.118 = (bf16[64,1536]{1,0:T(8,128)(2,1)}, bf16[64,1536]{1,0:T(8,128)(2,1)}, bf16[64,1536]{1,0:T(8,128)(2,1)}, bf16[64,1536]{1,0:T(8,128)(2,1)}, bf16[6...) custom-call(bf16[64,1536]{1,0:T(8,128)(2,1)} %get-tuple-element.293., ...), custom_call_target="tpu_custom_call", output_to_operand_aliasing={{16}: (21, {}), {17}: (22, {})} | custom-call | flops 9663676416 | bytes 12582912 | tf_op jit(solution)/shard_map/pallas_call | solution.py:70
  646.5 10.8 collective-permute-done.100.refs_10_.refs_33_.refs_11_
  703.2 12.4 %shard_map.123 = (bf16[64,1536]{1,0:T(8,128)(2,1)}, bf16[64,1536]{1,0:T(8,128)(2,1)}, bf16[64,1536]{1,0:T(8,128)(2,1)}, bf16[64,1536]{1,0:T(8,128)(2,1)}, bf16[6...) custom-call(bf16[64,1536]{1,0:T(8,128)(2,1)} %get-tuple-element.471., ...), custom_call_target="tpu_custom_call", output_to_operand_aliasing={{16}: (21, {}), {17}: (22, {})} | custom-call | flops 9663676416 | bytes 12582912 | tf_op jit(solution)/shard_map/pallas_call | solution.py:70
  792.3 11.3 collective-permute-done.135.refs_1_
  843.8 12.1 %shard_map.124 = (bf16[64,1536]{1,0:T(8,128)(2,1)}, bf16[64,1536]{1,0:T(8,128)(2,1)}, bf16[64,1536]{1,0:T(8,128)(2,1)}, bf16[64,1536]{1,0:T(8,128)(2,1)}, bf16[6...) custom-call(bf16[64,1536]{1,0:T(8,128)(2,1)} %get-tuple-element.455., ...), custom_call_target="tpu_custom_call", output_to_operand_aliasing={{16}: (21, {}), {17}: (22, {})} | custom-call | flops 9663676416 | bytes 12582912 | tf_op jit(solution)/shard_map/pallas_call | solution.py:70
  861.0 13.3 %shard_map.127 = (bf16[12288,1024]{1,0:T(8,128)(2,1)}, f32[8,128,128]{2,1,0:T(8,128)}) custom-call(bf16[64,1536]{1,0:T(8,128)(2,1)} %get-tuple-element.563.refs_0_, bf16[64,1536]{1,0:T(8,128)(2,1)} %copy-done.2, bf16[64,1536]{1,0:T(8,128)(2,1)} %copy-done.3, bf16[64,1536]{1,0:T(8,128)(2,1)} %copy-done.4, bf16[64,1536]{1,0:T(8,128)(2,1)} %copy-done.5, ...), custom_call_target="tpu_custom_call" | custom-call | flops 6442450944 | bytes 102760448 | tf_op jit(solution)/shard_map/pallas_call | solution.py:70
  894.3 13.2 %shard_map.128 = (bf16[12288,1024]{1,0:T(8,128)(2,1)}, f32[8,128,128]{2,1,0:T(8,128)}) custom-call(bf16[64,1536]{1,0:T(8,128)(2,1)} %get-tuple-element.562.refs_0_, bf16[64,1536]{1,0:T(8,128)(2,1)} %copy-done.16, bf16[64,1536]{1,0:T(8,128)(2,1)} %copy-done.18, bf16[64,1536]{1,0:T(8,128)(2,1)} %copy-done.19, ...), custom_call_target="tpu_custom_call", output_to_operand_aliasing={{0}: (19, {}), {1}: (20, {})} | custom-call | flops 6442450944 | bytes 102760448 | tf_op jit(solution)/shard_map/pallas_call | solution.py:70
  920.2 12.7 %collective-permute-done.205.refs_33_.refs_11_ = bf16[64,1536]{1,0:T(8,128)(2,1)S(1)} collective-permute-done((bf16[64,1536]{1,0:T(8,128)(2,1)S(1)}, bf16[64,1536]{1,0:T(8,128)(2,1)S(1)}, u32[]{:S(2)}, u32[]{:S(2)}) %collective-permute-start.205) | collective-permute-done | bytes 196640 | tf_op jit(solution)/shard_map/ppermute | solution.py:225
  936.4 11.1 collective-permute-done.209.refs_37_.refs_15_
  947.5 13.3 %shard_map.129 = (bf16[12288,1024]{1,0:T(8,128)(2,1)}, f32[8,128,128]{2,1,0:T(8,128)}) custom-call(bf16[64,1536]{1,0:T(8,128)(2,1)} %get-tuple-element.561.refs_0_, bf16[64,1536]{1,0:T(8,128)(2,1)} %copy-done.32, bf16[64,1536]{1,0:T(8,128)(2,1)} %copy-done.33, bf16[64,1536]{1,0:T(8,128)(2,1)} %copy-done.34, ...), custom_call_target="tpu_custom_call", output_to_operand_aliasing={{0}: (19, {}), {1}: (20, {})} | custom-call | flops 6442450944 | bytes 102760448 | tf_op jit(solution)/shard_map/pallas_call | solution.py:70
  967.0 13.5 %shard_map.130 = (bf16[12288,1024]{1,0:T(8,128)(2,1)}, f32[8,128,128]{2,1,0:T(8,128)}) custom-call(bf16[64,1536]{1,0:T(8,128)(2,1)} %get-tuple-element.560.refs_0_, bf16[64,1536]{1,0:T(8,128)(2,1)} %copy-done.52, bf16[64,1536]{1,0:T(8,128)(2,1)} %copy-done.53, bf16[64,1536]{1,0:T(8,128)(2,1)} %copy-done.54, ...), custom_call_target="tpu_custom_call", output_to_operand_aliasing={{0}: (19, {}), {1}: (20, {})} | custom-call | flops 6442450944 | bytes 102760448 | tf_op jit(solution)/shard_map/pallas_call | solution.py:70
  989.1 12.0 %shard_map.125 = (bf16[64,1536]{1,0:T(8,128)(2,1)}, bf16[64,1536]{1,0:T(8,128)(2,1)}, bf16[64,1536]{1,0:T(8,128)(2,1)}, bf16[64,1536]{1,0:T(8,128)(2,1)}, bf16[6...) custom-call(bf16[64,1536]{1,0:T(8,128)(2,1)} %get-tuple-element.439., ...), custom_call_target="tpu_custom_call", output_to_operand_aliasing={{16}: (21, {}), {17}: (22, {})} | custom-call | flops 9663676416 | bytes 12582912 | tf_op jit(solution)/shard_map/pallas_call | solution.py:70
  1012.1 12.4 %collective-permute-done.119.refs_15_ = bf16[64,1536]{1,0:T(8,128)(2,1)S(1)} collective-permute-done((bf16[64,1536]{1,0:T(8,128)(2,1)S(1)}, bf16[64,1536]{1,0:T(8,128)(2,1)S(1)}, u32[]{:S(2)}, u32[]{:S(2)}) %collective-permute-start.119) | collective-permute-done | bytes 196640 | tf_op jit(solution)/shard_map/ppermute | solution.py:225
  1025.2 12.0 %shard_map.126 = (bf16[64,1536]{1,0:T(8,128)(2,1)}, bf16[64,1536]{1,0:T(8,128)(2,1)}, bf16[64,1536]{1,0:T(8,128)(2,1)}, bf16[64,1536]{1,0:T(8,128)(2,1)}, bf16[6...) custom-call(bf16[64,1536]{1,0:T(8,128)(2,1)} %get-tuple-element.408., ...), custom_call_target="tpu_custom_call", output_to_operand_aliasing={{16}: (21, {}), {17}: (22, {})} | custom-call | flops 9663676416 | bytes 12582912 | tf_op jit(solution)/shard_map/pallas_call | solution.py:70
  1037.3 13.4 %shard_map.131 = (bf16[12288,1024]{1,0:T(8,128)(2,1)}, f32[8,128,128]{2,1,0:T(8,128)}) custom-call(bf16[64,1536]{1,0:T(8,128)(2,1)} %get-tuple-element.559.refs_0_, bf16[64,1536]{1,0:T(8,128)(2,1)} %copy-done.62, bf16[64,1536]{1,0:T(8,128)(2,1)} %copy-done.63, bf16[64,1536]{1,0:T(8,128)(2,1)} %copy-done.64, ...), custom_call_target="tpu_custom_call", output_to_operand_aliasing={{0}: (19, {}), {1}: (20, {})} | custom-call | flops 6442450944 | bytes 102760448 | tf_op jit(solution)/shard_map/pallas_call | solution.py:70
  1059.6 13.2 %shard_map.132 = (bf16[12288,1024]{1,0:T(8,128)(2,1)}, f32[8,128,128]{2,1,0:T(8,128)}) custom-call(bf16[64,1536]{1,0:T(8,128)(2,1)} %get-tuple-element.558.refs_0_, bf16[64,1536]{1,0:T(8,128)(2,1)} %copy-done.77, bf16[64,1536]{1,0:T(8,128)(2,1)} %copy-done.78, bf16[64,1536]{1,0:T(8,128)(2,1)} %copy-done.79, ...), custom_call_target="tpu_custom_call", output_to_operand_aliasing={{0}: (19, {}), {1}: (20, {})} | custom-call | flops 6442450944 | bytes 102760448 | tf_op jit(solution)/shard_map/pallas_call | solution.py:70
  1155.8 13.1 %shard_map.133 = (bf16[12288,1024]{1,0:T(8,128)(2,1)}, f32[8,128,128]{2,1,0:T(8,128)}) custom-call(bf16[64,1536]{1,0:T(8,128)(2,1)} %get-tuple-element.542.refs_0_, bf16[64,1536]{1,0:T(8,128)(2,1)} %copy-done.137, bf16[64,1536]{1,0:T(8,128)(2,1)} %copy-done.138, bf16[64,1536]{1,0:T(8,128)(2,1)} %copy-done.139, ...), custom_call_target="tpu_custom_call", output_to_operand_aliasing={{0}: (19, {}), {1}: (20, {})} | custom-call | flops 6442450944 | bytes 102760448 | tf_op jit(solution)/shard_map/pallas_call | solution.py:70
  1170.6 13.1 %shard_map.134 = (bf16[12288,1024]{1,0:T(8,128)(2,1)}, f32[8,128,128]{2,1,0:T(8,128)}) custom-call(bf16[64,1536]{1,0:T(8,128)(2,1)} %get-tuple-element.526.refs_0_, bf16[64,1536]{1,0:T(8,128)(2,1)} %copy-done.160, bf16[64,1536]{1,0:T(8,128)(2,1)} %copy-done.162, bf16[64,1536]{1,0:T(8,128)(2,1)} %copy-done.164, ...), custom_call_target="tpu_custom_call", output_to_operand_aliasing={{0}: (19, {}), {1}: (20, {})} | custom-call | flops 6442450944 | bytes 102760448 | tf_op jit(solution)/shard_map/pallas_call | solution.py:70
  (947 shorter events, 798.2 us)
Async XLA Ops:
  18.8 31.6 %collective-permute-start.49 = (bf16[64,1536]{1,0:T(8,128)(2,1)}, bf16[64,1536]{1,0:T(8,128)(2,1)S(1)}, u32[]{:S(2)}, u32[]{:S(2)}) collective-permute-start(bf16[64,1536]{1,0:T(8,128)(2,1)} %get-tuple-element.346), channel_id=1, source_target_pairs={{0,9},{1,8},{2,11},{3,10},{4,13},{5,12},{6,15},{7,14},{8,1},{9,0},... | collective-permute-start | bytes 589832 | tf_op jit(solution)/shard_map/ppermute | solution.py:225
  139.1 30.3 %collective-permute-start.44 = (bf16[64,1536]{1,0:T(8,128)(2,1)}, bf16[64,1536]{1,0:T(8,128)(2,1)}, u32[]{:S(2)}, u32[]{:S(2)}) collective-permute-start(bf16[64,1536]{1,0:T(8,128)(2,1)} %get-tuple-element.340), channel_id=1, source_target_pairs={{0,15},{1,14},{2,13},{3,12},{4,11},{5,10},{6,9},{7,8},{8,7},{9,6},... | collective-permute-start | bytes 589832 | tf_op jit(solution)/shard_map/ppermute | solution.py:225
  260.3 33.9 %collective-permute-start.5 = (bf16[64,1536]{1,0:T(8,128)(2,1)}, bf16[64,1536]{1,0:T(8,128)(2,1)S(1)}, u32[]{:S(2)}, u32[]{:S(2)}) collective-permute-start(bf16[64,1536]{1,0:T(8,128)(2,1)} %get-tuple-element.299), channel_id=1, source_target_pairs={{0,5},{1,4},{2,7},{3,6},{4,1},{5,0},{6,3},{7,2},{8,13},{9,12},{10,... | collective-permute-start | bytes 589832 | tf_op jit(solution)/shard_map/ppermute | solution.py:225
  329.0 33.1 %collective-permute-start.70 = (bf16[64,1536]{1,0:T(8,128)(2,1)}, bf16[64,1536]{1,0:T(8,128)(2,1)S(1)}, u32[]{:S(2)}, u32[]{:S(2)}) collective-permute-start(bf16[64,1536]{1,0:T(8,128)(2,1)} %get-tuple-element.371), channel_id=1, source_target_pairs={{0,14},{1,15},{2,12},{3,13},{4,10},{5,11},{6,8},{7,9},{8,6},{9,7},... | collective-permute-start | bytes 589832 | tf_op jit(solution)/shard_map/ppermute | solution.py:225
  332.9 30.1 %collective-permute-start.72 = (bf16[64,1536]{1,0:T(8,128)(2,1)}, bf16[64,1536]{1,0:T(8,128)(2,1)S(1)}, u32[]{:S(2)}, u32[]{:S(2)}) collective-permute-start(bf16[64,1536]{1,0:T(8,128)(2,1)} %get-tuple-element.373), channel_id=1, source_target_pairs={{0,11},{1,10},{2,9},{3,8},{4,15},{5,14},{6,13},{7,12},{8,3},{9,2},... | collective-permute-start | bytes 589832 | tf_op jit(solution)/shard_map/ppermute | solution.py:225
  415.1 30.4 %collective-permute-start.89 = (bf16[64,1536]{1,0:T(8,128)(2,1)}, bf16[64,1536]{1,0:T(8,128)(2,1)S(1)}, u32[]{:S(2)}, u32[]{:S(2)}) collective-permute-start(bf16[64,1536]{1,0:T(8,128)(2,1)} %get-tuple-element.392), channel_id=1, source_target_pairs={{0,15},{1,14},{2,13},{3,12},{4,11},{5,10},{6,9},{7,8},{8,7},{9,6},... | collective-permute-start | bytes 589832 | tf_op jit(solution)/shard_map/ppermute | solution.py:225
  467.3 32.1 %collective-permute-start.175 = (bf16[64,1536]{1,0:T(8,128)(2,1)}, bf16[64,1536]{1,0:T(8,128)(2,1)}, u32[]{:S(2)}, u32[]{:S(2)}) collective-permute-start(bf16[64,1536]{1,0:T(8,128)(2,1)} %get-tuple-element.482), channel_id=1, source_target_pairs={{0,14},{1,15},{2,12},{3,13},{4,10},{5,11},{6,8},{7,9},{8,6},{9,7},... | collective-permute-start | bytes 589832 | tf_op jit(solution)/shard_map/ppermute | solution.py:225
  471.7 30.2 %collective-permute-start.177 = (bf16[64,1536]{1,0:T(8,128)(2,1)}, bf16[64,1536]{1,0:T(8,128)(2,1)}, u32[]{:S(2)}, u32[]{:S(2)}) collective-permute-start(bf16[64,1536]{1,0:T(8,128)(2,1)} %get-tuple-element.484), channel_id=1, source_target_pairs={{0,11},{1,10},{2,9},{3,8},{4,15},{5,14},{6,13},{7,12},{8,3},{9,2},... | collective-permute-start | bytes 589832 | tf_op jit(solution)/shard_map/ppermute | solution.py:225
  503.0 33.1 %collective-permute-start.124 = (bf16[64,1536]{1,0:T(8,128)(2,1)}, bf16[64,1536]{1,0:T(8,128)(2,1)S(1)}, u32[]{:S(2)}, u32[]{:S(2)}) collective-permute-start(bf16[64,1536]{1,0:T(8,128)(2,1)} %get-tuple-element.428), channel_id=1, source_target_pairs={{0,9},{1,8},{2,11},{3,10},{4,13},{5,12},{6,15},{7,14},{8,1},{9,0},... | collective-permute-start | bytes 589832 | tf_op jit(solution)/shard_map/ppermute | solution.py:225
  604.5 33.4 %collective-permute-start.160 = (bf16[64,1536]{1,0:T(8,128)(2,1)}, bf16[64,1536]{1,0:T(8,128)(2,1)S(1)}, u32[]{:S(2)}, u32[]{:S(2)}) collective-permute-start(bf16[64,1536]{1,0:T(8,128)(2,1)} %get-tuple-element.466), channel_id=1, source_target_pairs={{0,14},{1,15},{2,12},{3,13},{4,10},{5,11},{6,8},{7,9},{8,6},{9,7},... | collective-permute-start | bytes 589832 | tf_op jit(solution)/shard_map/ppermute | solution.py:225
  610.6 30.5 %collective-permute-start.161 = (bf16[64,1536]{1,0:T(8,128)(2,1)}, bf16[64,1536]{1,0:T(8,128)(2,1)S(1)}, u32[]{:S(2)}, u32[]{:S(2)}) collective-permute-start(bf16[64,1536]{1,0:T(8,128)(2,1)} %get-tuple-element.467), channel_id=1, source_target_pairs={{0,3},{1,2},{2,1},{3,0},{4,7},{5,6},{6,5},{7,4},{8,11},{9,10},{10,... | collective-permute-start | bytes 589832 | tf_op jit(solution)/shard_map/ppermute | solution.py:225
  610.6 30.6 %collective-permute-start.162 = (bf16[64,1536]{1,0:T(8,128)(2,1)}, bf16[64,1536]{1,0:T(8,128)(2,1)S(1)}, u32[]{:S(2)}, u32[]{:S(2)}) collective-permute-start(bf16[64,1536]{1,0:T(8,128)(2,1)} %get-tuple-element.468), channel_id=1, source_target_pairs={{0,11},{1,10},{2,9},{3,8},{4,15},{5,14},{6,13},{7,12},{8,3},{9,2},... | collective-permute-start | bytes 589832 | tf_op jit(solution)/shard_map/ppermute | solution.py:225
  643.6 34.2 %collective-permute-start.104 = (bf16[64,1536]{1,0:T(8,128)(2,1)}, bf16[64,1536]{1,0:T(8,128)(2,1)S(1)}, u32[]{:S(2)}, u32[]{:S(2)}) collective-permute-start(bf16[64,1536]{1,0:T(8,128)(2,1)} %get-tuple-element.407), channel_id=1, source_target_pairs={{0,15},{1,14},{2,13},{3,12},{4,11},{5,10},{6,9},{7,8},{8,7},{9,6},... | collective-permute-start | bytes 589832 | tf_op jit(solution)/shard_map/ppermute | solution.py:225
  657.3 31.5 %collective-permute-start.91 = (bf16[64,1536]{1,0:T(8,128)(2,1)}, bf16[64,1536]{1,0:T(8,128)(2,1)S(1)}, u32[]{:S(2)}, u32[]{:S(2)}) collective-permute-start(bf16[64,1536]{1,0:T(8,128)(2,1)} %get-tuple-element.394), channel_id=1, source_target_pairs={{0,4},{1,5},{2,6},{3,7},{4,0},{5,1},{6,2},{7,3},{8,12},{9,13},{10,... | collective-permute-start | bytes 589832 | tf_op jit(solution)/shard_map/ppermute | solution.py:225
  688.8 30.2 %collective-permute-start.96 = (bf16[64,1536]{1,0:T(8,128)(2,1)}, bf16[64,1536]{1,0:T(8,128)(2,1)S(1)}, u32[]{:S(2)}, u32[]{:S(2)}) collective-permute-start(bf16[64,1536]{1,0:T(8,128)(2,1)} %get-tuple-element.399), channel_id=1, source_target_pairs={{0,13},{1,12},{2,15},{3,14},{4,9},{5,8},{6,11},{7,10},{8,5},{9,4},... | collective-permute-start | bytes 589832 | tf_op jit(solution)/shard_map/ppermute | solution.py:225
  720.3 32.6 %collective-permute-start.184 = (bf16[64,1536]{1,0:T(8,128)(2,1)}, bf16[64,1536]{1,0:T(8,128)(2,1)S(1)}, u32[]{:S(2)}, u32[]{:S(2)}) collective-permute-start(bf16[64,1536]{1,0:T(8,128)(2,1)} %get-tuple-element.497), channel_id=1, source_target_pairs={{0,9},{1,8},{2,11},{3,10},{4,13},{5,12},{6,15},{7,14},{8,1},{9,0},... | collective-permute-start | bytes 589832 | tf_op jit(solution)/shard_map/ppermute | solution.py:225
  824.5 31.5 %collective-permute-start.145 = (bf16[64,1536]{1,0:T(8,128)(2,1)}, bf16[64,1536]{1,0:T(8,128)(2,1)}, u32[]{:S(2)}, u32[]{:S(2)}) collective-permute-start(bf16[64,1536]{1,0:T(8,128)(2,1)} %get-tuple-element.450), channel_id=1, source_target_pairs={{0,14},{1,15},{2,12},{3,13},{4,10},{5,11},{6,8},{7,9},{8,6},{9,7},... | collective-permute-start | bytes 589832 | tf_op jit(solution)/shard_map/ppermute | solution.py:225
  828.0 30.4 %collective-permute-start.147 = (bf16[64,1536]{1,0:T(8,128)(2,1)}, bf16[64,1536]{1,0:T(8,128)(2,1)}, u32[]{:S(2)}, u32[]{:S(2)}) collective-permute-start(bf16[64,1536]{1,0:T(8,128)(2,1)} %get-tuple-element.452), channel_id=1, source_target_pairs={{0,11},{1,10},{2,9},{3,8},{4,15},{5,14},{6,13},{7,12},{8,3},{9,2},... | collective-permute-start | bytes 589832 | tf_op jit(solution)/shard_map/ppermute | solution.py:225
  859.6 30.9 %collective-permute-start.199 = (bf16[64,1536]{1,0:T(8,128)(2,1)}, bf16[64,1536]{1,0:T(8,128)(2,1)S(1)}, u32[]{:S(2)}, u32[]{:S(2)}) collective-permute-start(bf16[64,1536]{1,0:T(8,128)(2,1)} %get-tuple-element.514), channel_id=1, source_target_pairs={{0,9},{1,8},{2,11},{3,10},{4,13},{5,12},{6,15},{7,14},{8,1},{9,0},... | collective-permute-start | bytes 589832 | tf_op jit(solution)/shard_map/ppermute | solution.py:225
  874.4 33.2 %collective-permute-start.200 = (bf16[64,1536]{1,0:T(8,128)(2,1)S(1)}, bf16[64,1536]{1,0:T(8,128)(2,1)S(1)}, u32[]{:S(2)}, u32[]{:S(2)}) collective-permute-start(bf16[64,1536]{1,0:T(8,128)(2,1)S(1)} %copy-done.213), channel_id=1, source_target_pairs={{0,5},{1,4},{2,7},{3,6},{4,1},{5,0},{6,3},{7,2},{8,13},{9,12},{10,... | collective-permute-start | bytes 589832 | tf_op jit(solution)/shard_map/ppermute | solution.py:225
  875.2 32.5 %collective-permute-start.201 = (bf16[64,1536]{1,0:T(8,128)(2,1)S(1)}, bf16[64,1536]{1,0:T(8,128)(2,1)S(1)}, u32[]{:S(2)}, u32[]{:S(2)}) collective-permute-start(bf16[64,1536]{1,0:T(8,128)(2,1)S(1)} %copy-done.210), channel_id=1, source_target_pairs={{0,13},{1,12},{2,15},{3,14},{4,9},{5,8},{6,11},{7,10},{8,5},{9,4},... | collective-permute-start | bytes 589832 | tf_op jit(solution)/shard_map/ppermute | solution.py:225
  880.6 30.9 %collective-permute-start.203 = (bf16[64,1536]{1,0:T(8,128)(2,1)S(1)}, bf16[64,1536]{1,0:T(8,128)(2,1)S(1)}, u32[]{:S(2)}, u32[]{:S(2)}) collective-permute-start(bf16[64,1536]{1,0:T(8,128)(2,1)S(1)} %copy-done.205), channel_id=1, source_target_pairs={{0,10},{1,11},{2,8},{3,9},{4,14},{5,15},{6,12},{7,13},{8,2},{9,3},... | collective-permute-start | bytes 589832 | tf_op jit(solution)/shard_map/ppermute | solution.py:225
  912.5 34.9 %collective-permute-start.209 = (bf16[64,1536]{1,0:T(8,128)(2,1)S(1)}, bf16[64,1536]{1,0:T(8,128)(2,1)S(1)}, u32[]{:S(2)}, u32[]{:S(2)}) collective-permute-start(bf16[64,1536]{1,0:T(8,128)(2,1)S(1)} %copy-done.189), channel_id=1, source_target_pairs={{0,15},{1,14},{2,13},{3,12},{4,11},{5,10},{6,9},{7,8},{8,7},{9,6},... | collective-permute-start | bytes 589832 | tf_op jit(solution)/shard_map/ppermute | solution.py:225
  987.2 37.3 %collective-permute-start.119 = (bf16[64,1536]{1,0:T(8,128)(2,1)S(1)}, bf16[64,1536]{1,0:T(8,128)(2,1)S(1)}, u32[]{:S(2)}, u32[]{:S(2)}) collective-permute-start(bf16[64,1536]{1,0:T(8,128)(2,1)S(1)} %copy-done.188), channel_id=1, source_target_pairs={{0,15},{1,14},{2,13},{3,12},{4,11},{5,10},{6,9},{7,8},{8,7},{9,6},... | collective-permute-start | bytes 589832 | tf_op jit(solution)/shard_map/ppermute | solution.py:225
  1003.5 47.1 %collective-permute-start.225 = (bf16[64,1536]{1,0:T(8,128)(2,1)}, bf16[64,1536]{1,0:T(8,128)(2,1)S(1)}, u32[]{:S(2)}, u32[]{:S(2)}) collective-permute-start(bf16[64,1536]{1,0:T(8,128)(2,1)} %get-tuple-element.543), channel_id=1, source_target_pairs={{0,8},{1,9},{2,10},{3,11},{4,12},{5,13},{6,14},{7,15},{8,0},{9,1},... | collective-permute-start | bytes 589832 | tf_op jit(solution)/shard_map/ppermute | solution.py:225
  1004.4 46.4 %collective-permute-start.226 = (bf16[64,1536]{1,0:T(8,128)(2,1)}, bf16[64,1536]{1,0:T(8,128)(2,1)S(1)}, u32[]{:S(2)}, u32[]{:S(2)}) collective-permute-start(bf16[64,1536]{1,0:T(8,128)(2,1)} %get-tuple-element.544), channel_id=1, source_target_pairs={{0,4},{1,5},{2,6},{3,7},{4,0},{5,1},{6,2},{7,3},{8,12},{9,13},{10,... | collective-permute-start | bytes 589832 | tf_op jit(solution)/shard_map/ppermute | solution.py:225
  1012.0 38.9 %collective-permute-start.227 = (bf16[64,1536]{1,0:T(8,128)(2,1)}, bf16[64,1536]{1,0:T(8,128)(2,1)S(1)}, u32[]{:S(2)}, u32[]{:S(2)}) collective-permute-start(bf16[64,1536]{1,0:T(8,128)(2,1)} %get-tuple-element.545), channel_id=1, source_target_pairs={{0,12},{1,13},{2,14},{3,15},{4,8},{5,9},{6,10},{7,11},{8,4},{9,5},... | collective-permute-start | bytes 589832 | tf_op jit(solution)/shard_map/ppermute | solution.py:225
  1012.0 42.4 %collective-permute-start.228 = (bf16[64,1536]{1,0:T(8,128)(2,1)}, bf16[64,1536]{1,0:T(8,128)(2,1)S(1)}, u32[]{:S(2)}, u32[]{:S(2)}) collective-permute-start(bf16[64,1536]{1,0:T(8,128)(2,1)} %get-tuple-element.546), channel_id=1, source_target_pairs={{0,1},{1,0},{2,3},{3,2},{4,5},{5,4},{6,7},{7,6},{8,9},{9,8},{10,11... | collective-permute-start | bytes 589832 | tf_op jit(solution)/shard_map/ppermute | solution.py:225
  1024.5 32.0 %collective-permute-start.229 = (bf16[64,1536]{1,0:T(8,128)(2,1)}, bf16[64,1536]{1,0:T(8,128)(2,1)S(1)}, u32[]{:S(2)}, u32[]{:S(2)}) collective-permute-start(bf16[64,1536]{1,0:T(8,128)(2,1)} %get-tuple-element.547), channel_id=1, source_target_pairs={{0,9},{1,8},{2,11},{3,10},{4,13},{5,12},{6,15},{7,14},{8,1},{9,0},... | collective-permute-start | bytes 589832 | tf_op jit(solution)/shard_map/ppermute | solution.py:225
  1076.7 32.4 %collective-permute-start.239 = (bf16[64,1536]{1,0:T(8,128)(2,1)S(1)}, bf16[64,1536]{1,0:T(8,128)(2,1)S(1)}, u32[]{:S(2)}, u32[]{:S(2)}) collective-permute-start(bf16[64,1536]{1,0:T(8,128)(2,1)S(1)} %copy-done.185), channel_id=1, source_target_pairs={{0,15},{1,14},{2,13},{3,12},{4,11},{5,10},{6,9},{7,8},{8,7},{9,6},... | collective-permute-start | bytes 589832 | tf_op jit(solution)/shard_map/ppermute | solution.py:225
  1134.6 34.4 %collective-permute-start.220 = (bf16[64,1536]{1,0:T(8,128)(2,1)}, bf16[64,1536]{1,0:T(8,128)(2,1)}, u32[]{:S(2)}, u32[]{:S(2)}) collective-permute-start(bf16[64,1536]{1,0:T(8,128)(2,1)} %get-tuple-element.537), channel_id=1, source_target_pairs={{0,14},{1,15},{2,12},{3,13},{4,10},{5,11},{6,8},{7,9},{8,6},{9,7},... | collective-permute-start | bytes 589832 | tf_op jit(solution)/shard_map/ppermute | solution.py:225
  1138.8 31.8 %collective-permute-start.221 = (bf16[64,1536]{1,0:T(8,128)(2,1)}, bf16[64,1536]{1,0:T(8,128)(2,1)}, u32[]{:S(2)}, u32[]{:S(2)}) collective-permute-start(bf16[64,1536]{1,0:T(8,128)(2,1)} %get-tuple-element.538), channel_id=1, source_target_pairs={{0,3},{1,2},{2,1},{3,0},{4,7},{5,6},{6,5},{7,4},{8,11},{9,10},{10,... | collective-permute-start | bytes 589832 | tf_op jit(solution)/shard_map/ppermute | solution.py:225
  (425 other events, 16663.2 us)

commit v3 on v2

--- a/solution.py
+++ b/solution.py
@@ -30,14 +30,12 @@
         self.direct = (2 * own) % 16 == 0 and own >= 2
         self.pair = 2 if self.direct else own
         self.pairs = own // self.pair
-        self.slots = devices if self.direct else 1
-        quarter = max(devices // 4, 1)
-        near, far = list(range(devices // 2)), list(range(devices // 2, devices))
-        near = [hop for both in zip(near[:quarter], near[quarter:]) for hop in both]
-        far = [hop for both in zip(far[:quarter], far[quarter:]) for hop in both]
-        self.hops = [hop for both in zip(near, far) for hop in both]
         self.height = devices * own * own
-        self.slot_height = self.height // self.slots
+        self.near = devices // 2 if self.direct else devices
+        far = list(range(self.near, devices))
+        self.hops = [hop for both in zip(far[: len(far) // 2], far[len(far) // 2 :]) for hop in both]
+        self.heights = [self.near * own * own] + [own * own] * len(self.hops)
+        self.slots = len(self.heights)
         self.width = own * order
         self.chunks = CHUNKS
         self.chunk = rows // self.chunks
@@ -48,16 +46,18 @@
         return pl.BlockSpec((self.tile, self.width), lambda i: (chunk * self.steps + i, 0))
 
     def slot_specs(self):
-        return [pl.BlockSpec((self.slot_height, self.tile), lambda i: (0, i))] * self.slots
+        return [pl.BlockSpec((height, self.tile), lambda i: (0, i)) for height in self.heights]
 
     def slot_shapes(self):
-        return [jax.ShapeDtypeStruct((self.slot_height, self.chunk), jnp.bfloat16)] * self.slots
-
-    def pair_rows(self, refs, pair):
-        if self.pairs == 1 and self.slots == 1:
-            return refs[0][...]
-        size = self.pair * self.own
-        return jnp.concatenate([ref[pair * size : (pair + 1) * size, :] for ref in refs], axis=0)
+        return [jax.ShapeDtypeStruct((height, self.chunk), jnp.bfloat16) for height in self.heights]
+
+    def pieces(self, refs, pair):
+        size, step = self.pair * self.own, self.own * self.own
+        for device in range(self.near):
+            start = device * step + pair * size
+            yield refs[0], slice(start, start + size)
+        for ref in refs[1:]:
+            yield ref, slice(pair * size, (pair + 1) * size)
 
 
 def whole(array):
@@ -83,8 +83,10 @@
 def first_factor(plan, chunk, tokens, wide_left, after):
     def body(tokens_ref, left_ref, *refs):
         product = dot(left_ref[...], tokens_ref[...], NT).astype(jnp.bfloat16)
-        for slot, ref in enumerate(refs[len(after) :]):
-            ref[...] = product[slot * plan.slot_height : (slot + 1) * plan.slot_height, :]
+        start = 0
+        for ref in refs[len(after) :]:
+            ref[...] = product[start : start + ref.shape[0], :]
+            start += ref.shape[0]
 
     return call(
         body,
@@ -118,7 +120,9 @@
         for pair in range(plan.pairs):
             columns = slice(pair * span, (pair + 1) * span)
             kept = dot(mask, spread_ref[:, columns], TN) * jnp.float32(1.0 / keep_rate)
-            rows = plan.pair_rows(got, pair)
+            rows = got[0][...]
+            if plan.direct:
+                rows = jnp.concatenate([ref[piece, :] for ref, piece in plan.pieces(got, pair)], axis=0)
             mixing = dot(rows, right_ref[pair], TN)
             cdf = 0.5 * (1.0 + lax.erf(mixing * jnp.float32(1.0 / math.sqrt(2.0))))
             pdf = jnp.exp(-0.5 * mixing * mixing) * jnp.float32(1.0 / math.sqrt(2.0 * math.pi))
@@ -129,12 +133,12 @@
             )
             total_ref[pair] += dot(rows, grad_mix, NN)
             back = dot(right_ref[pair], grad_mix, NT).astype(jnp.bfloat16)
-            if plan.pairs == 1 and slots == 1:
+            if plan.direct:
+                size = plan.pair * plan.own
+                for device, (ref, piece) in enumerate(plan.pieces(sent, pair)):
+                    ref[piece, :] = back[device * size : (device + 1) * size, :]
+            else:
                 sent[0][...] = back
-            else:
-                size = plan.pair * plan.own
-                for slot, ref in enumerate(sent):
-                    ref[pair * size : (pair + 1) * size, :] = back[slot * size : (slot + 1) * size, :]
 
     ins = (*received, tokens, cotangent, keep_mask, spread, wide_right)
     in_specs = [
@@ -163,20 +167,36 @@
     return result[:slots], (result[slots], result[slots + 1])
 
 
-def first_factor_back(plan, chunk, received, tokens, cotangent, wide_left, state):
-    slots, own, order = plan.slots, plan.own, plan.order
+def tokens_back(plan, chunk, received, cotangent, wide_left, grad_tokens):
+    slots = plan.slots
 
     def body(*refs):
-        got = refs[:slots]
-        tokens_ref, cotangent_ref, left_ref = refs[slots : slots + 3]
-        grad_ref, total_ref, scratch_ref = refs[-3:]
-        step = pl.program_id(0)
-
-        rows = got[0][...] if slots == 1 else jnp.concatenate([ref[...] for ref in got], axis=0)
+        got, (cotangent_ref, left_ref), grad_ref = refs[:slots], refs[slots : slots + 2], refs[-1]
+        rows = jnp.concatenate([ref[...] for ref in got], axis=0) if slots > 1 else got[0][...]
         grad = dot(rows, left_ref[...], TN)
         grad_ref[...] = (cotangent_ref[...].astype(jnp.float32) + grad).astype(jnp.bfloat16)
+
+    ins = (*received, cotangent, wide_left)
+    in_specs = [*plan.slot_specs(), plan.token_spec(chunk), whole(wide_left)]
+    aliases = {}
+    if grad_tokens is not None:
+        aliases = {len(ins): 0}
+        ins = (*ins, grad_tokens)
+        in_specs.append(ANY)
+    outs = [jax.ShapeDtypeStruct(cotangent.shape, jnp.bfloat16)]
+    flops = 2 * plan.height * plan.width * plan.chunk
+    return call(body, plan, ins, in_specs, outs, [plan.token_spec(chunk)], aliases, flops)[0]
+
+
+def left_back(plan, chunk, received, tokens, total):
+    slots, own, order = plan.slots, plan.own, plan.order
+
+    def body(*refs):
+        got, tokens_ref = refs[:slots], refs[slots]
+        total_ref, scratch_ref = refs[-2:]
+        step = pl.program_id(0)
+        rows = jnp.concatenate([ref[...] for ref in got], axis=0) if slots > 1 else got[0][...]
         product = dot(rows, tokens_ref[...], NN)
-
         for block in range(own):
             part = product[:, block * order : (block + 1) * order]
 
@@ -192,41 +212,28 @@
         def _():
             for block in range(own):
                 part = scratch_ref[block, pl.ds(block, order, stride=own), :]
-                total_ref[block] = part if chunk == 0 else part + refs[slots + 4][block]
-
-    ins = (*received, tokens, cotangent, wide_left)
-    in_specs = [*plan.slot_specs(), plan.token_spec(chunk), plan.token_spec(chunk), whole(wide_left)]
-    aliases = {}
-    if state is not None:
-        aliases = {len(ins): 0, len(ins) + 1: 1}
-        ins = (*ins, *state)
-        in_specs += [ANY, whole(state[1])]
-    outs = [
-        jax.ShapeDtypeStruct(tokens.shape, jnp.bfloat16),
-        jax.ShapeDtypeStruct((own, order, order), jnp.float32),
+                total_ref[block] = part if total is None else part + refs[slots + 1][block]
+
+    ins = (*received, tokens)
+    in_specs = [*plan.slot_specs(), plan.token_spec(chunk)]
+    if total is not None:
+        ins = (*ins, total)
+        in_specs.append(whole(total))
+    outs = [jax.ShapeDtypeStruct((own, order, order), jnp.float32)]
+    scratch = [pltpu.VMEM((own, plan.height, order), jnp.float32)]
+    flops = 2 * plan.height * plan.width * plan.chunk
+    return call(body, plan, ins, in_specs, outs, [whole(outs[0])], {}, flops, scratch)[0]
+
+
+def exchange(plan, parts):
+    devices, near = plan.devices, plan.near
+    far = [
+        lax.ppermute(part, "blk", [(i, i ^ hop) for i in range(devices)]) for hop, part in zip(plan.hops, parts[1:])
     ]
-    out_specs = [plan.token_spec(chunk), whole(outs[1])]
-    return call(
-        body,
-        plan,
-        ins,
-        in_specs,
-        outs,
-        out_specs,
-        aliases,
-        4 * plan.height * plan.width * plan.chunk,
-        [pltpu.VMEM((own, plan.height, order), jnp.float32)],
-    )
-
-
-def exchange(plan, parts):
-    if plan.direct:
-        return [
-            part if hop == 0 else lax.ppermute(part, "blk", [(i, i ^ hop) for i in range(plan.devices)])
-            for hop, part in zip(plan.hops, parts)
-        ]
-    split = parts[0].reshape(plan.devices, plan.own * plan.own, plan.chunk)
-    return [lax.all_to_all(split, "blk", 0, 0, tiled=True).reshape(plan.height, plan.chunk)]
+    groups = [list(range(start, start + near)) for start in range(0, devices, near)]
+    split = parts[0].reshape(near, plan.own * plan.own, plan.chunk)
+    got = lax.all_to_all(split, "blk", 0, 0, axis_index_groups=groups, tiled=True)
+    return [got.reshape(parts[0].shape), *far]
 
 
 def sum_over_dp(value):
@@ -243,8 +250,13 @@
     pair, pairs, span = plan.pair, plan.pairs, plan.pair * order
     partner = place = lax.iota(jnp.int32, devices)
     if plan.direct:
-        place = jnp.take(jnp.array(np.argsort(plan.hops), jnp.int32), place ^ lax.axis_index("blk"))
-        partner = jnp.array(plan.hops, jnp.int32) ^ lax.axis_index("blk")
+        me, near = lax.axis_index("blk"), plan.near
+        hops = place ^ me
+        far_place = near + jnp.array(np.argsort(plan.hops), jnp.int32)
+        place = jnp.where(hops < near, place % near, jnp.take(far_place, hops % near))
+        partner = jnp.concatenate(
+            [me // near * near + lax.iota(jnp.int32, near), jnp.array(plan.hops, jnp.int32) ^ me]
+        )
     factor = 1.0 / math.sqrt(rows * lax.axis_size("dp"))
 
     selector = (channel_order[:, None] == lax.broadcasted_iota(jnp.int32, (order, order), 1)).astype(jnp.bfloat16)
@@ -264,11 +276,11 @@
     forward, backward, state = [], [], None
     for step in range(plan.chunks + SECOND_LAG):
         if step < plan.chunks:
-            after = backward[step - FIRST_LAG][1:] if step >= FIRST_LAG else []
+            after = backward[step - FIRST_LAG] if step >= FIRST_LAG else []
             forward.append(exchange(plan, first_factor(plan, step, tokens, wide_left, after)))
         chunk = step - SECOND_LAG
         if chunk >= 0:
-            after = backward[chunk - SECOND_LAG][1:] if chunk >= SECOND_LAG else []
+            after = backward[chunk - SECOND_LAG] if chunk >= SECOND_LAG else []
             sent, state = second_factor(
                 plan, chunk, forward[chunk], tokens, cotangent, keep_mask, spread, wide_right, state, after
             )
@@ -280,10 +292,10 @@
     part_right = jnp.take(part_right.reshape(own, devices, own, order), place, axis=1).reshape(own, order, order)
     grad_right = sum_over_dp(part_right.astype(jnp.bfloat16)) * factor
 
-    state = None
+    grad_tokens = part_left = None
     for chunk in range(plan.chunks):
-        state = first_factor_back(plan, chunk, backward[chunk], tokens, cotangent, wide_left, state)
-    grad_tokens, part_left = state
+        part_left = left_back(plan, chunk, backward[chunk], tokens, part_left)
+        grad_tokens = tokens_back(plan, chunk, backward[chunk], cotangent, wide_left, grad_tokens)
     part_left = jnp.take(part_left.astype(jnp.bfloat16).reshape(own, devices, own, order), place, axis=1)
     part_left = jnp.einsum(
         "km,bom->bko", selector, part_left.reshape(own, order, order), preferred_element_type=jnp.float32

time: 1210 us -> 1510 us (1.25)
  waiting for transfers between devices: 534 us -> 816 us
  starting transfers between devices: 378 us -> 328 us
  Pallas kernels: 257 us -> 285 us
  blocking collectives: 0 us -> 24.6 us
  local copies, waits for them, and re-layouts: 14.4 us -> 37.8 us
    ppermute x240 -> x128, waiting for transfers between devices: 528 us -> 751 us  [exchange(): lax.ppermute(part, 'blk', [(i, i ^ hop) for i in range(devices)])]
    ppermute x240 -> x128, starting transfers between devices: 375 us -> 269 us  [exchange(): lax.ppermute(part, 'blk', [(i, i ^ hop) for i in range(devices)])]
    all_to_all x0 -> x15, waiting for transfers between devices: none -> 65.6 us  [exchange(): lax.all_to_all(split, 'blk', 0, 0, axis_index_groups=groups, tiled=True)]
    all_to_all x0 -> x15, starting transfers between devices: none -> 55.1 us  [exchange(): lax.all_to_all(split, 'blk', 0, 0, axis_index_groups=groups, tiled=True)]
    pallas_call x24 -> x32, Pallas kernels: 257 us -> 285 us  [call(): pl.pallas_call(body, out_shape=outs, grid=(plan.steps,), in_specs=in_spec...]
    all_to_all x0 -> x1, blocking collectives: none -> 24.6 us  [exchange(): lax.all_to_all(split, 'blk', 0, 0, axis_index_groups=groups, tiled=True)]
    unnamed x433 -> x375, local copies, waits for them, and re-layouts: 7.08 us -> 31.1 us
  transfers between devices with their start and end apart: 242 -> 145, of which waited for: 81 -> 98; matrix products, arithmetic and copies ran while one was open for 1% -> 1% of each run, Pallas kernels for 21% -> 17%
where the time goes in v3:
time: 1510 us; the launch traced here: 1500 us
  waiting for transfers between devices  816 us (54%)
  starting transfers between devices  328 us (22%)
  Pallas kernels  285 us (19%)
  local copies, waits for them, and re-layouts  37.8 us (3%)
  blocking collectives  24.6 us (2%)
    ppermute x128, waiting for transfers between devices, exchange(): lax.ppermute(part, 'blk', [(i, i ^ hop) for i in range(devices)])  751 us
    pallas_call x32, Pallas kernels, call(): pl.pallas_call(body, out_shape=outs, grid=(plan.steps,), in_specs=in_spec...  285 us
    ppermute x128, starting transfers between devices, exchange(): lax.ppermute(part, 'blk', [(i, i ^ hop) for i in range(devices)])  269 us
    all_to_all x15, waiting for transfers between devices, exchange(): lax.all_to_all(split, 'blk', 0, 0, axis_index_groups=groups, tiled=True)  65.6 us
    all_to_all x15, starting transfers between devices, exchange(): lax.all_to_all(split, 'blk', 0, 0, axis_index_groups=groups, tiled=True)  55.1 us
    unnamed x375, local copies, waits for them, and re-layouts  31.1 us
  transfers between devices with their start and end apart: 145, of which 98 were waited for; matrix products, arithmetic and copies ran while one was open for 1% of the time, Pallas kernels for 17%

profile of v3, /device:TPU:16, one launch (start us, length us, event | category | flops | bytes accessed | tf_op | source)
XLA Modules:
  0.0 1501.5 jit_solution(17887652145979424378)
XLA Ops:
  24.0 13.2 all-to-all-done.3
  48.8 13.1 all-to-all-done.2
  73.6 13.1 all-to-all-done.1
  101.2 13.5 collective-permute-done.24.refs_1_
  127.2 18.4 %collective-permute-done.27.refs_4_ = bf16[64,1536]{1,0:T(8,128)(2,1)S(1)} collective-permute-done((bf16[64,1536]{1,0:T(8,128)(2,1)}, bf16[64,1536]{1,0:T(8,128)(2,1)S(1)}, u32[]{:S(2)}, u32[]{:S(2)}) %collective-permute-start.27) | collective-permute-done | bytes 196640 | tf_op jit(solution)/shard_map/ppermute | solution.py:231
  189.1 14.4 collective-permute-done.16.refs_1_
  216.1 19.0 %collective-permute-done.19.refs_4_ = bf16[64,1536]{1,0:T(8,128)(2,1)S(1)} collective-permute-done((bf16[64,1536]{1,0:T(8,128)(2,1)}, bf16[64,1536]{1,0:T(8,128)(2,1)S(1)}, u32[]{:S(2)}, u32[]{:S(2)}) %collective-permute-start.19) | collective-permute-done | bytes 196640 | tf_op jit(solution)/shard_map/ppermute | solution.py:231
  253.6 12.4 shard_map.116
  278.6 14.6 collective-permute-done.8.refs_1_
  305.8 19.1 %collective-permute-done.11.refs_4_ = bf16[64,1536]{1,0:T(8,128)(2,1)S(1)} collective-permute-done((bf16[64,1536]{1,0:T(8,128)(2,1)}, bf16[64,1536]{1,0:T(8,128)(2,1)S(1)}, u32[]{:S(2)}, u32[]{:S(2)}) %collective-permute-start.11) | collective-permute-done | bytes 196640 | tf_op jit(solution)/shard_map/ppermute | solution.py:231
  401.9 14.0 collective-permute-done.5.refs_6_
  417.0 14.1 collective-permute-done.7.refs_8_
  435.2 13.5 collective-permute-done.41.refs_18_.refs_2_
  495.6 13.0 collective-permute-done.37.refs_22_.refs_6_
  524.5 12.3 shard_map.117
  546.1 12.3 shard_map.118
  558.5 24.6 %all_to_all.80 = bf16[8,64,1536]{2,1,0:T(8,128)(2,1)} all-to-all(bf16[8,64,1536]{2,1,0:T(8,128)(2,1)} %bitcast.151), channel_id=1, replica_groups={{0,1,2,3,4,5,6,7},{8,9,10,11,12,13,14,15},{16,17,18,19,20,21,22,23},{24..., dimensions={0} | all-to-all | bytes 3145728 | tf_op jit(solution)/shard_map/all_to_all | solution.py:235
  594.2 13.0 all-to-all-done.8
  618.9 13.1 all-to-all-done.11
  644.7 14.3 collective-permute-done.64.refs_1_.refs_17_
  671.8 18.9 %collective-permute-done.67.refs_4_.refs_20_ = bf16[64,1536]{1,0:T(8,128)(2,1)S(1)} collective-permute-done((bf16[64,1536]{1,0:T(8,128)(2,1)}, bf16[64,1536]{1,0:T(8,128)(2,1)S(1)}, u32[]{:S(2)}, u32[]{:S(2)}) %collective-permute-start.67) | collective-permute-done | bytes 196640 | tf_op jit(solution)/shard_map/ppermute | solution.py:231
  728.6 14.6 collective-permute-done.48.refs_1_.refs_17_
  755.8 19.1 %collective-permute-done.51.refs_4_.refs_20_ = bf16[64,1536]{1,0:T(8,128)(2,1)S(1)} collective-permute-done((bf16[64,1536]{1,0:T(8,128)(2,1)}, bf16[64,1536]{1,0:T(8,128)(2,1)S(1)}, u32[]{:S(2)}, u32[]{:S(2)}) %collective-permute-start.51) | collective-permute-done | bytes 196640 | tf_op jit(solution)/shard_map/ppermute | solution.py:231
  812.9 14.6 collective-permute-done.88.refs_1_
  840.0 18.9 %collective-permute-done.91.refs_4_ = bf16[64,1536]{1,0:T(8,128)(2,1)S(1)} collective-permute-done((bf16[64,1536]{1,0:T(8,128)(2,1)}, bf16[64,1536]{1,0:T(8,128)(2,1)S(1)}, u32[]{:S(2)}, u32[]{:S(2)}) %collective-permute-start.91) | collective-permute-done | bytes 196640 | tf_op jit(solution)/shard_map/ppermute | solution.py:231
  902.8 14.4 collective-permute-done.80.refs_1_
  929.8 19.0 %collective-permute-done.83.refs_4_ = bf16[64,1536]{1,0:T(8,128)(2,1)S(1)} collective-permute-done((bf16[64,1536]{1,0:T(8,128)(2,1)}, bf16[64,1536]{1,0:T(8,128)(2,1)S(1)}, u32[]{:S(2)}, u32[]{:S(2)}) %collective-permute-start.83) | collective-permute-done | bytes 196640 | tf_op jit(solution)/shard_map/ppermute | solution.py:231
  967.2 12.3 shard_map.124
  993.1 13.7 collective-permute-done.72.refs_1_
  1019.5 19.1 %collective-permute-done.75.refs_4_ = bf16[64,1536]{1,0:T(8,128)(2,1)S(1)} collective-permute-done((bf16[64,1536]{1,0:T(8,128)(2,1)S(1)}, bf16[64,1536]{1,0:T(8,128)(2,1)S(1)}, u32[]{:S(2)}, u32[]{:S(2)}) %collective-permute-start.75) | collective-permute-done | bytes 196640 | tf_op jit(solution)/shard_map/ppermute | solution.py:231
  1306.4 12.3 shard_map.126
  1381.3 15.9 %collective-permute-start.112 = (bf16[64,1536]{1,0:T(8,128)(2,1)}, bf16[64,1536]{1,0:T(8,128)(2,1)}, u32[]{:S(2)}, u32[]{:S(2)}) collective-permute-start(bf16[64,1536]{1,0:T(8,128)(2,1)} %get-tuple-element.307), channel_id=1, source_target_pairs={{0,8},{1,9},{2,10},{3,11},{4,12},{5,13},{6,14},{7,15},{8,0},{9,1},... | collective-permute-start | bytes 589832 | tf_op jit(solution)/shard_map/ppermute | solution.py:231
  (709 shorter events, 1010.6 us)
Async XLA Ops:
  87.9 88.2 %all-to-all-start = ((bf16[8,64,1536]{2,1,0:T(8,128)(2,1)}), bf16[8,64,1536]{2,1,0:T(8,128)(2,1)S(1)}, u32[]{:S(2)}, u32[]{:S(2)}) async-start(bf16[8,64,1536]{2,1,0:T(8,128)(2,1)} %bitcast.141), calls=%async_computation | async-start | bytes 3145728 | tf_op jit(solution)/shard_map/all_to_all | solution.py:235
  95.3 50.4 %collective-permute-start.27 = (bf16[64,1536]{1,0:T(8,128)(2,1)}, bf16[64,1536]{1,0:T(8,128)(2,1)S(1)}, u32[]{:S(2)}, u32[]{:S(2)}) collective-permute-start(bf16[64,1536]{1,0:T(8,128)(2,1)} %get-tuple-element.196), channel_id=1, source_target_pairs={{0,13},{1,12},{2,15},{3,14},{4,9},{5,8},{6,11},{7,10},{8,5},{9,4},... | collective-permute-start | bytes 589832 | tf_op jit(solution)/shard_map/ppermute | solution.py:231
  97.1 51.0 %collective-permute-start.28 = (bf16[64,1536]{1,0:T(8,128)(2,1)}, bf16[64,1536]{1,0:T(8,128)(2,1)S(1)}, u32[]{:S(2)}, u32[]{:S(2)}) collective-permute-start(bf16[64,1536]{1,0:T(8,128)(2,1)} %get-tuple-element.197), channel_id=1, source_target_pairs={{0,10},{1,11},{2,8},{3,9},{4,14},{5,15},{6,12},{7,13},{8,2},{9,3},... | collective-permute-start | bytes 589832 | tf_op jit(solution)/shard_map/ppermute | solution.py:231
  177.2 88.8 %all-to-all-start.4 = ((bf16[8,64,1536]{2,1,0:T(8,128)(2,1)}), bf16[8,64,1536]{2,1,0:T(8,128)(2,1)S(1)}, u32[]{:S(2)}, u32[]{:S(2)}) async-start(bf16[8,64,1536]{2,1,0:T(8,128)(2,1)} %bitcast.143), calls=%async_computation.4 | async-start | bytes 3145728 | tf_op jit(solution)/shard_map/all_to_all | solution.py:235
  186.7 50.4 %collective-permute-start.20 = (bf16[64,1536]{1,0:T(8,128)(2,1)S(1)}, bf16[64,1536]{1,0:T(8,128)(2,1)S(1)}, u32[]{:S(2)}, u32[]{:S(2)}) collective-permute-start(bf16[64,1536]{1,0:T(8,128)(2,1)S(1)} %copy-done.172), channel_id=1, source_target_pairs={{0,10},{1,11},{2,8},{3,9},{4,14},{5,15},{6,12},{7,13},{8,2},{9,3},... | collective-permute-start | bytes 589832 | tf_op jit(solution)/shard_map/ppermute | solution.py:231
  267.1 277.9 %all-to-all-start.5 = ((bf16[8,64,1536]{2,1,0:T(8,128)(2,1)}), bf16[8,64,1536]{2,1,0:T(8,128)(2,1)S(1)}, u32[]{:S(2)}, u32[]{:S(2)}) async-start(bf16[8,64,1536]{2,1,0:T(8,128)(2,1)} %bitcast.137), calls=%async_computation.5 | async-start | bytes 3145728 | tf_op jit(solution)/shard_map/all_to_all | solution.py:235
  274.5 50.4 %collective-permute-start.11 = (bf16[64,1536]{1,0:T(8,128)(2,1)}, bf16[64,1536]{1,0:T(8,128)(2,1)S(1)}, u32[]{:S(2)}, u32[]{:S(2)}) collective-permute-start(bf16[64,1536]{1,0:T(8,128)(2,1)} %get-tuple-element.178), channel_id=1, source_target_pairs={{0,13},{1,12},{2,15},{3,14},{4,9},{5,8},{6,11},{7,10},{8,5},{9,4},... | collective-permute-start | bytes 589832 | tf_op jit(solution)/shard_map/ppermute | solution.py:231
  276.3 54.9 %collective-permute-start.12 = (bf16[64,1536]{1,0:T(8,128)(2,1)}, bf16[64,1536]{1,0:T(8,128)(2,1)S(1)}, u32[]{:S(2)}, u32[]{:S(2)}) collective-permute-start(bf16[64,1536]{1,0:T(8,128)(2,1)} %get-tuple-element.179), channel_id=1, source_target_pairs={{0,10},{1,11},{2,8},{3,9},{4,14},{5,15},{6,12},{7,13},{8,2},{9,3},... | collective-permute-start | bytes 589832 | tf_op jit(solution)/shard_map/ppermute | solution.py:231
  297.9 50.3 %collective-permute-start.14 = (bf16[64,1536]{1,0:T(8,128)(2,1)}, bf16[64,1536]{1,0:T(8,128)(2,1)S(1)}, u32[]{:S(2)}, u32[]{:S(2)}) collective-permute-start(bf16[64,1536]{1,0:T(8,128)(2,1)} %get-tuple-element.181), channel_id=1, source_target_pairs={{0,11},{1,10},{2,9},{3,8},{4,15},{5,14},{6,13},{7,12},{8,3},{9,2},... | collective-permute-start | bytes 589832 | tf_op jit(solution)/shard_map/ppermute | solution.py:231
  301.7 53.5 %collective-permute-start.15 = (bf16[64,1536]{1,0:T(8,128)(2,1)}, bf16[64,1536]{1,0:T(8,128)(2,1)S(1)}, u32[]{:S(2)}, u32[]{:S(2)}) collective-permute-start(bf16[64,1536]{1,0:T(8,128)(2,1)} %get-tuple-element.182), channel_id=1, source_target_pairs={{0,15},{1,14},{2,13},{3,12},{4,11},{5,10},{6,9},{7,8},{8,7},{9,6},... | collective-permute-start | bytes 589832 | tf_op jit(solution)/shard_map/ppermute | solution.py:231
  365.0 50.9 %collective-permute-start.5 = (bf16[64,1536]{1,0:T(8,128)(2,1)}, bf16[64,1536]{1,0:T(8,128)(2,1)S(1)}, u32[]{:S(2)}, u32[]{:S(2)}) collective-permute-start(bf16[64,1536]{1,0:T(8,128)(2,1)} %get-tuple-element.171), channel_id=1, source_target_pairs={{0,14},{1,15},{2,12},{3,13},{4,10},{5,11},{6,8},{7,9},{8,6},{9,7},... | collective-permute-start | bytes 589832 | tf_op jit(solution)/shard_map/ppermute | solution.py:231
  453.5 55.1 %collective-permute-start.37 = (bf16[64,1536]{1,0:T(8,128)(2,1)}, bf16[64,1536]{1,0:T(8,128)(2,1)S(1)}, u32[]{:S(2)}, u32[]{:S(2)}) collective-permute-start(bf16[64,1536]{1,0:T(8,128)(2,1)} %get-tuple-element.211), channel_id=1, source_target_pairs={{0,14},{1,15},{2,12},{3,13},{4,10},{5,11},{6,8},{7,9},{8,6},{9,7},... | collective-permute-start | bytes 589832 | tf_op jit(solution)/shard_map/ppermute | solution.py:231
  472.4 51.4 %collective-permute-start.39 = (bf16[64,1536]{1,0:T(8,128)(2,1)}, bf16[64,1536]{1,0:T(8,128)(2,1)S(1)}, u32[]{:S(2)}, u32[]{:S(2)}) collective-permute-start(bf16[64,1536]{1,0:T(8,128)(2,1)} %get-tuple-element.213), channel_id=1, source_target_pairs={{0,15},{1,14},{2,13},{3,12},{4,11},{5,10},{6,9},{7,8},{8,7},{9,6},... | collective-permute-start | bytes 589832 | tf_op jit(solution)/shard_map/ppermute | solution.py:231
  481.0 55.9 %collective-permute-start.43 = (bf16[64,1536]{1,0:T(8,128)(2,1)}, bf16[64,1536]{1,0:T(8,128)(2,1)S(1)}, u32[]{:S(2)}, u32[]{:S(2)}) collective-permute-start(bf16[64,1536]{1,0:T(8,128)(2,1)} %get-tuple-element.220), channel_id=1, source_target_pairs={{0,13},{1,12},{2,15},{3,14},{4,9},{5,8},{6,11},{7,10},{8,5},{9,4},... | collective-permute-start | bytes 589832 | tf_op jit(solution)/shard_map/ppermute | solution.py:231
  633.2 82.8 %all-to-all-start.10 = ((bf16[8,64,1536]{2,1,0:T(8,128)(2,1)}), bf16[8,64,1536]{2,1,0:T(8,128)(2,1)S(1)}, u32[]{:S(2)}, u32[]{:S(2)}) async-start(bf16[8,64,1536]{2,1,0:T(8,128)(2,1)} %bitcast.145), calls=%async_computation.10 | async-start | bytes 3145728 | tf_op jit(solution)/shard_map/all_to_all | solution.py:235
  640.6 50.1 %collective-permute-start.67 = (bf16[64,1536]{1,0:T(8,128)(2,1)}, bf16[64,1536]{1,0:T(8,128)(2,1)S(1)}, u32[]{:S(2)}, u32[]{:S(2)}) collective-permute-start(bf16[64,1536]{1,0:T(8,128)(2,1)} %get-tuple-element.247), channel_id=1, source_target_pairs={{0,13},{1,12},{2,15},{3,14},{4,9},{5,8},{6,11},{7,10},{8,5},{9,4},... | collective-permute-start | bytes 589832 | tf_op jit(solution)/shard_map/ppermute | solution.py:231
  642.4 50.3 %collective-permute-start.68 = (bf16[64,1536]{1,0:T(8,128)(2,1)S(1)}, bf16[64,1536]{1,0:T(8,128)(2,1)S(1)}, u32[]{:S(2)}, u32[]{:S(2)}) collective-permute-start(bf16[64,1536]{1,0:T(8,128)(2,1)S(1)} %copy-done.179), channel_id=1, source_target_pairs={{0,10},{1,11},{2,8},{3,9},{4,14},{5,15},{6,12},{7,13},{8,2},{9,3},... | collective-permute-start | bytes 589832 | tf_op jit(solution)/shard_map/ppermute | solution.py:231
  717.2 83.1 %all-to-all-start.9 = ((bf16[8,64,1536]{2,1,0:T(8,128)(2,1)}), bf16[8,64,1536]{2,1,0:T(8,128)(2,1)S(1)}, u32[]{:S(2)}, u32[]{:S(2)}) async-start(bf16[8,64,1536]{2,1,0:T(8,128)(2,1)} %bitcast.146), calls=%async_computation.9 | async-start | bytes 3145728 | tf_op jit(solution)/shard_map/all_to_all | solution.py:235
  724.5 50.4 %collective-permute-start.51 = (bf16[64,1536]{1,0:T(8,128)(2,1)}, bf16[64,1536]{1,0:T(8,128)(2,1)S(1)}, u32[]{:S(2)}, u32[]{:S(2)}) collective-permute-start(bf16[64,1536]{1,0:T(8,128)(2,1)} %get-tuple-element.229), channel_id=1, source_target_pairs={{0,13},{1,12},{2,15},{3,14},{4,9},{5,8},{6,11},{7,10},{8,5},{9,4},... | collective-permute-start | bytes 589832 | tf_op jit(solution)/shard_map/ppermute | solution.py:231
  726.4 50.7 %collective-permute-start.52 = (bf16[64,1536]{1,0:T(8,128)(2,1)}, bf16[64,1536]{1,0:T(8,128)(2,1)S(1)}, u32[]{:S(2)}, u32[]{:S(2)}) collective-permute-start(bf16[64,1536]{1,0:T(8,128)(2,1)} %get-tuple-element.230), channel_id=1, source_target_pairs={{0,10},{1,11},{2,8},{3,9},{4,14},{5,15},{6,12},{7,13},{8,2},{9,3},... | collective-permute-start | bytes 589832 | tf_op jit(solution)/shard_map/ppermute | solution.py:231
  801.4 88.4 %all-to-all-start.7 = ((bf16[8,64,1536]{2,1,0:T(8,128)(2,1)}), bf16[8,64,1536]{2,1,0:T(8,128)(2,1)S(1)}, u32[]{:S(2)}, u32[]{:S(2)}) async-start(bf16[8,64,1536]{2,1,0:T(8,128)(2,1)} %bitcast.144), calls=%async_computation.7 | async-start | bytes 3145728 | tf_op jit(solution)/shard_map/all_to_all | solution.py:235
  810.6 50.4 %collective-permute-start.92 = (bf16[64,1536]{1,0:T(8,128)(2,1)S(1)}, bf16[64,1536]{1,0:T(8,128)(2,1)S(1)}, u32[]{:S(2)}, u32[]{:S(2)}) collective-permute-start(bf16[64,1536]{1,0:T(8,128)(2,1)S(1)} %copy-done.165), channel_id=1, source_target_pairs={{0,10},{1,11},{2,8},{3,9},{4,14},{5,15},{6,12},{7,13},{8,2},{9,3},... | collective-permute-start | bytes 589832 | tf_op jit(solution)/shard_map/ppermute | solution.py:231
  891.0 88.6 %all-to-all-start.12 = ((bf16[8,64,1536]{2,1,0:T(8,128)(2,1)}), bf16[8,64,1536]{2,1,0:T(8,128)(2,1)S(1)}, u32[]{:S(2)}, u32[]{:S(2)}) async-start(bf16[8,64,1536]{2,1,0:T(8,128)(2,1)} %bitcast.142), calls=%async_computation.12 | async-start | bytes 3145728 | tf_op jit(solution)/shard_map/all_to_all | solution.py:235
  900.4 50.4 %collective-permute-start.84 = (bf16[64,1536]{1,0:T(8,128)(2,1)S(1)}, bf16[64,1536]{1,0:T(8,128)(2,1)S(1)}, u32[]{:S(2)}, u32[]{:S(2)}) collective-permute-start(bf16[64,1536]{1,0:T(8,128)(2,1)S(1)} %copy-done.157), channel_id=1, source_target_pairs={{0,10},{1,11},{2,8},{3,9},{4,14},{5,15},{6,12},{7,13},{8,2},{9,3},... | collective-permute-start | bytes 589832 | tf_op jit(solution)/shard_map/ppermute | solution.py:231
  980.8 156.0 %all-to-all-start.13 = ((bf16[8,64,1536]{2,1,0:T(8,128)(2,1)}), bf16[8,64,1536]{2,1,0:T(8,128)(2,1)S(1)}, u32[]{:S(2)}, u32[]{:S(2)}) async-start(bf16[8,64,1536]{2,1,0:T(8,128)(2,1)} %bitcast.140), calls=%async_computation.13 | async-start | bytes 3145728 | tf_op jit(solution)/shard_map/all_to_all | solution.py:235
  990.8 54.1 %collective-permute-start.76 = (bf16[64,1536]{1,0:T(8,128)(2,1)S(1)}, bf16[64,1536]{1,0:T(8,128)(2,1)S(1)}, u32[]{:S(2)}, u32[]{:S(2)}) collective-permute-start(bf16[64,1536]{1,0:T(8,128)(2,1)S(1)} %copy-done.149), channel_id=1, source_target_pairs={{0,10},{1,11},{2,8},{3,9},{4,14},{5,15},{6,12},{7,13},{8,2},{9,3},... | collective-permute-start | bytes 589832 | tf_op jit(solution)/shard_map/ppermute | solution.py:231
  1006.9 51.1 %collective-permute-start.77 = (bf16[64,1536]{1,0:T(8,128)(2,1)}, bf16[64,1536]{1,0:T(8,128)(2,1)S(1)}, u32[]{:S(2)}, u32[]{:S(2)}) collective-permute-start(bf16[64,1536]{1,0:T(8,128)(2,1)} %get-tuple-element.258), channel_id=1, source_target_pairs={{0,14},{1,15},{2,12},{3,13},{4,10},{5,11},{6,8},{7,9},{8,6},{9,7},... | collective-permute-start | bytes 589832 | tf_op jit(solution)/shard_map/ppermute | solution.py:231
  1015.5 55.7 %collective-permute-start.79 = (bf16[64,1536]{1,0:T(8,128)(2,1)}, bf16[64,1536]{1,0:T(8,128)(2,1)S(1)}, u32[]{:S(2)}, u32[]{:S(2)}) collective-permute-start(bf16[64,1536]{1,0:T(8,128)(2,1)} %get-tuple-element.260), channel_id=1, source_target_pairs={{0,15},{1,14},{2,13},{3,12},{4,11},{5,10},{6,9},{7,8},{8,7},{9,6},... | collective-permute-start | bytes 589832 | tf_op jit(solution)/shard_map/ppermute | solution.py:231
  1138.0 180.8 %all-to-all-start.15 = ((bf16[8,64,1536]{2,1,0:T(8,128)(2,1)}), bf16[8,64,1536]{2,1,0:T(8,128)(2,1)S(1)}, u32[]{:S(2)}, u32[]{:S(2)}) async-start(bf16[8,64,1536]{2,1,0:T(8,128)(2,1)} %bitcast.138), calls=%async_computation.15 | async-start | bytes 3145728 | tf_op jit(solution)/shard_map/all_to_all | solution.py:235
  1180.0 51.5 %collective-permute-start.60 = (bf16[64,1536]{1,0:T(8,128)(2,1)S(1)}, bf16[64,1536]{1,0:T(8,128)(2,1)S(1)}, u32[]{:S(2)}, u32[]{:S(2)}) collective-permute-start(bf16[64,1536]{1,0:T(8,128)(2,1)S(1)} %copy-done.145), channel_id=1, source_target_pairs={{0,10},{1,11},{2,8},{3,9},{4,14},{5,15},{6,12},{7,13},{8,2},{9,3},... | collective-permute-start | bytes 589832 | tf_op jit(solution)/shard_map/ppermute | solution.py:231
  1182.4 55.0 %collective-permute-start.61 = (bf16[64,1536]{1,0:T(8,128)(2,1)S(1)}, bf16[64,1536]{1,0:T(8,128)(2,1)S(1)}, u32[]{:S(2)}, u32[]{:S(2)}) collective-permute-start(bf16[64,1536]{1,0:T(8,128)(2,1)S(1)} %copy-done.144), channel_id=1, source_target_pairs={{0,14},{1,15},{2,12},{3,13},{4,10},{5,11},{6,8},{7,9},{8,6},{9,7},... | collective-permute-start | bytes 589832 | tf_op jit(solution)/shard_map/ppermute | solution.py:231
  1320.0 150.8 %all-to-all-start.14 = ((bf16[8,64,1536]{2,1,0:T(8,128)(2,1)}), bf16[8,64,1536]{2,1,0:T(8,128)(2,1)S(1)}, u32[]{:S(2)}, u32[]{:S(2)}) async-start(bf16[8,64,1536]{2,1,0:T(8,128)(2,1)} %bitcast.139), calls=%async_computation.14 | async-start | bytes 3145728 | tf_op jit(solution)/shard_map/all_to_all | solution.py:235
  (299 other events, 9666.9 us)

commit v4 on v2

--- a/solution.py
+++ b/solution.py
@@ -9,7 +9,7 @@
 from jax.sharding import PartitionSpec as P
 
 keep_rate = 0.9
-CHUNKS = 8
+CHUNKS = 6
 TILE = 512
 VMEM_LIMIT = 60 * 1024 * 1024
 FIRST_LAG = 4

time: 1210 us -> 1180 us (0.975)
  starting transfers between devices: 378 us -> 474 us
  waiting for transfers between devices: 534 us -> 440 us
  Pallas kernels: 257 us -> 235 us
    ppermute x240 -> x180, starting transfers between devices: 375 us -> 470 us  [exchange(): lax.ppermute(part, 'blk', [(i, i ^ hop) for i in range(plan.devices)])]
    ppermute x240 -> x180, waiting for transfers between devices: 528 us -> 435 us  [exchange(): lax.ppermute(part, 'blk', [(i, i ^ hop) for i in range(plan.devices)])]
    pallas_call x24 -> x18, Pallas kernels: 257 us -> 235 us  [call(): pl.pallas_call(body, out_shape=outs, grid=(plan.steps,), in_specs=in_spec...]
  transfers between devices with their start and end apart: 242 -> 182, of which waited for: 81 -> 52; matrix products, arithmetic and copies ran while one was open for 1% -> 1% of each run, Pallas kernels for 21% -> 19%
where the time goes in v4:
time: 1180 us; the launch traced here: 1170 us
  starting transfers between devices  474 us (40%)
  waiting for transfers between devices  440 us (37%)
  Pallas kernels  235 us (20%)
  local copies, waits for them, and re-layouts  12.4 us (1%)
    ppermute x180, starting transfers between devices, exchange(): lax.ppermute(part, 'blk', [(i, i ^ hop) for i in range(plan.devices)])  470 us
    ppermute x180, waiting for transfers between devices, exchange(): lax.ppermute(part, 'blk', [(i, i ^ hop) for i in range(plan.devices)])  435 us
    pallas_call x18, Pallas kernels, call(): pl.pallas_call(body, out_shape=outs, grid=(plan.steps,), in_specs=in_spec...  235 us
  transfers between devices with their start and end apart: 182, of which 52 were waited for; matrix products, arithmetic and copies ran while one was open for 1% of the time, Pallas kernels for 19%

profile of v4, /device:TPU:16, one launch (start us, length us, event | category | flops | bytes accessed | tf_op | source)
XLA Modules:
  0.0 1173.5 jit_solution(5928109192386885697)
XLA Ops:
  33.6 15.8 %collective-permute-done.17.refs_3_ = bf16[64,2048]{1,0:T(8,128)(2,1)S(1)} collective-permute-done((bf16[64,2048]{1,0:T(8,128)(2,1)}, bf16[64,2048]{1,0:T(8,128)(2,1)S(1)}, u32[]{:S(2)}, u32[]{:S(2)}) %collective-permute-start.17) | collective-permute-done | bytes 262176 | tf_op jit(solution)/shard_map/ppermute | solution.py:225
  72.0 13.5 %collective-permute-done.23.refs_9_ = bf16[64,2048]{1,0:T(8,128)(2,1)S(1)} collective-permute-done((bf16[64,2048]{1,0:T(8,128)(2,1)}, bf16[64,2048]{1,0:T(8,128)(2,1)S(1)}, u32[]{:S(2)}, u32[]{:S(2)}) %collective-permute-start.23) | collective-permute-done | bytes 262176 | tf_op jit(solution)/shard_map/ppermute | solution.py:225
  256.4 16.2 %collective-permute-start.118 = (bf16[64,2048]{1,0:T(8,128)(2,1)}, bf16[64,2048]{1,0:T(8,128)(2,1)S(1)}, u32[]{:S(2)}, u32[]{:S(2)}) collective-permute-start(bf16[64,2048]{1,0:T(8,128)(2,1)} %get-tuple-element.347), channel_id=1, source_target_pairs={{0,7},{1,6},{2,5},{3,4},{4,3},{5,2},{6,1},{7,0},{8,15},{9,14},{10,... | collective-permute-start | bytes 786440 | tf_op jit(solution)/shard_map/ppermute | solution.py:225
  310.5 17.2 %collective-permute-done.100.refs_11_ = bf16[64,2048]{1,0:T(8,128)(2,1)S(1)} collective-permute-done((bf16[64,2048]{1,0:T(8,128)(2,1)}, bf16[64,2048]{1,0:T(8,128)(2,1)S(1)}, u32[]{:S(2)}, u32[]{:S(2)}) %collective-permute-start.100) | collective-permute-done | bytes 262176 | tf_op jit(solution)/shard_map/ppermute | solution.py:225
  331.3 18.8 %collective-permute-done.104.refs_15_ = bf16[64,2048]{1,0:T(8,128)(2,1)S(1)} collective-permute-done((bf16[64,2048]{1,0:T(8,128)(2,1)}, bf16[64,2048]{1,0:T(8,128)(2,1)S(1)}, u32[]{:S(2)}, u32[]{:S(2)}) %collective-permute-start.104) | collective-permute-done | bytes 262176 | tf_op jit(solution)/shard_map/ppermute | solution.py:225
  362.2 17.7 %collective-permute-start.99 = (bf16[64,2048]{1,0:T(8,128)(2,1)}, bf16[64,2048]{1,0:T(8,128)(2,1)S(1)}, u32[]{:S(2)}, u32[]{:S(2)}) collective-permute-start(bf16[64,2048]{1,0:T(8,128)(2,1)} %get-tuple-element.327), channel_id=1, source_target_pairs={{0,6},{1,7},{2,4},{3,5},{4,2},{5,3},{6,0},{7,1},{8,14},{9,15},{10,... | collective-permute-start | bytes 786440 | tf_op jit(solution)/shard_map/ppermute | solution.py:225
  379.9 14.4 %shard_map.113 = (bf16[64,2048]{1,0:T(8,128)(2,1)}, bf16[64,2048]{1,0:T(8,128)(2,1)}, bf16[64,2048]{1,0:T(8,128)(2,1)}, bf16[64,2048]{1,0:T(8,128)(2,1)}, bf16[6...) custom-call(bf16[64,2048]{1,0:T(8,128)(2,1)} %get-tuple-element.237., ...), custom_call_target="tpu_custom_call" | custom-call | flops 12884901888 | bytes 16777216 | tf_op jit(solution)/shard_map/pallas_call | solution.py:70
  420.8 14.4 %collective-permute-done.64.refs_4_.refs_27_.refs_5_ = bf16[64,2048]{1,0:T(8,128)(2,1)S(1)} collective-permute-done((bf16[64,2048]{1,0:T(8,128)(2,1)}, bf16[64,2048]{1,0:T(8,128)(2,1)S(1)}, u32[]{:S(2)}, u32[]{:S(2)}) %collective-permute-start.64) | collective-permute-done | bytes 262176 | tf_op jit(solution)/shard_map/ppermute | solution.py:225
  461.9 14.8 %shard_map.114 = (bf16[64,2048]{1,0:T(8,128)(2,1)}, bf16[64,2048]{1,0:T(8,128)(2,1)}, bf16[64,2048]{1,0:T(8,128)(2,1)}, bf16[64,2048]{1,0:T(8,128)(2,1)}, bf16[6...) custom-call(bf16[64,2048]{1,0:T(8,128)(2,1)} %get-tuple-element.221., ...), custom_call_target="tpu_custom_call", output_to_operand_aliasing={{16}: (21, {}), {17}: (22, {})} | custom-call | flops 12884901888 | bytes 16777216 | tf_op jit(solution)/shard_map/pallas_call | solution.py:70
  487.9 16.8 %collective-permute-done.30.refs_0_.refs_23_.refs_1_ = bf16[64,2048]{1,0:T(8,128)(2,1)S(1)} collective-permute-done((bf16[64,2048]{1,0:T(8,128)(2,1)}, bf16[64,2048]{1,0:T(8,128)(2,1)S(1)}, u32[]{:S(2)}, u32[]{:S(2)}) %collective-permute-start.30) | collective-permute-done | bytes 262176 | tf_op jit(solution)/shard_map/ppermute | solution.py:225
  527.4 14.4 %collective-permute-done.36.refs_6_.refs_29_.refs_7_ = bf16[64,2048]{1,0:T(8,128)(2,1)S(1)} collective-permute-done((bf16[64,2048]{1,0:T(8,128)(2,1)}, bf16[64,2048]{1,0:T(8,128)(2,1)S(1)}, u32[]{:S(2)}, u32[]{:S(2)}) %collective-permute-start.36) | collective-permute-done | bytes 262176 | tf_op jit(solution)/shard_map/ppermute | solution.py:225
  549.6 14.8 %shard_map.119 = (bf16[64,2048]{1,0:T(8,128)(2,1)}, bf16[64,2048]{1,0:T(8,128)(2,1)}, bf16[64,2048]{1,0:T(8,128)(2,1)}, bf16[64,2048]{1,0:T(8,128)(2,1)}, bf16[6...) custom-call(bf16[64,2048]{1,0:T(8,128)(2,1)} %get-tuple-element.333., ...), custom_call_target="tpu_custom_call", output_to_operand_aliasing={{16}: (21, {}), {17}: (22, {})} | custom-call | flops 12884901888 | bytes 16777216 | tf_op jit(solution)/shard_map/pallas_call | solution.py:70
  590.5 13.6 %collective-permute-start.125 = (bf16[64,2048]{1,0:T(8,128)(2,1)}, bf16[64,2048]{1,0:T(8,128)(2,1)S(1)}, u32[]{:S(2)}, u32[]{:S(2)}) collective-permute-start(bf16[64,2048]{1,0:T(8,128)(2,1)} %get-tuple-element.360), channel_id=1, source_target_pairs={{0,5},{1,4},{2,7},{3,6},{4,1},{5,0},{6,3},{7,2},{8,13},{9,12},{10,... | collective-permute-start | bytes 786440 | tf_op jit(solution)/shard_map/ppermute | solution.py:225
  619.2 17.5 %collective-permute-done.126.refs_29_.refs_7_ = bf16[64,2048]{1,0:T(8,128)(2,1)S(1)} collective-permute-done((bf16[64,2048]{1,0:T(8,128)(2,1)}, bf16[64,2048]{1,0:T(8,128)(2,1)S(1)}, u32[]{:S(2)}, u32[]{:S(2)}) %collective-permute-start.126) | collective-permute-done | bytes 262176 | tf_op jit(solution)/shard_map/ppermute | solution.py:225
  673.8 23.8 %collective-permute-start.80 = (bf16[64,2048]{1,0:T(8,128)(2,1)}, bf16[64,2048]{1,0:T(8,128)(2,1)}, u32[]{:S(2)}, u32[]{:S(2)}) collective-permute-start(bf16[64,2048]{1,0:T(8,128)(2,1)} %get-tuple-element.307), channel_id=1, source_target_pairs={{0,5},{1,4},{2,7},{3,6},{4,1},{5,0},{6,3},{7,2},{8,13},{9,12},{10,... | collective-permute-start | bytes 786440 | tf_op jit(solution)/shard_map/ppermute | solution.py:225
  712.6 17.5 %collective-permute-done.81.refs_7_ = bf16[64,2048]{1,0:T(8,128)(2,1)} collective-permute-done((bf16[64,2048]{1,0:T(8,128)(2,1)}, bf16[64,2048]{1,0:T(8,128)(2,1)}, u32[]{:S(2)}, u32[]{:S(2)}) %collective-permute-start.81) | collective-permute-done | bytes 262176 | tf_op jit(solution)/shard_map/ppermute | solution.py:225
  737.9 14.7 %shard_map.120 = (bf16[64,2048]{1,0:T(8,128)(2,1)}, bf16[64,2048]{1,0:T(8,128)(2,1)}, bf16[64,2048]{1,0:T(8,128)(2,1)}, bf16[64,2048]{1,0:T(8,128)(2,1)}, bf16[6...) custom-call(bf16[64,2048]{1,0:T(8,128)(2,1)} %get-tuple-element.317., ...), custom_call_target="tpu_custom_call", output_to_operand_aliasing={{16}: (21, {}), {17}: (22, {})} | custom-call | flops 12884901888 | bytes 16777216 | tf_op jit(solution)/shard_map/pallas_call | solution.py:70
  770.5 20.9 %collective-permute-start.140 = (bf16[64,2048]{1,0:T(8,128)(2,1)}, bf16[64,2048]{1,0:T(8,128)(2,1)S(1)}, u32[]{:S(2)}, u32[]{:S(2)}) collective-permute-start(bf16[64,2048]{1,0:T(8,128)(2,1)} %get-tuple-element.377), channel_id=1, source_target_pairs={{0,5},{1,4},{2,7},{3,6},{4,1},{5,0},{6,3},{7,2},{8,13},{9,12},{10,... | collective-permute-start | bytes 786440 | tf_op jit(solution)/shard_map/ppermute | solution.py:225
  806.4 17.5 %collective-permute-done.141.refs_29_.refs_7_ = bf16[64,2048]{1,0:T(8,128)(2,1)S(1)} collective-permute-done((bf16[64,2048]{1,0:T(8,128)(2,1)}, bf16[64,2048]{1,0:T(8,128)(2,1)S(1)}, u32[]{:S(2)}, u32[]{:S(2)}) %collective-permute-start.141) | collective-permute-done | bytes 262176 | tf_op jit(solution)/shard_map/ppermute | solution.py:225
  861.3 16.2 %shard_map.123 = (bf16[12288,1024]{1,0:T(8,128)(2,1)}, f32[8,128,128]{2,1,0:T(8,128)}) custom-call(bf16[64,2048]{1,0:T(8,128)(2,1)} %get-tuple-element.423.refs_0_, bf16[64,2048]{1,0:T(8,128)(2,1)} %copy-done.2, bf16[64,2048]{1,0:T(8,128)(2,1)} %copy-done.3, bf16[64,2048]{1,0:T(8,128)(2,1)} %copy-done.4, bf16[64,2048]{1,0:T(8,128)(2,1)} %copy-done.5, ...), custom_call_target="tpu_custom_call" | custom-call | flops 8589934592 | bytes 102760448 | tf_op jit(solution)/shard_map/pallas_call | solution.py:70
  877.6 17.9 %collective-permute-start.50 = (bf16[64,2048]{1,0:T(8,128)(2,1)}, bf16[64,2048]{1,0:T(8,128)(2,1)S(1)}, u32[]{:S(2)}, u32[]{:S(2)}) collective-permute-start(bf16[64,2048]{1,0:T(8,128)(2,1)} %get-tuple-element.276), channel_id=1, source_target_pairs={{0,5},{1,4},{2,7},{3,6},{4,1},{5,0},{6,3},{7,2},{8,13},{9,12},{10,... | collective-permute-start | bytes 786440 | tf_op jit(solution)/shard_map/ppermute | solution.py:225
  901.7 16.7 %shard_map.124 = (bf16[12288,1024]{1,0:T(8,128)(2,1)}, f32[8,128,128]{2,1,0:T(8,128)}) custom-call(bf16[64,2048]{1,0:T(8,128)(2,1)} %get-tuple-element.422.refs_0_, bf16[64,2048]{1,0:T(8,128)(2,1)} %copy-done.16, bf16[64,2048]{1,0:T(8,128)(2,1)} %copy-done.18, bf16[64,2048]{1,0:T(8,128)(2,1)} %copy-done.19, ...), custom_call_target="tpu_custom_call", output_to_operand_aliasing={{0}: (19, {}), {1}: (20, {})} | custom-call | flops 8589934592 | bytes 102760448 | tf_op jit(solution)/shard_map/pallas_call | solution.py:70
  923.2 13.1 %collective-permute-start.59 = (bf16[64,2048]{1,0:T(8,128)(2,1)S(1)}, bf16[64,2048]{1,0:T(8,128)(2,1)S(1)}, u32[]{:S(2)}, u32[]{:S(2)}) collective-permute-start(bf16[64,2048]{1,0:T(8,128)(2,1)S(1)} %copy-done.134), channel_id=1, source_target_pairs={{0,15},{1,14},{2,13},{3,12},{4,11},{5,10},{6,9},{7,8},{8,7},{9,6},... | collective-permute-start | bytes 786440 | tf_op jit(solution)/shard_map/ppermute | solution.py:225
  936.3 14.7 %shard_map.121 = (bf16[64,2048]{1,0:T(8,128)(2,1)}, bf16[64,2048]{1,0:T(8,128)(2,1)}, bf16[64,2048]{1,0:T(8,128)(2,1)}, bf16[64,2048]{1,0:T(8,128)(2,1)}, bf16[6...) custom-call(bf16[64,2048]{1,0:T(8,128)(2,1)} %get-tuple-element.301., ...), custom_call_target="tpu_custom_call", output_to_operand_aliasing={{16}: (21, {}), {17}: (22, {})} | custom-call | flops 12884901888 | bytes 16777216 | tf_op jit(solution)/shard_map/pallas_call | solution.py:70
  957.3 12.1 %collective-permute-done.59.refs_15_ = bf16[64,2048]{1,0:T(8,128)(2,1)S(1)} collective-permute-done((bf16[64,2048]{1,0:T(8,128)(2,1)S(1)}, bf16[64,2048]{1,0:T(8,128)(2,1)S(1)}, u32[]{:S(2)}, u32[]{:S(2)}) %collective-permute-start.59) | collective-permute-done | bytes 262176 | tf_op jit(solution)/shard_map/ppermute | solution.py:225
  970.1 14.7 %shard_map.122 = (bf16[64,2048]{1,0:T(8,128)(2,1)}, bf16[64,2048]{1,0:T(8,128)(2,1)}, bf16[64,2048]{1,0:T(8,128)(2,1)}, bf16[64,2048]{1,0:T(8,128)(2,1)}, bf16[6...) custom-call(bf16[64,2048]{1,0:T(8,128)(2,1)} %get-tuple-element.270., ...), custom_call_target="tpu_custom_call", output_to_operand_aliasing={{16}: (21, {}), {17}: (22, {})} | custom-call | flops 12884901888 | bytes 16777216 | tf_op jit(solution)/shard_map/pallas_call | solution.py:70
  993.4 16.4 %shard_map.125 = (bf16[12288,1024]{1,0:T(8,128)(2,1)}, f32[8,128,128]{2,1,0:T(8,128)}) custom-call(bf16[64,2048]{1,0:T(8,128)(2,1)} %get-tuple-element.421.refs_0_, bf16[64,2048]{1,0:T(8,128)(2,1)} %copy-done.27, bf16[64,2048]{1,0:T(8,128)(2,1)} %copy-done.28, bf16[64,2048]{1,0:T(8,128)(2,1)} %copy-done.29, ...), custom_call_target="tpu_custom_call", output_to_operand_aliasing={{0}: (19, {}), {1}: (20, {})} | custom-call | flops 8589934592 | bytes 102760448 | tf_op jit(solution)/shard_map/pallas_call | solution.py:70
  1016.0 15.3 %collective-permute-start.179 = (bf16[64,2048]{1,0:T(8,128)(2,1)S(1)}, bf16[64,2048]{1,0:T(8,128)(2,1)S(1)}, u32[]{:S(2)}, u32[]{:S(2)}) collective-permute-start(bf16[64,2048]{1,0:T(8,128)(2,1)S(1)} %copy-done.130), channel_id=1, source_target_pairs={{0,15},{1,14},{2,13},{3,12},{4,11},{5,10},{6,9},{7,8},{8,7},{9,6},... | collective-permute-start | bytes 786440 | tf_op jit(solution)/shard_map/ppermute | solution.py:225
  1031.3 16.3 %shard_map.126 = (bf16[12288,1024]{1,0:T(8,128)(2,1)}, f32[8,128,128]{2,1,0:T(8,128)}) custom-call(bf16[64,2048]{1,0:T(8,128)(2,1)} %get-tuple-element.420.refs_0_, bf16[64,2048]{1,0:T(8,128)(2,1)} %copy-done.42, bf16[64,2048]{1,0:T(8,128)(2,1)} %copy-done.43, bf16[64,2048]{1,0:T(8,128)(2,1)} %copy-done.44, ...), custom_call_target="tpu_custom_call", output_to_operand_aliasing={{0}: (19, {}), {1}: (20, {})} | custom-call | flops 8589934592 | bytes 102760448 | tf_op jit(solution)/shard_map/pallas_call | solution.py:70
  1103.7 13.7 %collective-permute-start.163 = (bf16[64,2048]{1,0:T(8,128)(2,1)}, bf16[64,2048]{1,0:T(8,128)(2,1)}, u32[]{:S(2)}, u32[]{:S(2)}) collective-permute-start(bf16[64,2048]{1,0:T(8,128)(2,1)} %get-tuple-element.402), channel_id=1, source_target_pairs={{0,7},{1,6},{2,5},{3,4},{4,3},{5,2},{6,1},{7,0},{8,15},{9,14},{10,... | collective-permute-start | bytes 786440 | tf_op jit(solution)/shard_map/ppermute | solution.py:225
  1124.9 16.3 %shard_map.127 = (bf16[12288,1024]{1,0:T(8,128)(2,1)}, f32[8,128,128]{2,1,0:T(8,128)}) custom-call(bf16[64,2048]{1,0:T(8,128)(2,1)} %get-tuple-element.404.refs_0_, bf16[64,2048]{1,0:T(8,128)(2,1)} %copy-done.95, bf16[64,2048]{1,0:T(8,128)(2,1)} %copy-done.96, bf16[64,2048]{1,0:T(8,128)(2,1)} %copy-done.97, ...), custom_call_target="tpu_custom_call", output_to_operand_aliasing={{0}: (19, {}), {1}: (20, {})} | custom-call | flops 8589934592 | bytes 102760448 | tf_op jit(solution)/shard_map/pallas_call | solution.py:70
  1144.3 16.5 %shard_map.128 = (bf16[12288,1024]{1,0:T(8,128)(2,1)}, f32[8,128,128]{2,1,0:T(8,128)}) custom-call(bf16[64,2048]{1,0:T(8,128)(2,1)} %get-tuple-element.388.refs_0_, bf16[64,2048]{1,0:T(8,128)(2,1)} %copy-done.112, bf16[64,2048]{1,0:T(8,128)(2,1)} %copy-done.115, bf16[64,2048]{1,0:T(8,128)(2,1)} %copy-done.117, ...), custom_call_target="tpu_custom_call", output_to_operand_aliasing={{0}: (19, {}), {1}: (20, {})} | custom-call | flops 8589934592 | bytes 102760448 | tf_op jit(solution)/shard_map/pallas_call | solution.py:70
  (673 shorter events, 656.2 us)
Async XLA Ops:
  20.0 42.9 %collective-permute-start.19 = (bf16[64,2048]{1,0:T(8,128)(2,1)}, bf16[64,2048]{1,0:T(8,128)(2,1)S(1)}, u32[]{:S(2)}, u32[]{:S(2)}) collective-permute-start(bf16[64,2048]{1,0:T(8,128)(2,1)} %get-tuple-element.242), channel_id=1, source_target_pairs={{0,9},{1,8},{2,11},{3,10},{4,13},{5,12},{6,15},{7,14},{8,1},{9,0},... | collective-permute-start | bytes 786440 | tf_op jit(solution)/shard_map/ppermute | solution.py:225
  102.3 42.0 %collective-permute-start.10 = (bf16[64,2048]{1,0:T(8,128)(2,1)}, bf16[64,2048]{1,0:T(8,128)(2,1)}, u32[]{:S(2)}, u32[]{:S(2)}) collective-permute-start(bf16[64,2048]{1,0:T(8,128)(2,1)} %get-tuple-element.232), channel_id=1, source_target_pairs={{0,14},{1,15},{2,12},{3,13},{4,10},{5,11},{6,8},{7,9},{8,6},{9,7},... | collective-permute-start | bytes 786440 | tf_op jit(solution)/shard_map/ppermute | solution.py:225
  144.3 38.8 %collective-permute-start.3 = (bf16[64,2048]{1,0:T(8,128)(2,1)}, bf16[64,2048]{1,0:T(8,128)(2,1)S(1)}, u32[]{:S(2)}, u32[]{:S(2)}) collective-permute-start(bf16[64,2048]{1,0:T(8,128)(2,1)} %get-tuple-element.225), channel_id=1, source_target_pairs={{0,1},{1,0},{2,3},{3,2},{4,5},{5,4},{6,7},{7,6},{8,9},{9,8},{10,11... | collective-permute-start | bytes 786440 | tf_op jit(solution)/shard_map/ppermute | solution.py:225
  144.4 38.8 %collective-permute-start.4 = (bf16[64,2048]{1,0:T(8,128)(2,1)}, bf16[64,2048]{1,0:T(8,128)(2,1)S(1)}, u32[]{:S(2)}, u32[]{:S(2)}) collective-permute-start(bf16[64,2048]{1,0:T(8,128)(2,1)} %get-tuple-element.226), channel_id=1, source_target_pairs={{0,9},{1,8},{2,11},{3,10},{4,13},{5,12},{6,15},{7,14},{8,1},{9,0},... | collective-permute-start | bytes 786440 | tf_op jit(solution)/shard_map/ppermute | solution.py:225
  156.6 45.7 %collective-permute-start.5 = (bf16[64,2048]{1,0:T(8,128)(2,1)}, bf16[64,2048]{1,0:T(8,128)(2,1)S(1)}, u32[]{:S(2)}, u32[]{:S(2)}) collective-permute-start(bf16[64,2048]{1,0:T(8,128)(2,1)} %get-tuple-element.227), channel_id=1, source_target_pairs={{0,5},{1,4},{2,7},{3,6},{4,1},{5,0},{6,3},{7,2},{8,13},{9,12},{10,... | collective-permute-start | bytes 786440 | tf_op jit(solution)/shard_map/ppermute | solution.py:225
  212.8 38.6 %collective-permute-start.110 = (bf16[64,2048]{1,0:T(8,128)(2,1)}, bf16[64,2048]{1,0:T(8,128)(2,1)}, u32[]{:S(2)}, u32[]{:S(2)}) collective-permute-start(bf16[64,2048]{1,0:T(8,128)(2,1)} %get-tuple-element.339), channel_id=1, source_target_pairs={{0,5},{1,4},{2,7},{3,6},{4,1},{5,0},{6,3},{7,2},{8,13},{9,12},{10,... | collective-permute-start | bytes 786440 | tf_op jit(solution)/shard_map/ppermute | solution.py:225
  256.4 40.0 %collective-permute-start.118 = (bf16[64,2048]{1,0:T(8,128)(2,1)}, bf16[64,2048]{1,0:T(8,128)(2,1)S(1)}, u32[]{:S(2)}, u32[]{:S(2)}) collective-permute-start(bf16[64,2048]{1,0:T(8,128)(2,1)} %get-tuple-element.347), channel_id=1, source_target_pairs={{0,7},{1,6},{2,5},{3,4},{4,3},{5,2},{6,1},{7,0},{8,15},{9,14},{10,... | collective-permute-start | bytes 786440 | tf_op jit(solution)/shard_map/ppermute | solution.py:225
  286.0 41.7 %collective-permute-start.100 = (bf16[64,2048]{1,0:T(8,128)(2,1)}, bf16[64,2048]{1,0:T(8,128)(2,1)S(1)}, u32[]{:S(2)}, u32[]{:S(2)}) collective-permute-start(bf16[64,2048]{1,0:T(8,128)(2,1)} %get-tuple-element.328), channel_id=1, source_target_pairs={{0,14},{1,15},{2,12},{3,13},{4,10},{5,11},{6,8},{7,9},{8,6},{9,7},... | collective-permute-start | bytes 786440 | tf_op jit(solution)/shard_map/ppermute | solution.py:225
  286.0 41.7 %collective-permute-start.101 = (bf16[64,2048]{1,0:T(8,128)(2,1)}, bf16[64,2048]{1,0:T(8,128)(2,1)S(1)}, u32[]{:S(2)}, u32[]{:S(2)}) collective-permute-start(bf16[64,2048]{1,0:T(8,128)(2,1)} %get-tuple-element.329), channel_id=1, source_target_pairs={{0,3},{1,2},{2,1},{3,0},{4,7},{5,6},{6,5},{7,4},{8,11},{9,10},{10,... | collective-permute-start | bytes 786440 | tf_op jit(solution)/shard_map/ppermute | solution.py:225
  286.1 41.7 %collective-permute-start.102 = (bf16[64,2048]{1,0:T(8,128)(2,1)}, bf16[64,2048]{1,0:T(8,128)(2,1)S(1)}, u32[]{:S(2)}, u32[]{:S(2)}) collective-permute-start(bf16[64,2048]{1,0:T(8,128)(2,1)} %get-tuple-element.330), channel_id=1, source_target_pairs={{0,11},{1,10},{2,9},{3,8},{4,15},{5,14},{6,13},{7,12},{8,3},{9,2},... | collective-permute-start | bytes 786440 | tf_op jit(solution)/shard_map/ppermute | solution.py:225
  309.1 41.0 %collective-permute-start.104 = (bf16[64,2048]{1,0:T(8,128)(2,1)}, bf16[64,2048]{1,0:T(8,128)(2,1)S(1)}, u32[]{:S(2)}, u32[]{:S(2)}) collective-permute-start(bf16[64,2048]{1,0:T(8,128)(2,1)} %get-tuple-element.332), channel_id=1, source_target_pairs={{0,15},{1,14},{2,13},{3,12},{4,11},{5,10},{6,9},{7,8},{8,7},{9,6},... | collective-permute-start | bytes 786440 | tf_op jit(solution)/shard_map/ppermute | solution.py:225
  351.1 43.2 %collective-permute-start.95 = (bf16[64,2048]{1,0:T(8,128)(2,1)}, bf16[64,2048]{1,0:T(8,128)(2,1)S(1)}, u32[]{:S(2)}, u32[]{:S(2)}) collective-permute-start(bf16[64,2048]{1,0:T(8,128)(2,1)} %get-tuple-element.323), channel_id=1, source_target_pairs={{0,5},{1,4},{2,7},{3,6},{4,1},{5,0},{6,3},{7,2},{8,13},{9,12},{10,... | collective-permute-start | bytes 786440 | tf_op jit(solution)/shard_map/ppermute | solution.py:225
  351.1 43.3 %collective-permute-start.96 = (bf16[64,2048]{1,0:T(8,128)(2,1)}, bf16[64,2048]{1,0:T(8,128)(2,1)S(1)}, u32[]{:S(2)}, u32[]{:S(2)}) collective-permute-start(bf16[64,2048]{1,0:T(8,128)(2,1)} %get-tuple-element.324), channel_id=1, source_target_pairs={{0,13},{1,12},{2,15},{3,14},{4,9},{5,8},{6,11},{7,10},{8,5},{9,4},... | collective-permute-start | bytes 786440 | tf_op jit(solution)/shard_map/ppermute | solution.py:225
  354.0 41.1 %collective-permute-start.97 = (bf16[64,2048]{1,0:T(8,128)(2,1)}, bf16[64,2048]{1,0:T(8,128)(2,1)S(1)}, u32[]{:S(2)}, u32[]{:S(2)}) collective-permute-start(bf16[64,2048]{1,0:T(8,128)(2,1)} %get-tuple-element.325), channel_id=1, source_target_pairs={{0,2},{1,3},{2,0},{3,1},{4,6},{5,7},{6,4},{7,5},{8,10},{9,11},{10,... | collective-permute-start | bytes 786440 | tf_op jit(solution)/shard_map/ppermute | solution.py:225
  404.8 41.6 %collective-permute-start.66 = (bf16[64,2048]{1,0:T(8,128)(2,1)}, bf16[64,2048]{1,0:T(8,128)(2,1)S(1)}, u32[]{:S(2)}, u32[]{:S(2)}) collective-permute-start(bf16[64,2048]{1,0:T(8,128)(2,1)} %get-tuple-element.292), channel_id=1, source_target_pairs={{0,13},{1,12},{2,15},{3,14},{4,9},{5,8},{6,11},{7,10},{8,5},{9,4},... | collective-permute-start | bytes 786440 | tf_op jit(solution)/shard_map/ppermute | solution.py:225
  437.0 39.8 %collective-permute-start.70 = (bf16[64,2048]{1,0:T(8,128)(2,1)}, bf16[64,2048]{1,0:T(8,128)(2,1)S(1)}, u32[]{:S(2)}, u32[]{:S(2)}) collective-permute-start(bf16[64,2048]{1,0:T(8,128)(2,1)} %get-tuple-element.296), channel_id=1, source_target_pairs={{0,14},{1,15},{2,12},{3,13},{4,10},{5,11},{6,8},{7,9},{8,6},{9,7},... | collective-permute-start | bytes 786440 | tf_op jit(solution)/shard_map/ppermute | solution.py:225
  487.9 39.2 %collective-permute-start.34 = (bf16[64,2048]{1,0:T(8,128)(2,1)}, bf16[64,2048]{1,0:T(8,128)(2,1)S(1)}, u32[]{:S(2)}, u32[]{:S(2)}) collective-permute-start(bf16[64,2048]{1,0:T(8,128)(2,1)} %get-tuple-element.259), channel_id=1, source_target_pairs={{0,9},{1,8},{2,11},{3,10},{4,13},{5,12},{6,15},{7,14},{8,1},{9,0},... | collective-permute-start | bytes 786440 | tf_op jit(solution)/shard_map/ppermute | solution.py:225
  544.0 39.1 %collective-permute-start.43 = (bf16[64,2048]{1,0:T(8,128)(2,1)}, bf16[64,2048]{1,0:T(8,128)(2,1)}, u32[]{:S(2)}, u32[]{:S(2)}) collective-permute-start(bf16[64,2048]{1,0:T(8,128)(2,1)} %get-tuple-element.268), channel_id=1, source_target_pairs={{0,7},{1,6},{2,5},{3,4},{4,3},{5,2},{6,1},{7,0},{8,15},{9,14},{10,... | collective-permute-start | bytes 786440 | tf_op jit(solution)/shard_map/ppermute | solution.py:225
  608.8 39.5 %collective-permute-start.129 = (bf16[64,2048]{1,0:T(8,128)(2,1)}, bf16[64,2048]{1,0:T(8,128)(2,1)S(1)}, u32[]{:S(2)}, u32[]{:S(2)}) collective-permute-start(bf16[64,2048]{1,0:T(8,128)(2,1)} %get-tuple-element.364), channel_id=1, source_target_pairs={{0,6},{1,7},{2,4},{3,5},{4,2},{5,3},{6,0},{7,1},{8,14},{9,15},{10,... | collective-permute-start | bytes 786440 | tf_op jit(solution)/shard_map/ppermute | solution.py:225
  673.8 38.9 %collective-permute-start.80 = (bf16[64,2048]{1,0:T(8,128)(2,1)}, bf16[64,2048]{1,0:T(8,128)(2,1)}, u32[]{:S(2)}, u32[]{:S(2)}) collective-permute-start(bf16[64,2048]{1,0:T(8,128)(2,1)} %get-tuple-element.307), channel_id=1, source_target_pairs={{0,5},{1,4},{2,7},{3,6},{4,1},{5,0},{6,3},{7,2},{8,13},{9,12},{10,... | collective-permute-start | bytes 786440 | tf_op jit(solution)/shard_map/ppermute | solution.py:225
  712.6 40.1 %collective-permute-start.85 = (bf16[64,2048]{1,0:T(8,128)(2,1)}, bf16[64,2048]{1,0:T(8,128)(2,1)}, u32[]{:S(2)}, u32[]{:S(2)}) collective-permute-start(bf16[64,2048]{1,0:T(8,128)(2,1)} %get-tuple-element.312), channel_id=1, source_target_pairs={{0,14},{1,15},{2,12},{3,13},{4,10},{5,11},{6,8},{7,9},{8,6},{9,7},... | collective-permute-start | bytes 786440 | tf_op jit(solution)/shard_map/ppermute | solution.py:225
  730.2 40.2 %collective-permute-start.88 = (bf16[64,2048]{1,0:T(8,128)(2,1)}, bf16[64,2048]{1,0:T(8,128)(2,1)}, u32[]{:S(2)}, u32[]{:S(2)}) collective-permute-start(bf16[64,2048]{1,0:T(8,128)(2,1)} %get-tuple-element.315), channel_id=1, source_target_pairs={{0,7},{1,6},{2,5},{3,4},{4,3},{5,2},{6,1},{7,0},{8,15},{9,14},{10,... | collective-permute-start | bytes 786440 | tf_op jit(solution)/shard_map/ppermute | solution.py:225
  796.1 39.4 %collective-permute-start.144 = (bf16[64,2048]{1,0:T(8,128)(2,1)}, bf16[64,2048]{1,0:T(8,128)(2,1)S(1)}, u32[]{:S(2)}, u32[]{:S(2)}) collective-permute-start(bf16[64,2048]{1,0:T(8,128)(2,1)} %get-tuple-element.381), channel_id=1, source_target_pairs={{0,6},{1,7},{2,4},{3,5},{4,2},{5,3},{6,0},{7,1},{8,14},{9,15},{10,... | collective-permute-start | bytes 786440 | tf_op jit(solution)/shard_map/ppermute | solution.py:225
  846.2 49.3 %collective-permute-start.46 = (bf16[64,2048]{1,0:T(8,128)(2,1)}, bf16[64,2048]{1,0:T(8,128)(2,1)}, u32[]{:S(2)}, u32[]{:S(2)}) collective-permute-start(bf16[64,2048]{1,0:T(8,128)(2,1)} %get-tuple-element.272), channel_id=1, source_target_pairs={{0,4},{1,5},{2,6},{3,7},{4,0},{5,1},{6,2},{7,3},{8,12},{9,13},{10,... | collective-permute-start | bytes 786440 | tf_op jit(solution)/shard_map/ppermute | solution.py:225
  857.0 38.6 %collective-permute-start.47 = (bf16[64,2048]{1,0:T(8,128)(2,1)}, bf16[64,2048]{1,0:T(8,128)(2,1)}, u32[]{:S(2)}, u32[]{:S(2)}) collective-permute-start(bf16[64,2048]{1,0:T(8,128)(2,1)} %get-tuple-element.273), channel_id=1, source_target_pairs={{0,12},{1,13},{2,14},{3,15},{4,8},{5,9},{6,10},{7,11},{8,4},{9,5},... | collective-permute-start | bytes 786440 | tf_op jit(solution)/shard_map/ppermute | solution.py:225
  877.6 40.8 %collective-permute-start.50 = (bf16[64,2048]{1,0:T(8,128)(2,1)}, bf16[64,2048]{1,0:T(8,128)(2,1)S(1)}, u32[]{:S(2)}, u32[]{:S(2)}) collective-permute-start(bf16[64,2048]{1,0:T(8,128)(2,1)} %get-tuple-element.276), channel_id=1, source_target_pairs={{0,5},{1,4},{2,7},{3,6},{4,1},{5,0},{6,3},{7,2},{8,13},{9,12},{10,... | collective-permute-start | bytes 786440 | tf_op jit(solution)/shard_map/ppermute | solution.py:225
  923.2 46.2 %collective-permute-start.59 = (bf16[64,2048]{1,0:T(8,128)(2,1)S(1)}, bf16[64,2048]{1,0:T(8,128)(2,1)S(1)}, u32[]{:S(2)}, u32[]{:S(2)}) collective-permute-start(bf16[64,2048]{1,0:T(8,128)(2,1)S(1)} %copy-done.134), channel_id=1, source_target_pairs={{0,15},{1,14},{2,13},{3,12},{4,11},{5,10},{6,9},{7,8},{8,7},{9,6},... | collective-permute-start | bytes 786440 | tf_op jit(solution)/shard_map/ppermute | solution.py:225
  1016.0 40.9 %collective-permute-start.179 = (bf16[64,2048]{1,0:T(8,128)(2,1)S(1)}, bf16[64,2048]{1,0:T(8,128)(2,1)S(1)}, u32[]{:S(2)}, u32[]{:S(2)}) collective-permute-start(bf16[64,2048]{1,0:T(8,128)(2,1)S(1)} %copy-done.130), channel_id=1, source_target_pairs={{0,15},{1,14},{2,13},{3,12},{4,11},{5,10},{6,9},{7,8},{8,7},{9,6},... | collective-permute-start | bytes 786440 | tf_op jit(solution)/shard_map/ppermute | solution.py:225
  1098.7 42.5 %collective-permute-start.160 = (bf16[64,2048]{1,0:T(8,128)(2,1)}, bf16[64,2048]{1,0:T(8,128)(2,1)S(1)}, u32[]{:S(2)}, u32[]{:S(2)}) collective-permute-start(bf16[64,2048]{1,0:T(8,128)(2,1)} %get-tuple-element.399), channel_id=1, source_target_pairs={{0,14},{1,15},{2,12},{3,13},{4,10},{5,11},{6,8},{7,9},{8,6},{9,7},... | collective-permute-start | bytes 786440 | tf_op jit(solution)/shard_map/ppermute | solution.py:225
  1098.8 43.9 %collective-permute-start.161 = (bf16[64,2048]{1,0:T(8,128)(2,1)}, bf16[64,2048]{1,0:T(8,128)(2,1)S(1)}, u32[]{:S(2)}, u32[]{:S(2)}) collective-permute-start(bf16[64,2048]{1,0:T(8,128)(2,1)} %get-tuple-element.400), channel_id=1, source_target_pairs={{0,3},{1,2},{2,1},{3,0},{4,7},{5,6},{6,5},{7,4},{8,11},{9,10},{10,... | collective-permute-start | bytes 786440 | tf_op jit(solution)/shard_map/ppermute | solution.py:225
  1103.2 39.5 %collective-permute-start.162 = (bf16[64,2048]{1,0:T(8,128)(2,1)}, bf16[64,2048]{1,0:T(8,128)(2,1)S(1)}, u32[]{:S(2)}, u32[]{:S(2)}) collective-permute-start(bf16[64,2048]{1,0:T(8,128)(2,1)} %get-tuple-element.401), channel_id=1, source_target_pairs={{0,11},{1,10},{2,9},{3,8},{4,15},{5,14},{6,13},{7,12},{8,3},{9,2},... | collective-permute-start | bytes 786440 | tf_op jit(solution)/shard_map/ppermute | solution.py:225
  1103.7 39.0 %collective-permute-start.163 = (bf16[64,2048]{1,0:T(8,128)(2,1)}, bf16[64,2048]{1,0:T(8,128)(2,1)}, u32[]{:S(2)}, u32[]{:S(2)}) collective-permute-start(bf16[64,2048]{1,0:T(8,128)(2,1)} %get-tuple-element.402), channel_id=1, source_target_pairs={{0,7},{1,6},{2,5},{3,4},{4,3},{5,2},{6,1},{7,0},{8,15},{9,14},{10,... | collective-permute-start | bytes 786440 | tf_op jit(solution)/shard_map/ppermute | solution.py:225
  (291 other events, 12605.3 us)

commit v5 on v4

--- a/solution.py
+++ b/solution.py
@@ -9,10 +9,10 @@
 from jax.sharding import PartitionSpec as P
 
 keep_rate = 0.9
-CHUNKS = 6
+CHUNKS = 4
 TILE = 512
 VMEM_LIMIT = 60 * 1024 * 1024
-FIRST_LAG = 4
+FIRST_LAG = 3
 SECOND_LAG = 2
 ANY = pl.BlockSpec(memory_space=pl.ANY)
 NT = (((1,), (1,)), ((), ()))

time: 1180 us -> 1180 us (level)
  Pallas kernels: 235 us -> 214 us
  waiting for transfers between devices: 440 us -> 455 us
    pallas_call x18 -> x12, Pallas kernels: 235 us -> 214 us  [call(): pl.pallas_call(body, out_shape=outs, grid=(plan.steps,), in_specs=in_spec...]
    ppermute x180 -> x120, waiting for transfers between devices: 435 us -> 451 us  [exchange(): lax.ppermute(part, 'blk', [(i, i ^ hop) for i in range(plan.devices)])]
    ppermute x180 -> x120, starting transfers between devices: 470 us -> 467 us  [exchange(): lax.ppermute(part, 'blk', [(i, i ^ hop) for i in range(plan.devices)])]
  transfers between devices with their start and end apart: 182 -> 122, of which waited for: 52 -> 41; matrix products, arithmetic and copies ran while one was open for 1% -> 1% of each run, Pallas kernels for 19% -> 17%
where the time goes in v5:
time: 1180 us; the launch traced here: 1170 us
  starting transfers between devices  475 us (40%)
  waiting for transfers between devices  455 us (39%)
  Pallas kernels  214 us (18%)
  local copies, waits for them, and re-layouts  14.6 us (1%)
    ppermute x120, starting transfers between devices, exchange(): lax.ppermute(part, 'blk', [(i, i ^ hop) for i in range(plan.devices)])  467 us
    ppermute x120, waiting for transfers between devices, exchange(): lax.ppermute(part, 'blk', [(i, i ^ hop) for i in range(plan.devices)])  451 us
    pallas_call x12, Pallas kernels, call(): pl.pallas_call(body, out_shape=outs, grid=(plan.steps,), in_specs=in_spec...  214 us
  transfers between devices with their start and end apart: 122, of which 41 were waited for; matrix products, arithmetic and copies ran while one was open for 1% of the time, Pallas kernels for 17%

profile of v5, /device:TPU:16, one launch (start us, length us, event | category | flops | bytes accessed | tf_op | source)
XLA Modules:
  0.0 1169.4 jit_solution(8428795883044512648)
XLA Ops:
  43.0 46.1 %collective-permute-done.10.refs_11_ = bf16[64,3072]{1,0:T(8,128)(2,1)S(1)} collective-permute-done((bf16[64,3072]{1,0:T(8,128)(2,1)}, bf16[64,3072]{1,0:T(8,128)(2,1)S(1)}, u32[]{:S(2)}, u32[]{:S(2)}) %collective-permute-start.10) | collective-permute-done | bytes 393248 | tf_op jit(solution)/shard_map/ppermute | solution.py:225
  98.7 15.6 %collective-permute-done.14.refs_15_ = bf16[64,3072]{1,0:T(8,128)(2,1)S(1)} collective-permute-done((bf16[64,3072]{1,0:T(8,128)(2,1)}, bf16[64,3072]{1,0:T(8,128)(2,1)S(1)}, u32[]{:S(2)}, u32[]{:S(2)}) %collective-permute-start.14) | collective-permute-done | bytes 393248 | tf_op jit(solution)/shard_map/ppermute | solution.py:225
  114.2 16.9 %collective-permute-done.2.refs_3_ = bf16[64,3072]{1,0:T(8,128)(2,1)} collective-permute-done((bf16[64,3072]{1,0:T(8,128)(2,1)}, bf16[64,3072]{1,0:T(8,128)(2,1)}, u32[]{:S(2)}, u32[]{:S(2)}) %collective-permute-start.2) | collective-permute-done | bytes 393248 | tf_op jit(solution)/shard_map/ppermute | solution.py:225
  178.0 21.6 %collective-permute-start.65 = (bf16[64,3072]{1,0:T(8,128)(2,1)}, bf16[64,3072]{1,0:T(8,128)(2,1)}, u32[]{:S(2)}, u32[]{:S(2)}) collective-permute-start(bf16[64,3072]{1,0:T(8,128)(2,1)} %get-tuple-element.218), channel_id=1, source_target_pairs={{0,5},{1,4},{2,7},{3,6},{4,1},{5,0},{6,3},{7,2},{8,13},{9,12},{10,... | collective-permute-start | bytes 1179656 | tf_op jit(solution)/shard_map/ppermute | solution.py:225
  207.9 20.6 %collective-permute-done.64.refs_5_ = bf16[64,3072]{1,0:T(8,128)(2,1)} collective-permute-done((bf16[64,3072]{1,0:T(8,128)(2,1)}, bf16[64,3072]{1,0:T(8,128)(2,1)}, u32[]{:S(2)}, u32[]{:S(2)}) %collective-permute-start.64) | collective-permute-done | bytes 393248 | tf_op jit(solution)/shard_map/ppermute | solution.py:225
  241.4 21.0 %collective-permute-done.68.refs_9_ = bf16[64,3072]{1,0:T(8,128)(2,1)} collective-permute-done((bf16[64,3072]{1,0:T(8,128)(2,1)}, bf16[64,3072]{1,0:T(8,128)(2,1)}, u32[]{:S(2)}, u32[]{:S(2)}) %collective-permute-start.68) | collective-permute-done | bytes 393248 | tf_op jit(solution)/shard_map/ppermute | solution.py:225
  284.4 20.2 %collective-permute-start.47 = (bf16[64,3072]{1,0:T(8,128)(2,1)}, bf16[64,3072]{1,0:T(8,128)(2,1)S(1)}, u32[]{:S(2)}, u32[]{:S(2)}) collective-permute-start(bf16[64,3072]{1,0:T(8,128)(2,1)} %get-tuple-element.199), channel_id=1, source_target_pairs={{0,12},{1,13},{2,14},{3,15},{4,8},{5,9},{6,10},{7,11},{8,4},{9,5},... | collective-permute-start | bytes 1179656 | tf_op jit(solution)/shard_map/ppermute | solution.py:225
  305.4 15.4 %collective-permute-done.74.refs_15_ = bf16[64,3072]{1,0:T(8,128)(2,1)S(1)} collective-permute-done((bf16[64,3072]{1,0:T(8,128)(2,1)}, bf16[64,3072]{1,0:T(8,128)(2,1)S(1)}, u32[]{:S(2)}, u32[]{:S(2)}) %collective-permute-start.74) | collective-permute-done | bytes 393248 | tf_op jit(solution)/shard_map/ppermute | solution.py:225
  346.8 19.5 %collective-permute-done.49.refs_5_ = bf16[64,3072]{1,0:T(8,128)(2,1)S(1)} collective-permute-done((bf16[64,3072]{1,0:T(8,128)(2,1)}, bf16[64,3072]{1,0:T(8,128)(2,1)S(1)}, u32[]{:S(2)}, u32[]{:S(2)}) %collective-permute-start.49) | collective-permute-done | bytes 393248 | tf_op jit(solution)/shard_map/ppermute | solution.py:225
  380.4 19.7 %collective-permute-done.53.refs_9_ = bf16[64,3072]{1,0:T(8,128)(2,1)} collective-permute-done((bf16[64,3072]{1,0:T(8,128)(2,1)}, bf16[64,3072]{1,0:T(8,128)(2,1)}, u32[]{:S(2)}, u32[]{:S(2)}) %collective-permute-start.53) | collective-permute-done | bytes 393248 | tf_op jit(solution)/shard_map/ppermute | solution.py:225
  407.4 19.6 %shard_map.112 = (bf16[64,3072]{1,0:T(8,128)(2,1)}, bf16[64,3072]{1,0:T(8,128)(2,1)}, bf16[64,3072]{1,0:T(8,128)(2,1)}, bf16[64,3072]{1,0:T(8,128)(2,1)}, bf16[6...) custom-call(bf16[64,3072]{1,0:T(8,128)(2,1)} %get-tuple-element.149., ...), custom_call_target="tpu_custom_call" | custom-call | flops 19327352832 | bytes 25165824 | tf_op jit(solution)/shard_map/pallas_call | solution.py:70
  443.5 16.0 %collective-permute-done.59.refs_15_ = bf16[64,3072]{1,0:T(8,128)(2,1)} collective-permute-done((bf16[64,3072]{1,0:T(8,128)(2,1)}, bf16[64,3072]{1,0:T(8,128)(2,1)}, u32[]{:S(2)}, u32[]{:S(2)}) %collective-permute-start.59) | collective-permute-done | bytes 393248 | tf_op jit(solution)/shard_map/ppermute | solution.py:225
  460.6 17.9 %collective-permute-start.20 = (bf16[64,3072]{1,0:T(8,128)(2,1)}, bf16[64,3072]{1,0:T(8,128)(2,1)S(1)}, u32[]{:S(2)}, u32[]{:S(2)}) collective-permute-start(bf16[64,3072]{1,0:T(8,128)(2,1)} %get-tuple-element.170), channel_id=1, source_target_pairs={{0,5},{1,4},{2,7},{3,6},{4,1},{5,0},{6,3},{7,2},{8,13},{9,12},{10,... | collective-permute-start | bytes 1179656 | tf_op jit(solution)/shard_map/ppermute | solution.py:225
  486.2 25.4 %collective-permute-start.24 = (bf16[64,3072]{1,0:T(8,128)(2,1)}, bf16[64,3072]{1,0:T(8,128)(2,1)S(1)}, u32[]{:S(2)}, u32[]{:S(2)}) collective-permute-start(bf16[64,3072]{1,0:T(8,128)(2,1)} %get-tuple-element.174), channel_id=1, source_target_pairs={{0,6},{1,7},{2,4},{3,5},{4,2},{5,3},{6,0},{7,1},{8,14},{9,15},{10,... | collective-permute-start | bytes 1179656 | tf_op jit(solution)/shard_map/ppermute | solution.py:225
  519.8 27.1 %collective-permute-start.28 = (bf16[64,3072]{1,0:T(8,128)(2,1)}, bf16[64,3072]{1,0:T(8,128)(2,1)}, u32[]{:S(2)}, u32[]{:S(2)}) collective-permute-start(bf16[64,3072]{1,0:T(8,128)(2,1)} %get-tuple-element.178), channel_id=1, source_target_pairs={{0,7},{1,6},{2,5},{3,4},{4,3},{5,2},{6,1},{7,0},{8,15},{9,14},{10,... | collective-permute-start | bytes 1179656 | tf_op jit(solution)/shard_map/ppermute | solution.py:225
  546.9 20.3 %shard_map.116 = (bf16[64,3072]{1,0:T(8,128)(2,1)}, bf16[64,3072]{1,0:T(8,128)(2,1)}, bf16[64,3072]{1,0:T(8,128)(2,1)}, bf16[64,3072]{1,0:T(8,128)(2,1)}, bf16[6...) custom-call(bf16[64,3072]{1,0:T(8,128)(2,1)} %get-tuple-element.212., ...), custom_call_target="tpu_custom_call", output_to_operand_aliasing={{16}: (21, {}), {17}: (22, {})} | custom-call | flops 19327352832 | bytes 25165824 | tf_op jit(solution)/shard_map/pallas_call | solution.py:70
  597.4 20.0 %collective-permute-start.80 = (bf16[64,3072]{1,0:T(8,128)(2,1)}, bf16[64,3072]{1,0:T(8,128)(2,1)S(1)}, u32[]{:S(2)}, u32[]{:S(2)}) collective-permute-start(bf16[64,3072]{1,0:T(8,128)(2,1)} %get-tuple-element.239), channel_id=1, source_target_pairs={{0,5},{1,4},{2,7},{3,6},{4,1},{5,0},{6,3},{7,2},{8,13},{9,12},{10,... | collective-permute-start | bytes 1179656 | tf_op jit(solution)/shard_map/ppermute | solution.py:225
  624.9 24.4 %collective-permute-start.84 = (bf16[64,3072]{1,0:T(8,128)(2,1)}, bf16[64,3072]{1,0:T(8,128)(2,1)}, u32[]{:S(2)}, u32[]{:S(2)}) collective-permute-start(bf16[64,3072]{1,0:T(8,128)(2,1)} %get-tuple-element.243), channel_id=1, source_target_pairs={{0,6},{1,7},{2,4},{3,5},{4,2},{5,3},{6,0},{7,1},{8,14},{9,15},{10,... | collective-permute-start | bytes 1179656 | tf_op jit(solution)/shard_map/ppermute | solution.py:225
  659.5 26.2 %collective-permute-start.88 = (bf16[64,3072]{1,0:T(8,128)(2,1)}, bf16[64,3072]{1,0:T(8,128)(2,1)}, u32[]{:S(2)}, u32[]{:S(2)}) collective-permute-start(bf16[64,3072]{1,0:T(8,128)(2,1)} %get-tuple-element.247), channel_id=1, source_target_pairs={{0,7},{1,6},{2,5},{3,4},{4,3},{5,2},{6,1},{7,0},{8,15},{9,14},{10,... | collective-permute-start | bytes 1179656 | tf_op jit(solution)/shard_map/ppermute | solution.py:225
  699.0 15.3 %collective-permute-start.31 = (bf16[64,3072]{1,0:T(8,128)(2,1)}, bf16[64,3072]{1,0:T(8,128)(2,1)}, u32[]{:S(2)}, u32[]{:S(2)}) collective-permute-start(bf16[64,3072]{1,0:T(8,128)(2,1)} %get-tuple-element.182), channel_id=1, source_target_pairs={{0,4},{1,5},{2,6},{3,7},{4,0},{5,1},{6,2},{7,3},{8,12},{9,13},{10,... | collective-permute-start | bytes 1179656 | tf_op jit(solution)/shard_map/ppermute | solution.py:225
  725.1 30.9 %collective-permute-start.35 = (bf16[64,3072]{1,0:T(8,128)(2,1)}, bf16[64,3072]{1,0:T(8,128)(2,1)}, u32[]{:S(2)}, u32[]{:S(2)}) collective-permute-start(bf16[64,3072]{1,0:T(8,128)(2,1)} %get-tuple-element.186), channel_id=1, source_target_pairs={{0,5},{1,4},{2,7},{3,6},{4,1},{5,0},{6,3},{7,2},{8,13},{9,12},{10,... | collective-permute-start | bytes 1179656 | tf_op jit(solution)/shard_map/ppermute | solution.py:225
  776.6 28.8 %collective-permute-done.36.refs_7_ = bf16[64,3072]{1,0:T(8,128)(2,1)} collective-permute-done((bf16[64,3072]{1,0:T(8,128)(2,1)}, bf16[64,3072]{1,0:T(8,128)(2,1)}, u32[]{:S(2)}, u32[]{:S(2)}) %collective-permute-start.36) | collective-permute-done | bytes 393248 | tf_op jit(solution)/shard_map/ppermute | solution.py:225
  805.4 18.9 %collective-permute-start.43 = (bf16[64,3072]{1,0:T(8,128)(2,1)}, bf16[64,3072]{1,0:T(8,128)(2,1)}, u32[]{:S(2)}, u32[]{:S(2)}) collective-permute-start(bf16[64,3072]{1,0:T(8,128)(2,1)} %get-tuple-element.194), channel_id=1, source_target_pairs={{0,7},{1,6},{2,5},{3,4},{4,3},{5,2},{6,1},{7,0},{8,15},{9,14},{10,... | collective-permute-start | bytes 1179656 | tf_op jit(solution)/shard_map/ppermute | solution.py:225
  824.4 20.0 %shard_map.117 = (bf16[64,3072]{1,0:T(8,128)(2,1)}, bf16[64,3072]{1,0:T(8,128)(2,1)}, bf16[64,3072]{1,0:T(8,128)(2,1)}, bf16[64,3072]{1,0:T(8,128)(2,1)}, bf16[6...) custom-call(bf16[64,3072]{1,0:T(8,128)(2,1)} %get-tuple-element.196., ...), custom_call_target="tpu_custom_call", output_to_operand_aliasing={{16}: (21, {}), {17}: (22, {})} | custom-call | flops 19327352832 | bytes 25165824 | tf_op jit(solution)/shard_map/pallas_call | solution.py:70
  864.0 29.4 %collective-permute-start.110 = (bf16[64,3072]{1,0:T(8,128)(2,1)}, bf16[64,3072]{1,0:T(8,128)(2,1)S(1)}, u32[]{:S(2)}, u32[]{:S(2)}) collective-permute-start(bf16[64,3072]{1,0:T(8,128)(2,1)} %get-tuple-element.272), channel_id=1, source_target_pairs={{0,5},{1,4},{2,7},{3,6},{4,1},{5,0},{6,3},{7,2},{8,13},{9,12},{10,... | collective-permute-start | bytes 1179656 | tf_op jit(solution)/shard_map/ppermute | solution.py:225
  904.9 22.5 %shard_map.119 = (bf16[12288,1024]{1,0:T(8,128)(2,1)}, f32[8,128,128]{2,1,0:T(8,128)}) custom-call(bf16[64,3072]{1,0:T(8,128)(2,1)} %get-tuple-element.283.refs_0_, bf16[64,3072]{1,0:T(8,128)(2,1)} %copy-done.2, bf16[64,3072]{1,0:T(8,128)(2,1)} %copy-done.3, bf16[64,3072]{1,0:T(8,128)(2,1)} %copy-done.4, bf16[64,3072]{1,0:T(8,128)(2,1)} %copy-done.5, ...), custom_call_target="tpu_custom_call" | custom-call | flops 12884901888 | bytes 102760448 | tf_op jit(solution)/shard_map/pallas_call | solution.py:70
  955.3 20.1 %shard_map.118 = (bf16[64,3072]{1,0:T(8,128)(2,1)}, bf16[64,3072]{1,0:T(8,128)(2,1)}, bf16[64,3072]{1,0:T(8,128)(2,1)}, bf16[64,3072]{1,0:T(8,128)(2,1)}, bf16[6...) custom-call(bf16[64,3072]{1,0:T(8,128)(2,1)} %get-tuple-element.180., ...), custom_call_target="tpu_custom_call", output_to_operand_aliasing={{16}: (21, {}), {17}: (22, {})} | custom-call | flops 19327352832 | bytes 25165824 | tf_op jit(solution)/shard_map/pallas_call | solution.py:70
  989.1 17.3 %collective-permute-start.102 = (bf16[64,3072]{1,0:T(8,128)(2,1)}, bf16[64,3072]{1,0:T(8,128)(2,1)S(1)}, u32[]{:S(2)}, u32[]{:S(2)}) collective-permute-start(bf16[64,3072]{1,0:T(8,128)(2,1)} %get-tuple-element.263), channel_id=1, source_target_pairs={{0,11},{1,10},{2,9},{3,8},{4,15},{5,14},{6,13},{7,12},{8,3},{9,2},... | collective-permute-start | bytes 1179656 | tf_op jit(solution)/shard_map/ppermute | solution.py:225
  1008.1 22.5 %shard_map.120 = (bf16[12288,1024]{1,0:T(8,128)(2,1)}, f32[8,128,128]{2,1,0:T(8,128)}) custom-call(bf16[64,3072]{1,0:T(8,128)(2,1)} %get-tuple-element.282.refs_0_, bf16[64,3072]{1,0:T(8,128)(2,1)} %copy-done.12, bf16[64,3072]{1,0:T(8,128)(2,1)} %copy-done.13, bf16[64,3072]{1,0:T(8,128)(2,1)} %copy-done.14, ...), custom_call_target="tpu_custom_call", output_to_operand_aliasing={{0}: (19, {}), {1}: (20, {})} | custom-call | flops 12884901888 | bytes 102760448 | tf_op jit(solution)/shard_map/pallas_call | solution.py:70
  1051.7 16.6 %collective-permute-done.104.refs_15_ = bf16[64,3072]{1,0:T(8,128)(2,1)S(1)} collective-permute-done((bf16[64,3072]{1,0:T(8,128)(2,1)}, bf16[64,3072]{1,0:T(8,128)(2,1)S(1)}, u32[]{:S(2)}, u32[]{:S(2)}) %collective-permute-start.104) | collective-permute-done | bytes 393248 | tf_op jit(solution)/shard_map/ppermute | solution.py:225
  1068.2 22.7 %shard_map.121 = (bf16[12288,1024]{1,0:T(8,128)(2,1)}, f32[8,128,128]{2,1,0:T(8,128)}) custom-call(bf16[64,3072]{1,0:T(8,128)(2,1)} %get-tuple-element.266.refs_0_, bf16[64,3072]{1,0:T(8,128)(2,1)} %copy-done.34, bf16[64,3072]{1,0:T(8,128)(2,1)} %copy-done.35, bf16[64,3072]{1,0:T(8,128)(2,1)} %copy-done.36, ...), custom_call_target="tpu_custom_call", output_to_operand_aliasing={{0}: (19, {}), {1}: (20, {})} | custom-call | flops 12884901888 | bytes 102760448 | tf_op jit(solution)/shard_map/pallas_call | solution.py:70
  1133.0 22.5 %shard_map.122 = (bf16[12288,1024]{1,0:T(8,128)(2,1)}, f32[8,128,128]{2,1,0:T(8,128)}) custom-call(bf16[64,3072]{1,0:T(8,128)(2,1)} %get-tuple-element.250.refs_0_, bf16[64,3072]{1,0:T(8,128)(2,1)} %copy-done.53, bf16[64,3072]{1,0:T(8,128)(2,1)} %copy-done.54, ...), custom_call_target="tpu_custom_call", output_to_operand_aliasing={{0}: (19, {}), {1}: (20, {})} | custom-call | flops 12884901888 | bytes 102760448 | tf_op jit(solution)/shard_map/pallas_call | solution.py:70
  (403 shorter events, 466.3 us)
Async XLA Ops:
  21.3 67.8 %collective-permute-start.10 = (bf16[64,3072]{1,0:T(8,128)(2,1)}, bf16[64,3072]{1,0:T(8,128)(2,1)S(1)}, u32[]{:S(2)}, u32[]{:S(2)}) collective-permute-start(bf16[64,3072]{1,0:T(8,128)(2,1)} %get-tuple-element.160), channel_id=1, source_target_pairs={{0,14},{1,15},{2,12},{3,13},{4,10},{5,11},{6,8},{7,9},{8,6},{9,7},... | collective-permute-start | bytes 1179656 | tf_op jit(solution)/shard_map/ppermute | solution.py:225
  23.9 65.3 %collective-permute-start.11 = (bf16[64,3072]{1,0:T(8,128)(2,1)}, bf16[64,3072]{1,0:T(8,128)(2,1)S(1)}, u32[]{:S(2)}, u32[]{:S(2)}) collective-permute-start(bf16[64,3072]{1,0:T(8,128)(2,1)} %get-tuple-element.161), channel_id=1, source_target_pairs={{0,3},{1,2},{2,1},{3,0},{4,7},{5,6},{6,5},{7,4},{8,11},{9,10},{10,... | collective-permute-start | bytes 1179656 | tf_op jit(solution)/shard_map/ppermute | solution.py:225
  23.9 70.3 %collective-permute-start.12 = (bf16[64,3072]{1,0:T(8,128)(2,1)}, bf16[64,3072]{1,0:T(8,128)(2,1)S(1)}, u32[]{:S(2)}, u32[]{:S(2)}) collective-permute-start(bf16[64,3072]{1,0:T(8,128)(2,1)} %get-tuple-element.162), channel_id=1, source_target_pairs={{0,11},{1,10},{2,9},{3,8},{4,15},{5,14},{6,13},{7,12},{8,3},{9,2},... | collective-permute-start | bytes 1179656 | tf_op jit(solution)/shard_map/ppermute | solution.py:225
  38.1 59.8 %collective-permute-start.13 = (bf16[64,3072]{1,0:T(8,128)(2,1)}, bf16[64,3072]{1,0:T(8,128)(2,1)S(1)}, u32[]{:S(2)}, u32[]{:S(2)}) collective-permute-start(bf16[64,3072]{1,0:T(8,128)(2,1)} %get-tuple-element.163), channel_id=1, source_target_pairs={{0,7},{1,6},{2,5},{3,4},{4,3},{5,2},{6,1},{7,0},{8,15},{9,14},{10,... | collective-permute-start | bytes 1179656 | tf_op jit(solution)/shard_map/ppermute | solution.py:225
  42.9 71.4 %collective-permute-start.14 = (bf16[64,3072]{1,0:T(8,128)(2,1)}, bf16[64,3072]{1,0:T(8,128)(2,1)S(1)}, u32[]{:S(2)}, u32[]{:S(2)}) collective-permute-start(bf16[64,3072]{1,0:T(8,128)(2,1)} %get-tuple-element.164), channel_id=1, source_target_pairs={{0,15},{1,14},{2,13},{3,12},{4,11},{5,10},{6,9},{7,8},{8,7},{9,6},... | collective-permute-start | bytes 1179656 | tf_op jit(solution)/shard_map/ppermute | solution.py:225
  97.9 62.4 %collective-permute-start.5 = (bf16[64,3072]{1,0:T(8,128)(2,1)}, bf16[64,3072]{1,0:T(8,128)(2,1)S(1)}, u32[]{:S(2)}, u32[]{:S(2)}) collective-permute-start(bf16[64,3072]{1,0:T(8,128)(2,1)} %get-tuple-element.155), channel_id=1, source_target_pairs={{0,5},{1,4},{2,7},{3,6},{4,1},{5,0},{6,3},{7,2},{8,13},{9,12},{10,... | collective-permute-start | bytes 1179656 | tf_op jit(solution)/shard_map/ppermute | solution.py:225
  167.1 61.5 %collective-permute-start.64 = (bf16[64,3072]{1,0:T(8,128)(2,1)}, bf16[64,3072]{1,0:T(8,128)(2,1)}, u32[]{:S(2)}, u32[]{:S(2)}) collective-permute-start(bf16[64,3072]{1,0:T(8,128)(2,1)} %get-tuple-element.217), channel_id=1, source_target_pairs={{0,9},{1,8},{2,11},{3,10},{4,13},{5,12},{6,15},{7,14},{8,1},{9,0},... | collective-permute-start | bytes 1179656 | tf_op jit(solution)/shard_map/ppermute | solution.py:225
  178.0 55.9 %collective-permute-start.65 = (bf16[64,3072]{1,0:T(8,128)(2,1)}, bf16[64,3072]{1,0:T(8,128)(2,1)}, u32[]{:S(2)}, u32[]{:S(2)}) collective-permute-start(bf16[64,3072]{1,0:T(8,128)(2,1)} %get-tuple-element.218), channel_id=1, source_target_pairs={{0,5},{1,4},{2,7},{3,6},{4,1},{5,0},{6,3},{7,2},{8,13},{9,12},{10,... | collective-permute-start | bytes 1179656 | tf_op jit(solution)/shard_map/ppermute | solution.py:225
  207.9 54.4 %collective-permute-start.68 = (bf16[64,3072]{1,0:T(8,128)(2,1)}, bf16[64,3072]{1,0:T(8,128)(2,1)}, u32[]{:S(2)}, u32[]{:S(2)}) collective-permute-start(bf16[64,3072]{1,0:T(8,128)(2,1)} %get-tuple-element.221), channel_id=1, source_target_pairs={{0,10},{1,11},{2,8},{3,9},{4,14},{5,15},{6,12},{7,13},{8,2},{9,3},... | collective-permute-start | bytes 1179656 | tf_op jit(solution)/shard_map/ppermute | solution.py:225
  282.1 56.8 %collective-permute-start.46 = (bf16[64,3072]{1,0:T(8,128)(2,1)}, bf16[64,3072]{1,0:T(8,128)(2,1)S(1)}, u32[]{:S(2)}, u32[]{:S(2)}) collective-permute-start(bf16[64,3072]{1,0:T(8,128)(2,1)} %get-tuple-element.198), channel_id=1, source_target_pairs={{0,4},{1,5},{2,6},{3,7},{4,0},{5,1},{6,2},{7,3},{8,12},{9,13},{10,... | collective-permute-start | bytes 1179656 | tf_op jit(solution)/shard_map/ppermute | solution.py:225
  284.4 61.9 %collective-permute-start.47 = (bf16[64,3072]{1,0:T(8,128)(2,1)}, bf16[64,3072]{1,0:T(8,128)(2,1)S(1)}, u32[]{:S(2)}, u32[]{:S(2)}) collective-permute-start(bf16[64,3072]{1,0:T(8,128)(2,1)} %get-tuple-element.199), channel_id=1, source_target_pairs={{0,12},{1,13},{2,14},{3,15},{4,8},{5,9},{6,10},{7,11},{8,4},{9,5},... | collective-permute-start | bytes 1179656 | tf_op jit(solution)/shard_map/ppermute | solution.py:225
  346.8 53.3 %collective-permute-start.53 = (bf16[64,3072]{1,0:T(8,128)(2,1)}, bf16[64,3072]{1,0:T(8,128)(2,1)}, u32[]{:S(2)}, u32[]{:S(2)}) collective-permute-start(bf16[64,3072]{1,0:T(8,128)(2,1)} %get-tuple-element.205), channel_id=1, source_target_pairs={{0,10},{1,11},{2,8},{3,9},{4,14},{5,15},{6,12},{7,13},{8,2},{9,3},... | collective-permute-start | bytes 1179656 | tf_op jit(solution)/shard_map/ppermute | solution.py:225
  430.7 55.3 %collective-permute-start.17 = (bf16[64,3072]{1,0:T(8,128)(2,1)}, bf16[64,3072]{1,0:T(8,128)(2,1)S(1)}, u32[]{:S(2)}, u32[]{:S(2)}) collective-permute-start(bf16[64,3072]{1,0:T(8,128)(2,1)} %get-tuple-element.167), channel_id=1, source_target_pairs={{0,12},{1,13},{2,14},{3,15},{4,8},{5,9},{6,10},{7,11},{8,4},{9,5},... | collective-permute-start | bytes 1179656 | tf_op jit(solution)/shard_map/ppermute | solution.py:225
  486.2 60.8 %collective-permute-start.24 = (bf16[64,3072]{1,0:T(8,128)(2,1)}, bf16[64,3072]{1,0:T(8,128)(2,1)S(1)}, u32[]{:S(2)}, u32[]{:S(2)}) collective-permute-start(bf16[64,3072]{1,0:T(8,128)(2,1)} %get-tuple-element.174), channel_id=1, source_target_pairs={{0,6},{1,7},{2,4},{3,5},{4,2},{5,3},{6,0},{7,1},{8,14},{9,15},{10,... | collective-permute-start | bytes 1179656 | tf_op jit(solution)/shard_map/ppermute | solution.py:225
  511.5 55.8 %collective-permute-start.25 = (bf16[64,3072]{1,0:T(8,128)(2,1)}, bf16[64,3072]{1,0:T(8,128)(2,1)}, u32[]{:S(2)}, u32[]{:S(2)}) collective-permute-start(bf16[64,3072]{1,0:T(8,128)(2,1)} %get-tuple-element.175), channel_id=1, source_target_pairs={{0,14},{1,15},{2,12},{3,13},{4,10},{5,11},{6,8},{7,9},{8,6},{9,7},... | collective-permute-start | bytes 1179656 | tf_op jit(solution)/shard_map/ppermute | solution.py:225
  519.7 54.5 %collective-permute-start.27 = (bf16[64,3072]{1,0:T(8,128)(2,1)}, bf16[64,3072]{1,0:T(8,128)(2,1)}, u32[]{:S(2)}, u32[]{:S(2)}) collective-permute-start(bf16[64,3072]{1,0:T(8,128)(2,1)} %get-tuple-element.177), channel_id=1, source_target_pairs={{0,11},{1,10},{2,9},{3,8},{4,15},{5,14},{6,13},{7,12},{8,3},{9,2},... | collective-permute-start | bytes 1179656 | tf_op jit(solution)/shard_map/ppermute | solution.py:225
  519.8 62.5 %collective-permute-start.28 = (bf16[64,3072]{1,0:T(8,128)(2,1)}, bf16[64,3072]{1,0:T(8,128)(2,1)}, u32[]{:S(2)}, u32[]{:S(2)}) collective-permute-start(bf16[64,3072]{1,0:T(8,128)(2,1)} %get-tuple-element.178), channel_id=1, source_target_pairs={{0,7},{1,6},{2,5},{3,4},{4,3},{5,2},{6,1},{7,0},{8,15},{9,14},{10,... | collective-permute-start | bytes 1179656 | tf_op jit(solution)/shard_map/ppermute | solution.py:225
  624.9 60.8 %collective-permute-start.84 = (bf16[64,3072]{1,0:T(8,128)(2,1)}, bf16[64,3072]{1,0:T(8,128)(2,1)}, u32[]{:S(2)}, u32[]{:S(2)}) collective-permute-start(bf16[64,3072]{1,0:T(8,128)(2,1)} %get-tuple-element.243), channel_id=1, source_target_pairs={{0,6},{1,7},{2,4},{3,5},{4,2},{5,3},{6,0},{7,1},{8,14},{9,15},{10,... | collective-permute-start | bytes 1179656 | tf_op jit(solution)/shard_map/ppermute | solution.py:225
  659.4 54.9 %collective-permute-start.87 = (bf16[64,3072]{1,0:T(8,128)(2,1)}, bf16[64,3072]{1,0:T(8,128)(2,1)}, u32[]{:S(2)}, u32[]{:S(2)}) collective-permute-start(bf16[64,3072]{1,0:T(8,128)(2,1)} %get-tuple-element.246), channel_id=1, source_target_pairs={{0,11},{1,10},{2,9},{3,8},{4,15},{5,14},{6,13},{7,12},{8,3},{9,2},... | collective-permute-start | bytes 1179656 | tf_op jit(solution)/shard_map/ppermute | solution.py:225
  659.5 61.3 %collective-permute-start.88 = (bf16[64,3072]{1,0:T(8,128)(2,1)}, bf16[64,3072]{1,0:T(8,128)(2,1)}, u32[]{:S(2)}, u32[]{:S(2)}) collective-permute-start(bf16[64,3072]{1,0:T(8,128)(2,1)} %get-tuple-element.247), channel_id=1, source_target_pairs={{0,7},{1,6},{2,5},{3,4},{4,3},{5,2},{6,1},{7,0},{8,15},{9,14},{10,... | collective-permute-start | bytes 1179656 | tf_op jit(solution)/shard_map/ppermute | solution.py:225
  699.0 57.0 %collective-permute-start.31 = (bf16[64,3072]{1,0:T(8,128)(2,1)}, bf16[64,3072]{1,0:T(8,128)(2,1)}, u32[]{:S(2)}, u32[]{:S(2)}) collective-permute-start(bf16[64,3072]{1,0:T(8,128)(2,1)} %get-tuple-element.182), channel_id=1, source_target_pairs={{0,4},{1,5},{2,6},{3,7},{4,0},{5,1},{6,2},{7,3},{8,12},{9,13},{10,... | collective-permute-start | bytes 1179656 | tf_op jit(solution)/shard_map/ppermute | solution.py:225
  763.4 60.9 %collective-permute-start.39 = (bf16[64,3072]{1,0:T(8,128)(2,1)}, bf16[64,3072]{1,0:T(8,128)(2,1)}, u32[]{:S(2)}, u32[]{:S(2)}) collective-permute-start(bf16[64,3072]{1,0:T(8,128)(2,1)} %get-tuple-element.190), channel_id=1, source_target_pairs={{0,6},{1,7},{2,4},{3,5},{4,2},{5,3},{6,0},{7,1},{8,14},{9,15},{10,... | collective-permute-start | bytes 1179656 | tf_op jit(solution)/shard_map/ppermute | solution.py:225
  776.6 67.8 %collective-permute-start.40 = (bf16[64,3072]{1,0:T(8,128)(2,1)}, bf16[64,3072]{1,0:T(8,128)(2,1)S(1)}, u32[]{:S(2)}, u32[]{:S(2)}) collective-permute-start(bf16[64,3072]{1,0:T(8,128)(2,1)} %get-tuple-element.191), channel_id=1, source_target_pairs={{0,14},{1,15},{2,12},{3,13},{4,10},{5,11},{6,8},{7,9},{8,6},{9,7},... | collective-permute-start | bytes 1179656 | tf_op jit(solution)/shard_map/ppermute | solution.py:225
  805.4 52.8 %collective-permute-start.43 = (bf16[64,3072]{1,0:T(8,128)(2,1)}, bf16[64,3072]{1,0:T(8,128)(2,1)}, u32[]{:S(2)}, u32[]{:S(2)}) collective-permute-start(bf16[64,3072]{1,0:T(8,128)(2,1)} %get-tuple-element.194), channel_id=1, source_target_pairs={{0,7},{1,6},{2,5},{3,4},{4,3},{5,2},{6,1},{7,0},{8,15},{9,14},{10,... | collective-permute-start | bytes 1179656 | tf_op jit(solution)/shard_map/ppermute | solution.py:225
  864.0 63.5 %collective-permute-start.110 = (bf16[64,3072]{1,0:T(8,128)(2,1)}, bf16[64,3072]{1,0:T(8,128)(2,1)S(1)}, u32[]{:S(2)}, u32[]{:S(2)}) collective-permute-start(bf16[64,3072]{1,0:T(8,128)(2,1)} %get-tuple-element.272), channel_id=1, source_target_pairs={{0,5},{1,4},{2,7},{3,6},{4,1},{5,0},{6,3},{7,2},{8,13},{9,12},{10,... | collective-permute-start | bytes 1179656 | tf_op jit(solution)/shard_map/ppermute | solution.py:225
  900.9 54.4 %collective-permute-start.114 = (bf16[64,3072]{1,0:T(8,128)(2,1)}, bf16[64,3072]{1,0:T(8,128)(2,1)S(1)}, u32[]{:S(2)}, u32[]{:S(2)}) collective-permute-start(bf16[64,3072]{1,0:T(8,128)(2,1)} %get-tuple-element.276), channel_id=1, source_target_pairs={{0,6},{1,7},{2,4},{3,5},{4,2},{5,3},{6,0},{7,1},{8,14},{9,15},{10,... | collective-permute-start | bytes 1179656 | tf_op jit(solution)/shard_map/ppermute | solution.py:225
  952.9 53.4 %collective-permute-start.118 = (bf16[64,3072]{1,0:T(8,128)(2,1)}, bf16[64,3072]{1,0:T(8,128)(2,1)}, u32[]{:S(2)}, u32[]{:S(2)}) collective-permute-start(bf16[64,3072]{1,0:T(8,128)(2,1)} %get-tuple-element.280), channel_id=1, source_target_pairs={{0,7},{1,6},{2,5},{3,4},{4,3},{5,2},{6,1},{7,0},{8,15},{9,14},{10,... | collective-permute-start | bytes 1179656 | tf_op jit(solution)/shard_map/ppermute | solution.py:225
  975.5 55.2 %collective-permute-start.100 = (bf16[64,3072]{1,0:T(8,128)(2,1)}, bf16[64,3072]{1,0:T(8,128)(2,1)S(1)}, u32[]{:S(2)}, u32[]{:S(2)}) collective-permute-start(bf16[64,3072]{1,0:T(8,128)(2,1)} %get-tuple-element.261), channel_id=1, source_target_pairs={{0,14},{1,15},{2,12},{3,13},{4,10},{5,11},{6,8},{7,9},{8,6},{9,7},... | collective-permute-start | bytes 1179656 | tf_op jit(solution)/shard_map/ppermute | solution.py:225
  989.1 58.7 %collective-permute-start.102 = (bf16[64,3072]{1,0:T(8,128)(2,1)}, bf16[64,3072]{1,0:T(8,128)(2,1)S(1)}, u32[]{:S(2)}, u32[]{:S(2)}) collective-permute-start(bf16[64,3072]{1,0:T(8,128)(2,1)} %get-tuple-element.263), channel_id=1, source_target_pairs={{0,11},{1,10},{2,9},{3,8},{4,15},{5,14},{6,13},{7,12},{8,3},{9,2},... | collective-permute-start | bytes 1179656 | tf_op jit(solution)/shard_map/ppermute | solution.py:225
  1006.9 61.3 %collective-permute-start.104 = (bf16[64,3072]{1,0:T(8,128)(2,1)}, bf16[64,3072]{1,0:T(8,128)(2,1)S(1)}, u32[]{:S(2)}, u32[]{:S(2)}) collective-permute-start(bf16[64,3072]{1,0:T(8,128)(2,1)} %get-tuple-element.265), channel_id=1, source_target_pairs={{0,15},{1,14},{2,13},{3,12},{4,11},{5,10},{6,9},{7,8},{8,7},{9,6},... | collective-permute-start | bytes 1179656 | tf_op jit(solution)/shard_map/ppermute | solution.py:225
  1030.7 62.1 %collective-permute-start.90 = (bf16[64,3072]{1,0:T(8,128)(2,1)}, bf16[64,3072]{1,0:T(8,128)(2,1)S(1)}, u32[]{:S(2)}, u32[]{:S(2)}) collective-permute-start(bf16[64,3072]{1,0:T(8,128)(2,1)} %get-tuple-element.251), channel_id=1, source_target_pairs={{0,8},{1,9},{2,10},{3,11},{4,12},{5,13},{6,14},{7,15},{8,0},{9,1},... | collective-permute-start | bytes 1179656 | tf_op jit(solution)/shard_map/ppermute | solution.py:225
  1034.0 60.3 %collective-permute-start.91 = (bf16[64,3072]{1,0:T(8,128)(2,1)}, bf16[64,3072]{1,0:T(8,128)(2,1)S(1)}, u32[]{:S(2)}, u32[]{:S(2)}) collective-permute-start(bf16[64,3072]{1,0:T(8,128)(2,1)} %get-tuple-element.252), channel_id=1, source_target_pairs={{0,4},{1,5},{2,6},{3,7},{4,0},{5,1},{6,2},{7,3},{8,12},{9,13},{10,... | collective-permute-start | bytes 1179656 | tf_op jit(solution)/shard_map/ppermute | solution.py:225
  (159 other events, 9321.0 us)

commit v6 on v5

--- a/solution.py
+++ b/solution.py
@@ -1,3 +1,4 @@
+import copy
 import math
 
 import jax
@@ -9,10 +10,9 @@
 from jax.sharding import PartitionSpec as P
 
 keep_rate = 0.9
-CHUNKS = 4
+SHARES = (3,8,8,5)
 TILE = 512
 VMEM_LIMIT = 60 * 1024 * 1024
-FIRST_LAG = 3
 SECOND_LAG = 2
 ANY = pl.BlockSpec(memory_space=pl.ANY)
 NT = (((1,), (1,)), ((), ()))
@@ -39,13 +39,18 @@
         self.height = devices * own * own
         self.slot_height = self.height // self.slots
         self.width = own * order
-        self.chunks = CHUNKS
-        self.chunk = rows // self.chunks
-        self.tile = math.gcd(self.chunk, TILE)
-        self.steps = self.chunk // self.tile
-
-    def token_spec(self, chunk):
-        return pl.BlockSpec((self.tile, self.width), lambda i: (chunk * self.steps + i, 0))
+        self.chunks = len(SHARES)
+        self.tile = math.gcd(rows // sum(SHARES), TILE)
+
+    def part(self, chunk):
+        plan, unit = copy.copy(self), self.rows // sum(SHARES)
+        plan.chunk = SHARES[chunk] * unit
+        plan.steps = plan.chunk // plan.tile
+        plan.first = sum(SHARES[:chunk]) * unit // plan.tile
+        return plan
+
+    def token_spec(self):
+        return pl.BlockSpec((self.tile, self.width), lambda i: (self.first + i, 0))
 
     def slot_specs(self):
         return [pl.BlockSpec((self.slot_height, self.tile), lambda i: (0, i))] * self.slots
@@ -80,17 +85,17 @@
     )(*ins)
 
 
-def first_factor(plan, chunk, tokens, wide_left, after):
+def first_factor(plan, tokens, wide_left):
     def body(tokens_ref, left_ref, *refs):
         product = dot(left_ref[...], tokens_ref[...], NT).astype(jnp.bfloat16)
-        for slot, ref in enumerate(refs[len(after) :]):
+        for slot, ref in enumerate(refs):
             ref[...] = product[slot * plan.slot_height : (slot + 1) * plan.slot_height, :]
 
     return call(
         body,
         plan,
-        (tokens, wide_left, *after),
-        [plan.token_spec(chunk), whole(wide_left), *[ANY] * len(after)],
+        (tokens, wide_left),
+        [plan.token_spec(), whole(wide_left)],
         plan.slot_shapes(),
         plan.slot_specs(),
         {},
@@ -139,9 +144,9 @@
     ins = (*received, tokens, cotangent, keep_mask, spread, wide_right)
     in_specs = [
         *plan.slot_specs(),
-        plan.token_spec(chunk),
-        plan.token_spec(chunk),
-        pl.BlockSpec((plan.own, plan.tile), lambda i: (0, chunk * plan.steps + i)),
+        plan.token_spec(),
+        plan.token_spec(),
+        pl.BlockSpec((plan.own, plan.tile), lambda i: (0, plan.first + i)),
         whole(spread),
         whole(wide_right),
     ]
@@ -157,7 +162,7 @@
         jax.ShapeDtypeStruct(tokens.shape, jnp.bfloat16),
         jax.ShapeDtypeStruct((plan.pairs, plan.pair * plan.order, span), jnp.float32),
     ]
-    out_specs = [*plan.slot_specs(), plan.token_spec(chunk), whole(outs[-1])]
+    out_specs = [*plan.slot_specs(), plan.token_spec(), whole(outs[-1])]
     flops = 6 * plan.height * span * plan.chunk * 4
     result = call(body, plan, ins, in_specs, outs, out_specs, aliases, flops)
     return result[:slots], (result[slots], result[slots + 1])
@@ -195,7 +200,7 @@
                 total_ref[block] = part if chunk == 0 else part + refs[slots + 4][block]
 
     ins = (*received, tokens, cotangent, wide_left)
-    in_specs = [*plan.slot_specs(), plan.token_spec(chunk), plan.token_spec(chunk), whole(wide_left)]
+    in_specs = [*plan.slot_specs(), plan.token_spec(), plan.token_spec(), whole(wide_left)]
     aliases = {}
     if state is not None:
         aliases = {len(ins): 0, len(ins) + 1: 1}
@@ -205,7 +210,7 @@
         jax.ShapeDtypeStruct(tokens.shape, jnp.bfloat16),
         jax.ShapeDtypeStruct((own, order, order), jnp.float32),
     ]
-    out_specs = [plan.token_spec(chunk), whole(outs[1])]
+    out_specs = [plan.token_spec(), whole(outs[1])]
     return call(
         body,
         plan,
@@ -264,15 +269,16 @@
     forward, backward, state = [], [], None
     for step in range(plan.chunks + SECOND_LAG):
         if step < plan.chunks:
-            after = backward[step - FIRST_LAG][1:] if step >= FIRST_LAG else []
-            forward.append(exchange(plan, first_factor(plan, step, tokens, wide_left, after)))
+            part = plan.part(step)
+            forward.append(exchange(part, first_factor(part, tokens, wide_left)))
         chunk = step - SECOND_LAG
         if chunk >= 0:
             after = backward[chunk - SECOND_LAG][1:] if chunk >= SECOND_LAG else []
+            part = plan.part(chunk)
             sent, state = second_factor(
-                plan, chunk, forward[chunk], tokens, cotangent, keep_mask, spread, wide_right, state, after
+                part, chunk, forward[chunk], tokens, cotangent, keep_mask, spread, wide_right, state, after
             )
-            backward.append(exchange(plan, sent))
+            backward.append(exchange(part, sent))
     mixed, wide_total = state
 
     split_total = wide_total.reshape(pairs, devices, pair, own, pair, order)
@@ -282,7 +288,7 @@
 
     state = None
     for chunk in range(plan.chunks):
-        state = first_factor_back(plan, chunk, backward[chunk], tokens, cotangent, wide_left, state)
+        state = first_factor_back(plan.part(chunk), chunk, backward[chunk], tokens, cotangent, wide_left, state)
     grad_tokens, part_left = state
     part_left = jnp.take(part_left.astype(jnp.bfloat16).reshape(own, devices, own, order), place, axis=1)
     part_left = jnp.einsum(

time: 1180 us -> 1180 us (level)
  starting transfers between devices: 475 us -> 338 us
  waiting for transfers between devices: 455 us -> 586 us
    ppermute x120, starting transfers between devices: 467 us -> 335 us  [exchange(): lax.ppermute(part, 'blk', [(i, i ^ hop) for i in range(plan.devices)])]
    ppermute x120, waiting for transfers between devices: 451 us -> 582 us  [exchange(): lax.ppermute(part, 'blk', [(i, i ^ hop) for i in range(plan.devices)])]
  transfers between devices with their start and end apart: 122 -> 122, of which waited for: 41 -> 49; matrix products, arithmetic and copies ran while one was open for 1% -> 1% of each run, Pallas kernels for 17% -> 18%
where the time goes in v6:
time: 1180 us; the launch traced here: 1160 us
  waiting for transfers between devices  586 us (50%)
  starting transfers between devices  338 us (29%)
  Pallas kernels  213 us (18%)
  local copies, waits for them, and re-layouts  15.2 us (1%)
    ppermute x120, waiting for transfers between devices, exchange(): lax.ppermute(part, 'blk', [(i, i ^ hop) for i in range(plan.devices)])  582 us
    ppermute x120, starting transfers between devices, exchange(): lax.ppermute(part, 'blk', [(i, i ^ hop) for i in range(plan.devices)])  335 us
    pallas_call x12, Pallas kernels, call(): pl.pallas_call(body, out_shape=outs, grid=(plan.steps,), in_specs=in_spec...  213 us
  transfers between devices with their start and end apart: 122, of which 49 were waited for; matrix products, arithmetic and copies ran while one was open for 1% of the time, Pallas kernels for 18%

profile of v6, /device:TPU:16, one launch (start us, length us, event | category | flops | bytes accessed | tf_op | source)
XLA Modules:
  0.0 1164.4 jit_solution(15614332943530652699)
XLA Ops:
  98.8 17.6 %collective-permute-start.13 = (bf16[64,2560]{1,0:T(8,128)(2,1)}, bf16[64,2560]{1,0:T(8,128)(2,1)S(1)}, u32[]{:S(2)}, u32[]{:S(2)}) collective-permute-start(bf16[64,2560]{1,0:T(8,128)(2,1)} %get-tuple-element.163), channel_id=1, source_target_pairs={{0,7},{1,6},{2,5},{3,4},{4,3},{5,2},{6,1},{7,0},{8,15},{9,14},{10,... | collective-permute-start | bytes 983048 | tf_op jit(solution)/shard_map/ppermute | solution.py:230
  130.0 13.4 %collective-permute-done.12.refs_13_ = bf16[64,2560]{1,0:T(8,128)(2,1)S(1)} collective-permute-done((bf16[64,2560]{1,0:T(8,128)(2,1)}, bf16[64,2560]{1,0:T(8,128)(2,1)S(1)}, u32[]{:S(2)}, u32[]{:S(2)}) %collective-permute-start.12) | collective-permute-done | bytes 327712 | tf_op jit(solution)/shard_map/ppermute | solution.py:230
  143.5 14.8 %collective-permute-start.4 = (bf16[64,2560]{1,0:T(8,128)(2,1)}, bf16[64,2560]{1,0:T(8,128)(2,1)}, u32[]{:S(2)}, u32[]{:S(2)}) collective-permute-start(bf16[64,2560]{1,0:T(8,128)(2,1)} %get-tuple-element.154), channel_id=1, source_target_pairs={{0,9},{1,8},{2,11},{3,10},{4,13},{5,12},{6,15},{7,14},{8,1},{9,0},... | collective-permute-start | bytes 983048 | tf_op jit(solution)/shard_map/ppermute | solution.py:230
  255.6 13.4 %shard_map.113 = (bf16[64,4096]{1,0:T(8,128)(2,1)}, bf16[64,4096]{1,0:T(8,128)(2,1)}, bf16[64,4096]{1,0:T(8,128)(2,1)}, bf16[64,4096]{1,0:T(8,128)(2,1)}, bf16[6...) custom-call(bf16[12288,1024]{1,0:T(8,128)(2,1)} %refs_16_.15, ...), custom_call_target="tpu_custom_call" | custom-call | flops 8589934592 | bytes 33554432 | tf_op jit(solution)/shard_map/pallas_call | solution.py:75
  285.0 33.7 %collective-permute-done.30.refs_1_ = bf16[64,4096]{1,0:T(8,128)(2,1)} collective-permute-done((bf16[64,4096]{1,0:T(8,128)(2,1)}, bf16[64,4096]{1,0:T(8,128)(2,1)}, u32[]{:S(2)}, u32[]{:S(2)}) %collective-permute-start.30) | collective-permute-done | bytes 524320 | tf_op jit(solution)/shard_map/ppermute | solution.py:230
  322.4 18.7 %collective-permute-done.32.refs_3_ = bf16[64,4096]{1,0:T(8,128)(2,1)} collective-permute-done((bf16[64,4096]{1,0:T(8,128)(2,1)}, bf16[64,4096]{1,0:T(8,128)(2,1)}, u32[]{:S(2)}, u32[]{:S(2)}) %collective-permute-start.32) | collective-permute-done | bytes 524320 | tf_op jit(solution)/shard_map/ppermute | solution.py:230
  341.2 22.5 %collective-permute-done.34.refs_5_ = bf16[64,4096]{1,0:T(8,128)(2,1)} collective-permute-done((bf16[64,4096]{1,0:T(8,128)(2,1)}, bf16[64,4096]{1,0:T(8,128)(2,1)}, u32[]{:S(2)}, u32[]{:S(2)}) %collective-permute-start.34) | collective-permute-done | bytes 524320 | tf_op jit(solution)/shard_map/ppermute | solution.py:230
  376.0 32.6 %collective-permute-done.38.refs_9_ = bf16[64,4096]{1,0:T(8,128)(2,1)} collective-permute-done((bf16[64,4096]{1,0:T(8,128)(2,1)}, bf16[64,4096]{1,0:T(8,128)(2,1)}, u32[]{:S(2)}, u32[]{:S(2)}) %collective-permute-start.38) | collective-permute-done | bytes 524320 | tf_op jit(solution)/shard_map/ppermute | solution.py:230
  414.3 13.6 %shard_map.112 = (bf16[64,4096]{1,0:T(8,128)(2,1)}, bf16[64,4096]{1,0:T(8,128)(2,1)}, bf16[64,4096]{1,0:T(8,128)(2,1)}, bf16[64,4096]{1,0:T(8,128)(2,1)}, bf16[6...) custom-call(bf16[12288,1024]{1,0:T(8,128)(2,1)} %refs_16_.15, ...), custom_call_target="tpu_custom_call" | custom-call | flops 8589934592 | bytes 33554432 | tf_op jit(solution)/shard_map/pallas_call | solution.py:75
  433.5 26.6 %collective-permute-done.42.refs_13_ = bf16[64,4096]{1,0:T(8,128)(2,1)} collective-permute-done((bf16[64,4096]{1,0:T(8,128)(2,1)}, bf16[64,4096]{1,0:T(8,128)(2,1)}, u32[]{:S(2)}, u32[]{:S(2)}) %collective-permute-start.42) | collective-permute-done | bytes 524320 | tf_op jit(solution)/shard_map/ppermute | solution.py:230
  460.1 22.5 %collective-permute-done.44.refs_15_ = bf16[64,4096]{1,0:T(8,128)(2,1)} collective-permute-done((bf16[64,4096]{1,0:T(8,128)(2,1)}, bf16[64,4096]{1,0:T(8,128)(2,1)}, u32[]{:S(2)}, u32[]{:S(2)}) %collective-permute-start.44) | collective-permute-done | bytes 524320 | tf_op jit(solution)/shard_map/ppermute | solution.py:230
  482.6 22.5 %collective-permute-done.15.refs_1_ = bf16[64,4096]{1,0:T(8,128)(2,1)S(1)} collective-permute-done((bf16[64,4096]{1,0:T(8,128)(2,1)}, bf16[64,4096]{1,0:T(8,128)(2,1)S(1)}, u32[]{:S(2)}, u32[]{:S(2)}) %collective-permute-start.15) | collective-permute-done | bytes 524320 | tf_op jit(solution)/shard_map/ppermute | solution.py:230
  519.1 31.0 %collective-permute-done.19.refs_5_ = bf16[64,4096]{1,0:T(8,128)(2,1)} collective-permute-done((bf16[64,4096]{1,0:T(8,128)(2,1)}, bf16[64,4096]{1,0:T(8,128)(2,1)}, u32[]{:S(2)}, u32[]{:S(2)}) %collective-permute-start.19) | collective-permute-done | bytes 524320 | tf_op jit(solution)/shard_map/ppermute | solution.py:230
  563.5 31.6 %collective-permute-done.23.refs_9_ = bf16[64,4096]{1,0:T(8,128)(2,1)} collective-permute-done((bf16[64,4096]{1,0:T(8,128)(2,1)}, bf16[64,4096]{1,0:T(8,128)(2,1)}, u32[]{:S(2)}, u32[]{:S(2)}) %collective-permute-start.23) | collective-permute-done | bytes 524320 | tf_op jit(solution)/shard_map/ppermute | solution.py:230
  601.8 25.3 %shard_map.116 = (bf16[64,4096]{1,0:T(8,128)(2,1)}, bf16[64,4096]{1,0:T(8,128)(2,1)}, bf16[64,4096]{1,0:T(8,128)(2,1)}, bf16[64,4096]{1,0:T(8,128)(2,1)}, bf16[6...) custom-call(bf16[64,4096]{1,0:T(8,128)(2,1)} %get-tuple-element.181., ...), custom_call_target="tpu_custom_call", output_to_operand_aliasing={{16}: (21, {}), {17}: (22, {})} | custom-call | flops 25769803776 | bytes 33554432 | tf_op jit(solution)/shard_map/pallas_call | solution.py:75
  631.5 13.9 %collective-permute-done.27.refs_13_ = bf16[64,4096]{1,0:T(8,128)(2,1)S(1)} collective-permute-done((bf16[64,4096]{1,0:T(8,128)(2,1)}, bf16[64,4096]{1,0:T(8,128)(2,1)S(1)}, u32[]{:S(2)}, u32[]{:S(2)}) %collective-permute-start.27) | collective-permute-done | bytes 524320 | tf_op jit(solution)/shard_map/ppermute | solution.py:230
  646.2 21.6 %collective-permute-done.29.refs_15_ = bf16[64,4096]{1,0:T(8,128)(2,1)} collective-permute-done((bf16[64,4096]{1,0:T(8,128)(2,1)}, bf16[64,4096]{1,0:T(8,128)(2,1)}, u32[]{:S(2)}, u32[]{:S(2)}) %collective-permute-start.29) | collective-permute-done | bytes 524320 | tf_op jit(solution)/shard_map/ppermute | solution.py:230
  667.8 22.5 %collective-permute-done.75.refs_23_.refs_1_ = bf16[64,4096]{1,0:T(8,128)(2,1)S(1)} collective-permute-done((bf16[64,4096]{1,0:T(8,128)(2,1)}, bf16[64,4096]{1,0:T(8,128)(2,1)S(1)}, u32[]{:S(2)}, u32[]{:S(2)}) %collective-permute-start.75) | collective-permute-done | bytes 524320 | tf_op jit(solution)/shard_map/ppermute | solution.py:230
  706.1 29.2 %collective-permute-done.79.refs_27_.refs_5_ = bf16[64,4096]{1,0:T(8,128)(2,1)S(1)} collective-permute-done((bf16[64,4096]{1,0:T(8,128)(2,1)}, bf16[64,4096]{1,0:T(8,128)(2,1)S(1)}, u32[]{:S(2)}, u32[]{:S(2)}) %collective-permute-start.79) | collective-permute-done | bytes 524320 | tf_op jit(solution)/shard_map/ppermute | solution.py:230
  746.5 15.3 %collective-permute-start.86 = (bf16[64,4096]{1,0:T(8,128)(2,1)}, bf16[64,4096]{1,0:T(8,128)(2,1)}, u32[]{:S(2)}, u32[]{:S(2)}) collective-permute-start(bf16[64,4096]{1,0:T(8,128)(2,1)} %get-tuple-element.245), channel_id=1, source_target_pairs={{0,3},{1,2},{2,1},{3,0},{4,7},{5,6},{6,5},{7,4},{8,11},{9,10},{10,... | collective-permute-start | bytes 1572872 | tf_op jit(solution)/shard_map/ppermute | solution.py:230
  761.8 18.5 %collective-permute-done.83.refs_31_.refs_9_ = bf16[64,4096]{1,0:T(8,128)(2,1)} collective-permute-done((bf16[64,4096]{1,0:T(8,128)(2,1)}, bf16[64,4096]{1,0:T(8,128)(2,1)}, u32[]{:S(2)}, u32[]{:S(2)}) %collective-permute-start.83) | collective-permute-done | bytes 524320 | tf_op jit(solution)/shard_map/ppermute | solution.py:230
  788.8 25.3 %shard_map.117 = (bf16[64,4096]{1,0:T(8,128)(2,1)}, bf16[64,4096]{1,0:T(8,128)(2,1)}, bf16[64,4096]{1,0:T(8,128)(2,1)}, bf16[64,4096]{1,0:T(8,128)(2,1)}, bf16[6...) custom-call(bf16[64,4096]{1,0:T(8,128)(2,1)} %get-tuple-element.165., ...), custom_call_target="tpu_custom_call", output_to_operand_aliasing={{16}: (21, {}), {17}: (22, {})} | custom-call | flops 25769803776 | bytes 33554432 | tf_op jit(solution)/shard_map/pallas_call | solution.py:75
  829.0 22.5 %collective-permute-done.89.refs_37_.refs_15_ = bf16[64,4096]{1,0:T(8,128)(2,1)} collective-permute-done((bf16[64,4096]{1,0:T(8,128)(2,1)}, bf16[64,4096]{1,0:T(8,128)(2,1)}, u32[]{:S(2)}, u32[]{:S(2)}) %collective-permute-start.89) | collective-permute-done | bytes 524320 | tf_op jit(solution)/shard_map/ppermute | solution.py:230
  851.5 13.2 %shard_map.119 = (bf16[12288,1024]{1,0:T(8,128)(2,1)}, f32[8,128,128]{2,1,0:T(8,128)}) custom-call(bf16[64,1536]{1,0:T(8,128)(2,1)} %get-tuple-element.283.refs_0_, bf16[64,1536]{1,0:T(8,128)(2,1)} %copy-done.42, bf16[64,1536]{1,0:T(8,128)(2,1)} %copy-done.43, bf16[64,1536]{1,0:T(8,128)(2,1)} %copy-done.44, bf16[64,1536]{1,0:T(8,128)(2,1)} %copy-done.45, ...), custom_call_target="tpu_custom_call" | custom-call | flops 6442450944 | bytes 102760448 | tf_op jit(solution)/shard_map/pallas_call | solution.py:75
  864.8 21.0 %collective-permute-start.110 = (bf16[64,4096]{1,0:T(8,128)(2,1)}, bf16[64,4096]{1,0:T(8,128)(2,1)S(1)}, u32[]{:S(2)}, u32[]{:S(2)}) collective-permute-start(bf16[64,4096]{1,0:T(8,128)(2,1)} %get-tuple-element.272), channel_id=1, source_target_pairs={{0,5},{1,4},{2,7},{3,6},{4,1},{5,0},{6,3},{7,2},{8,13},{9,12},{10,... | collective-permute-start | bytes 1572872 | tf_op jit(solution)/shard_map/ppermute | solution.py:230
  896.7 28.8 %shard_map.120 = (bf16[12288,1024]{1,0:T(8,128)(2,1)}, f32[8,128,128]{2,1,0:T(8,128)}) custom-call(bf16[64,4096]{1,0:T(8,128)(2,1)} %get-tuple-element.282.refs_0_, bf16[64,4096]{1,0:T(8,128)(2,1)} %copy-done.2, bf16[64,4096]{1,0:T(8,128)(2,1)} %copy-done.3, bf16[64,4096]{1,0:T(8,128)(2,1)} %copy-done.4, ...), custom_call_target="tpu_custom_call", output_to_operand_aliasing={{0}: (19, {}), {1}: (20, {})} | custom-call | flops 17179869184 | bytes 102760448 | tf_op jit(solution)/shard_map/pallas_call | solution.py:75
  930.2 28.1 %collective-permute-start.116 = (bf16[64,4096]{1,0:T(8,128)(2,1)}, bf16[64,4096]{1,0:T(8,128)(2,1)S(1)}, u32[]{:S(2)}, u32[]{:S(2)}) collective-permute-start(bf16[64,4096]{1,0:T(8,128)(2,1)} %get-tuple-element.278), channel_id=1, source_target_pairs={{0,3},{1,2},{2,1},{3,0},{4,7},{5,6},{6,5},{7,4},{8,11},{9,10},{10,... | collective-permute-start | bytes 1572872 | tf_op jit(solution)/shard_map/ppermute | solution.py:230
  963.5 17.3 %shard_map.118 = (bf16[64,2560]{1,0:T(8,128)(2,1)}, bf16[64,2560]{1,0:T(8,128)(2,1)}, bf16[64,2560]{1,0:T(8,128)(2,1)}, bf16[64,2560]{1,0:T(8,128)(2,1)}, bf16[6...) custom-call(bf16[64,2560]{1,0:T(8,128)(2,1)} %get-tuple-element.149., ...), custom_call_target="tpu_custom_call", output_to_operand_aliasing={{16}: (21, {}), {17}: (22, {})} | custom-call | flops 16106127360 | bytes 20971520 | tf_op jit(solution)/shard_map/pallas_call | solution.py:75
  980.9 23.5 %collective-permute-done.116.refs_12_ = bf16[64,4096]{1,0:T(8,128)(2,1)S(1)} collective-permute-done((bf16[64,4096]{1,0:T(8,128)(2,1)}, bf16[64,4096]{1,0:T(8,128)(2,1)S(1)}, u32[]{:S(2)}, u32[]{:S(2)}) %collective-permute-start.116) | collective-permute-done | bytes 524320 | tf_op jit(solution)/shard_map/ppermute | solution.py:230
  1006.5 18.1 %collective-permute-start.102 = (bf16[64,2560]{1,0:T(8,128)(2,1)}, bf16[64,2560]{1,0:T(8,128)(2,1)S(1)}, u32[]{:S(2)}, u32[]{:S(2)}) collective-permute-start(bf16[64,2560]{1,0:T(8,128)(2,1)} %get-tuple-element.263), channel_id=1, source_target_pairs={{0,11},{1,10},{2,9},{3,8},{4,15},{5,14},{6,13},{7,12},{8,3},{9,2},... | collective-permute-start | bytes 983048 | tf_op jit(solution)/shard_map/ppermute | solution.py:230
  1026.7 29.0 %shard_map.121 = (bf16[12288,1024]{1,0:T(8,128)(2,1)}, f32[8,128,128]{2,1,0:T(8,128)}) custom-call(bf16[64,4096]{1,0:T(8,128)(2,1)} %get-tuple-element.266.refs_0_, bf16[64,4096]{1,0:T(8,128)(2,1)} %copy-done.9, bf16[64,4096]{1,0:T(8,128)(2,1)} %copy-done.10, bf16[64,4096]{1,0:T(8,128)(2,1)} %copy-done.11, ...), custom_call_target="tpu_custom_call", output_to_operand_aliasing={{0}: (19, {}), {1}: (20, {})} | custom-call | flops 17179869184 | bytes 102760448 | tf_op jit(solution)/shard_map/pallas_call | solution.py:75
  1133.7 19.4 %shard_map.122 = (bf16[12288,1024]{1,0:T(8,128)(2,1)}, f32[8,128,128]{2,1,0:T(8,128)}) custom-call(bf16[64,2560]{1,0:T(8,128)(2,1)} %get-tuple-element.250.refs_0_, bf16[64,2560]{1,0:T(8,128)(2,1)} %copy-done.37, bf16[64,2560]{1,0:T(8,128)(2,1)} %copy-done.38, bf16[64,2560]{1,0:T(8,128)(2,1)} %copy-done.39, ...), custom_call_target="tpu_custom_call", output_to_operand_aliasing={{0}: (19, {}), {1}: (20, {})} | custom-call | flops 10737418240 | bytes 102760448 | tf_op jit(solution)/shard_map/pallas_call | solution.py:75
  (405 shorter events, 454.9 us)
Async XLA Ops:
  272.6 68.5 %collective-permute-start.32 = (bf16[64,4096]{1,0:T(8,128)(2,1)}, bf16[64,4096]{1,0:T(8,128)(2,1)}, u32[]{:S(2)}, u32[]{:S(2)}) collective-permute-start(bf16[64,4096]{1,0:T(8,128)(2,1)} %get-tuple-element.184), channel_id=1, source_target_pairs={{0,12},{1,13},{2,14},{3,15},{4,8},{5,9},{6,10},{7,11},{8,4},{9,5},... | collective-permute-start | bytes 1572872 | tf_op jit(solution)/shard_map/ppermute | solution.py:230
  274.1 67.1 %collective-permute-start.33 = (bf16[64,4096]{1,0:T(8,128)(2,1)}, bf16[64,4096]{1,0:T(8,128)(2,1)}, u32[]{:S(2)}, u32[]{:S(2)}) collective-permute-start(bf16[64,4096]{1,0:T(8,128)(2,1)} %get-tuple-element.185), channel_id=1, source_target_pairs={{0,1},{1,0},{2,3},{3,2},{4,5},{5,4},{6,7},{7,6},{8,9},{9,8},{10,11... | collective-permute-start | bytes 1572872 | tf_op jit(solution)/shard_map/ppermute | solution.py:230
  285.0 78.7 %collective-permute-start.34 = (bf16[64,4096]{1,0:T(8,128)(2,1)}, bf16[64,4096]{1,0:T(8,128)(2,1)}, u32[]{:S(2)}, u32[]{:S(2)}) collective-permute-start(bf16[64,4096]{1,0:T(8,128)(2,1)} %get-tuple-element.186), channel_id=1, source_target_pairs={{0,9},{1,8},{2,11},{3,10},{4,13},{5,12},{6,15},{7,14},{8,1},{9,0},... | collective-permute-start | bytes 1572872 | tf_op jit(solution)/shard_map/ppermute | solution.py:230
  341.2 67.5 %collective-permute-start.38 = (bf16[64,4096]{1,0:T(8,128)(2,1)}, bf16[64,4096]{1,0:T(8,128)(2,1)}, u32[]{:S(2)}, u32[]{:S(2)}) collective-permute-start(bf16[64,4096]{1,0:T(8,128)(2,1)} %get-tuple-element.190), channel_id=1, source_target_pairs={{0,10},{1,11},{2,8},{3,9},{4,14},{5,15},{6,12},{7,13},{8,2},{9,3},... | collective-permute-start | bytes 1572872 | tf_op jit(solution)/shard_map/ppermute | solution.py:230
  363.9 64.1 %collective-permute-start.40 = (bf16[64,4096]{1,0:T(8,128)(2,1)}, bf16[64,4096]{1,0:T(8,128)(2,1)}, u32[]{:S(2)}, u32[]{:S(2)}) collective-permute-start(bf16[64,4096]{1,0:T(8,128)(2,1)} %get-tuple-element.192), channel_id=1, source_target_pairs={{0,14},{1,15},{2,12},{3,13},{4,10},{5,11},{6,8},{7,9},{8,6},{9,7},... | collective-permute-start | bytes 1572872 | tf_op jit(solution)/shard_map/ppermute | solution.py:230
  376.0 84.1 %collective-permute-start.42 = (bf16[64,4096]{1,0:T(8,128)(2,1)}, bf16[64,4096]{1,0:T(8,128)(2,1)}, u32[]{:S(2)}, u32[]{:S(2)}) collective-permute-start(bf16[64,4096]{1,0:T(8,128)(2,1)} %get-tuple-element.194), channel_id=1, source_target_pairs={{0,11},{1,10},{2,9},{3,8},{4,15},{5,14},{6,13},{7,12},{8,3},{9,2},... | collective-permute-start | bytes 1572872 | tf_op jit(solution)/shard_map/ppermute | solution.py:230
  409.8 72.8 %collective-permute-start.44 = (bf16[64,4096]{1,0:T(8,128)(2,1)}, bf16[64,4096]{1,0:T(8,128)(2,1)}, u32[]{:S(2)}, u32[]{:S(2)}) collective-permute-start(bf16[64,4096]{1,0:T(8,128)(2,1)} %get-tuple-element.196), channel_id=1, source_target_pairs={{0,15},{1,14},{2,13},{3,12},{4,11},{5,10},{6,9},{7,8},{8,7},{9,6},... | collective-permute-start | bytes 1572872 | tf_op jit(solution)/shard_map/ppermute | solution.py:230
  428.1 77.0 %collective-permute-start.15 = (bf16[64,4096]{1,0:T(8,128)(2,1)}, bf16[64,4096]{1,0:T(8,128)(2,1)S(1)}, u32[]{:S(2)}, u32[]{:S(2)}) collective-permute-start(bf16[64,4096]{1,0:T(8,128)(2,1)} %get-tuple-element.166), channel_id=1, source_target_pairs={{0,8},{1,9},{2,10},{3,11},{4,12},{5,13},{6,14},{7,15},{8,0},{9,1},... | collective-permute-start | bytes 1572872 | tf_op jit(solution)/shard_map/ppermute | solution.py:230
  428.1 76.9 %collective-permute-start.16 = (bf16[64,4096]{1,0:T(8,128)(2,1)}, bf16[64,4096]{1,0:T(8,128)(2,1)}, u32[]{:S(2)}, u32[]{:S(2)}) collective-permute-start(bf16[64,4096]{1,0:T(8,128)(2,1)} %get-tuple-element.167), channel_id=1, source_target_pairs={{0,4},{1,5},{2,6},{3,7},{4,0},{5,1},{6,2},{7,3},{8,12},{9,13},{10,... | collective-permute-start | bytes 1572872 | tf_op jit(solution)/shard_map/ppermute | solution.py:230
  482.6 67.5 %collective-permute-start.19 = (bf16[64,4096]{1,0:T(8,128)(2,1)}, bf16[64,4096]{1,0:T(8,128)(2,1)}, u32[]{:S(2)}, u32[]{:S(2)}) collective-permute-start(bf16[64,4096]{1,0:T(8,128)(2,1)} %get-tuple-element.170), channel_id=1, source_target_pairs={{0,9},{1,8},{2,11},{3,10},{4,13},{5,12},{6,15},{7,14},{8,1},{9,0},... | collective-permute-start | bytes 1572872 | tf_op jit(solution)/shard_map/ppermute | solution.py:230
  519.1 76.0 %collective-permute-start.23 = (bf16[64,4096]{1,0:T(8,128)(2,1)}, bf16[64,4096]{1,0:T(8,128)(2,1)}, u32[]{:S(2)}, u32[]{:S(2)}) collective-permute-start(bf16[64,4096]{1,0:T(8,128)(2,1)} %get-tuple-element.174), channel_id=1, source_target_pairs={{0,10},{1,11},{2,8},{3,9},{4,14},{5,15},{6,12},{7,13},{8,2},{9,3},... | collective-permute-start | bytes 1572872 | tf_op jit(solution)/shard_map/ppermute | solution.py:230
  550.1 77.1 %collective-permute-start.25 = (bf16[64,4096]{1,0:T(8,128)(2,1)}, bf16[64,4096]{1,0:T(8,128)(2,1)S(1)}, u32[]{:S(2)}, u32[]{:S(2)}) collective-permute-start(bf16[64,4096]{1,0:T(8,128)(2,1)} %get-tuple-element.176), channel_id=1, source_target_pairs={{0,14},{1,15},{2,12},{3,13},{4,10},{5,11},{6,8},{7,9},{8,6},{9,7},... | collective-permute-start | bytes 1572872 | tf_op jit(solution)/shard_map/ppermute | solution.py:230
  561.3 66.0 %collective-permute-start.26 = (bf16[64,4096]{1,0:T(8,128)(2,1)}, bf16[64,4096]{1,0:T(8,128)(2,1)S(1)}, u32[]{:S(2)}, u32[]{:S(2)}) collective-permute-start(bf16[64,4096]{1,0:T(8,128)(2,1)} %get-tuple-element.177), channel_id=1, source_target_pairs={{0,3},{1,2},{2,1},{3,0},{4,7},{5,6},{6,5},{7,4},{8,11},{9,10},{10,... | collective-permute-start | bytes 1572872 | tf_op jit(solution)/shard_map/ppermute | solution.py:230
  563.5 81.9 %collective-permute-start.27 = (bf16[64,4096]{1,0:T(8,128)(2,1)}, bf16[64,4096]{1,0:T(8,128)(2,1)S(1)}, u32[]{:S(2)}, u32[]{:S(2)}) collective-permute-start(bf16[64,4096]{1,0:T(8,128)(2,1)} %get-tuple-element.178), channel_id=1, source_target_pairs={{0,11},{1,10},{2,9},{3,8},{4,15},{5,14},{6,13},{7,12},{8,3},{9,2},... | collective-permute-start | bytes 1572872 | tf_op jit(solution)/shard_map/ppermute | solution.py:230
  595.1 72.8 %collective-permute-start.29 = (bf16[64,4096]{1,0:T(8,128)(2,1)}, bf16[64,4096]{1,0:T(8,128)(2,1)}, u32[]{:S(2)}, u32[]{:S(2)}) collective-permute-start(bf16[64,4096]{1,0:T(8,128)(2,1)} %get-tuple-element.180), channel_id=1, source_target_pairs={{0,15},{1,14},{2,13},{3,12},{4,11},{5,10},{6,9},{7,8},{8,7},{9,6},... | collective-permute-start | bytes 1572872 | tf_op jit(solution)/shard_map/ppermute | solution.py:230
  627.2 63.1 %collective-permute-start.75 = (bf16[64,4096]{1,0:T(8,128)(2,1)}, bf16[64,4096]{1,0:T(8,128)(2,1)S(1)}, u32[]{:S(2)}, u32[]{:S(2)}) collective-permute-start(bf16[64,4096]{1,0:T(8,128)(2,1)} %get-tuple-element.234), channel_id=1, source_target_pairs={{0,8},{1,9},{2,10},{3,11},{4,12},{5,13},{6,14},{7,15},{8,0},{9,1},... | collective-permute-start | bytes 1572872 | tf_op jit(solution)/shard_map/ppermute | solution.py:230
  628.2 62.1 %collective-permute-start.76 = (bf16[64,4096]{1,0:T(8,128)(2,1)}, bf16[64,4096]{1,0:T(8,128)(2,1)S(1)}, u32[]{:S(2)}, u32[]{:S(2)}) collective-permute-start(bf16[64,4096]{1,0:T(8,128)(2,1)} %get-tuple-element.235), channel_id=1, source_target_pairs={{0,4},{1,5},{2,6},{3,7},{4,0},{5,1},{6,2},{7,3},{8,12},{9,13},{10,... | collective-permute-start | bytes 1572872 | tf_op jit(solution)/shard_map/ppermute | solution.py:230
  667.8 67.5 %collective-permute-start.79 = (bf16[64,4096]{1,0:T(8,128)(2,1)}, bf16[64,4096]{1,0:T(8,128)(2,1)S(1)}, u32[]{:S(2)}, u32[]{:S(2)}) collective-permute-start(bf16[64,4096]{1,0:T(8,128)(2,1)} %get-tuple-element.238), channel_id=1, source_target_pairs={{0,9},{1,8},{2,11},{3,10},{4,13},{5,12},{6,15},{7,14},{8,1},{9,0},... | collective-permute-start | bytes 1572872 | tf_op jit(solution)/shard_map/ppermute | solution.py:230
  706.1 74.2 %collective-permute-start.83 = (bf16[64,4096]{1,0:T(8,128)(2,1)}, bf16[64,4096]{1,0:T(8,128)(2,1)}, u32[]{:S(2)}, u32[]{:S(2)}) collective-permute-start(bf16[64,4096]{1,0:T(8,128)(2,1)} %get-tuple-element.242), channel_id=1, source_target_pairs={{0,10},{1,11},{2,8},{3,9},{4,14},{5,15},{6,12},{7,13},{8,2},{9,3},... | collective-permute-start | bytes 1572872 | tf_op jit(solution)/shard_map/ppermute | solution.py:230
  737.2 77.0 %collective-permute-start.85 = (bf16[64,4096]{1,0:T(8,128)(2,1)}, bf16[64,4096]{1,0:T(8,128)(2,1)S(1)}, u32[]{:S(2)}, u32[]{:S(2)}) collective-permute-start(bf16[64,4096]{1,0:T(8,128)(2,1)} %get-tuple-element.244), channel_id=1, source_target_pairs={{0,14},{1,15},{2,12},{3,13},{4,10},{5,11},{6,8},{7,9},{8,6},{9,7},... | collective-permute-start | bytes 1572872 | tf_op jit(solution)/shard_map/ppermute | solution.py:230
  746.5 67.8 %collective-permute-start.86 = (bf16[64,4096]{1,0:T(8,128)(2,1)}, bf16[64,4096]{1,0:T(8,128)(2,1)}, u32[]{:S(2)}, u32[]{:S(2)}) collective-permute-start(bf16[64,4096]{1,0:T(8,128)(2,1)} %get-tuple-element.245), channel_id=1, source_target_pairs={{0,3},{1,2},{2,1},{3,0},{4,7},{5,6},{6,5},{7,4},{8,11},{9,10},{10,... | collective-permute-start | bytes 1572872 | tf_op jit(solution)/shard_map/ppermute | solution.py:230
  761.8 67.2 %collective-permute-start.87 = (bf16[64,4096]{1,0:T(8,128)(2,1)}, bf16[64,4096]{1,0:T(8,128)(2,1)}, u32[]{:S(2)}, u32[]{:S(2)}) collective-permute-start(bf16[64,4096]{1,0:T(8,128)(2,1)} %get-tuple-element.246), channel_id=1, source_target_pairs={{0,11},{1,10},{2,9},{3,8},{4,15},{5,14},{6,13},{7,12},{8,3},{9,2},... | collective-permute-start | bytes 1572872 | tf_op jit(solution)/shard_map/ppermute | solution.py:230
  780.3 71.2 %collective-permute-start.89 = (bf16[64,4096]{1,0:T(8,128)(2,1)}, bf16[64,4096]{1,0:T(8,128)(2,1)}, u32[]{:S(2)}, u32[]{:S(2)}) collective-permute-start(bf16[64,4096]{1,0:T(8,128)(2,1)} %get-tuple-element.248), channel_id=1, source_target_pairs={{0,15},{1,14},{2,13},{3,12},{4,11},{5,10},{6,9},{7,8},{8,7},{9,6},... | collective-permute-start | bytes 1572872 | tf_op jit(solution)/shard_map/ppermute | solution.py:230
  814.3 71.4 %collective-permute-start.106 = (bf16[64,4096]{1,0:T(8,128)(2,1)}, bf16[64,4096]{1,0:T(8,128)(2,1)S(1)}, u32[]{:S(2)}, u32[]{:S(2)}) collective-permute-start(bf16[64,4096]{1,0:T(8,128)(2,1)} %get-tuple-element.268), channel_id=1, source_target_pairs={{0,4},{1,5},{2,6},{3,7},{4,0},{5,1},{6,2},{7,3},{8,12},{9,13},{10,... | collective-permute-start | bytes 1572872 | tf_op jit(solution)/shard_map/ppermute | solution.py:230
  829.0 63.0 %collective-permute-start.108 = (bf16[64,4096]{1,0:T(8,128)(2,1)}, bf16[64,4096]{1,0:T(8,128)(2,1)S(1)}, u32[]{:S(2)}, u32[]{:S(2)}) collective-permute-start(bf16[64,4096]{1,0:T(8,128)(2,1)} %get-tuple-element.270), channel_id=1, source_target_pairs={{0,1},{1,0},{2,3},{3,2},{4,5},{5,4},{6,7},{7,6},{8,9},{9,8},{10,11... | collective-permute-start | bytes 1572872 | tf_op jit(solution)/shard_map/ppermute | solution.py:230
  885.7 72.6 %collective-permute-start.112 = (bf16[64,4096]{1,0:T(8,128)(2,1)}, bf16[64,4096]{1,0:T(8,128)(2,1)}, u32[]{:S(2)}, u32[]{:S(2)}) collective-permute-start(bf16[64,4096]{1,0:T(8,128)(2,1)} %get-tuple-element.274), channel_id=1, source_target_pairs={{0,2},{1,3},{2,0},{3,1},{4,6},{5,7},{6,4},{7,5},{8,10},{9,11},{10,... | collective-permute-start | bytes 1572872 | tf_op jit(solution)/shard_map/ppermute | solution.py:230
  892.0 66.4 %collective-permute-start.113 = (bf16[64,4096]{1,0:T(8,128)(2,1)}, bf16[64,4096]{1,0:T(8,128)(2,1)}, u32[]{:S(2)}, u32[]{:S(2)}) collective-permute-start(bf16[64,4096]{1,0:T(8,128)(2,1)} %get-tuple-element.275), channel_id=1, source_target_pairs={{0,10},{1,11},{2,8},{3,9},{4,14},{5,15},{6,12},{7,13},{8,2},{9,3},... | collective-permute-start | bytes 1572872 | tf_op jit(solution)/shard_map/ppermute | solution.py:230
  896.5 63.6 %collective-permute-start.114 = (bf16[64,4096]{1,0:T(8,128)(2,1)}, bf16[64,4096]{1,0:T(8,128)(2,1)}, u32[]{:S(2)}, u32[]{:S(2)}) collective-permute-start(bf16[64,4096]{1,0:T(8,128)(2,1)} %get-tuple-element.276), channel_id=1, source_target_pairs={{0,6},{1,7},{2,4},{3,5},{4,2},{5,3},{6,0},{7,1},{8,14},{9,15},{10,... | collective-permute-start | bytes 1572872 | tf_op jit(solution)/shard_map/ppermute | solution.py:230
  930.2 74.2 %collective-permute-start.116 = (bf16[64,4096]{1,0:T(8,128)(2,1)}, bf16[64,4096]{1,0:T(8,128)(2,1)S(1)}, u32[]{:S(2)}, u32[]{:S(2)}) collective-permute-start(bf16[64,4096]{1,0:T(8,128)(2,1)} %get-tuple-element.278), channel_id=1, source_target_pairs={{0,3},{1,2},{2,1},{3,0},{4,7},{5,6},{6,5},{7,4},{8,11},{9,10},{10,... | collective-permute-start | bytes 1572872 | tf_op jit(solution)/shard_map/ppermute | solution.py:230
  958.4 66.3 %collective-permute-start.118 = (bf16[64,4096]{1,0:T(8,128)(2,1)}, bf16[64,4096]{1,0:T(8,128)(2,1)S(1)}, u32[]{:S(2)}, u32[]{:S(2)}) collective-permute-start(bf16[64,4096]{1,0:T(8,128)(2,1)} %get-tuple-element.280), channel_id=1, source_target_pairs={{0,7},{1,6},{2,5},{3,4},{4,3},{5,2},{6,1},{7,0},{8,15},{9,14},{10,... | collective-permute-start | bytes 1572872 | tf_op jit(solution)/shard_map/ppermute | solution.py:230
  960.1 65.7 %collective-permute-start.119 = (bf16[64,4096]{1,0:T(8,128)(2,1)}, bf16[64,4096]{1,0:T(8,128)(2,1)S(1)}, u32[]{:S(2)}, u32[]{:S(2)}) collective-permute-start(bf16[64,4096]{1,0:T(8,128)(2,1)} %get-tuple-element.281), channel_id=1, source_target_pairs={{0,15},{1,14},{2,13},{3,12},{4,11},{5,10},{6,9},{7,8},{8,7},{9,6},... | collective-permute-start | bytes 1572872 | tf_op jit(solution)/shard_map/ppermute | solution.py:230
  980.9 74.9 %collective-permute-start.100 = (bf16[64,2560]{1,0:T(8,128)(2,1)}, bf16[64,2560]{1,0:T(8,128)(2,1)S(1)}, u32[]{:S(2)}, u32[]{:S(2)}) collective-permute-start(bf16[64,2560]{1,0:T(8,128)(2,1)} %get-tuple-element.261), channel_id=1, source_target_pairs={{0,14},{1,15},{2,12},{3,13},{4,10},{5,11},{6,8},{7,9},{8,6},{9,7},... | collective-permute-start | bytes 983048 | tf_op jit(solution)/shard_map/ppermute | solution.py:230
  (160 other events, 10834.8 us)
